TPU v7x, 512 devices: a whole 4x8x8 slice. The times are simulated.
512 devices in a mesh: row: 16 (over y, core), col: 32 (over z, x).
Axes of the slice: x: 4, y: 8, z: 8, core: 2. Of those that a mesh axis runs over, the one named last changes fastest.
Arguments:
- acts: bfloat16 [192, 2, 28672], P('col', None, 'row'), may hold values from -6 to 6
- grads: bfloat16 [192, 2, 8192], P('row', None, 'col'), may hold values from -0.3984375 to 0.3984375
- basis_in: bfloat16 [28672, 28672], P('row', 'col'), may hold values from -0.03125 to 0.03125
- basis_out: bfloat16 [8192, 8192], P('col', 'row'), may hold values from -0.0625 to 0.0625
- eigen: bfloat16 [28672, 8192], P('col', 'row'), may hold values from 0.5 to 8
- sketch: bfloat16 [72, 8192], P(None, 'col'), may hold values from -0.0625 to 0.0625
Outputs:
- range_basis: float32 [2, 72, 28672], P(None, None, 'row')
- projected: float32 [2, 72, 8192], P(None, None, 'col')
All inputs are finite; a program needn't handle non-finite values.
Results may differ from a plain program's by a relative error of at most 0.018.
Values may be sent and summed in bfloat16 or wider, within the bound.
No kernel may reach another device: no remote copies, remote signals or barrier semaphores. Data moves between devices by JAX's collectives and lax.ppermute only.
A program may use at most 64 MiB of HBM per device.

v0:
```python
import functools

import jax
import jax.numpy as jnp
from jax import lax
from jax.experimental import pallas as pl
from jax.experimental.pallas import tpu as pltpu
from jax.sharding import Mesh
from jax.sharding import PartitionSpec as P

COL = ("z", "x")
ROW = ("y", "core")
BF = jnp.bfloat16
F32 = jnp.float32
MIB = 1024 * 1024


def call(body, out, *args, limit=32):
    many = isinstance(out, list)
    shapes = [jax.ShapeDtypeStruct(s, d) for s, d in (out if many else [out])]
    got = pl.pallas_call(
        body,
        out_shape=shapes,
        in_specs=[
            pl.BlockSpec(memory_space=pltpu.SMEM if a.size == 1 else pltpu.VMEM) for a in args
        ],
        out_specs=[pl.BlockSpec(memory_space=pltpu.VMEM)] * len(shapes),
        compiler_params=pltpu.CompilerParams(vmem_limit_bytes=limit * MIB),
    )(*args)
    return got if many else got[0]


def swap(x, axes):
    return lax.all_to_all(x, axes, 0, 0, tiled=True)


def dot(a, b, ca=1, cb=0, **kw):
    return lax.dot_general(a, b, (((ca,), (cb,)), ((), ())), preferred_element_type=F32, **kw)


def to_tiles(y, out_ref, slots):
    lanes = y.shape[1] // 128
    count = (y.shape[0] // 16) * lanes
    y = y.astype(BF)
    for t in range(out_ref.shape[0] * slots):
        if t < count:
            r, g = divmod(t, lanes)
            tile = y[r * 16 : r * 16 + 16, g * 128 : g * 128 + 128]
        else:
            tile = jnp.zeros((16, 128), BF)
        out_ref[t // slots, t % slots] = tile


def from_tiles(ref, slots, rows, lanes):
    lines = []
    for r in range(rows):
        at = [divmod(r * lanes + g, slots) for g in range(lanes)]
        lines.append(jnp.concatenate([ref[p, s] for p, s in at], axis=1))
    return jnp.concatenate(lines, axis=0)


def sum_body(x_ref, out_ref):
    total = jnp.sum(x_ref[...].astype(F32), axis=0).astype(BF)
    out_ref[...] = jnp.broadcast_to(total[None], out_ref.shape)


def sum_over(pieces, axes):
    own = swap(pieces, axes)
    return swap(call(sum_body, (own.shape, BF), own), axes)


def pack_body(x_ref, out_ref):
    x = x_ref[...].astype(F32)
    half = x.shape[1] // 2
    first, rest = x[:8], x[8:]
    low, high = rest[:, :half], rest[:, half:]
    rest = jnp.concatenate([low, high], axis=0)
    wide = out_ref.shape[2]
    left = x.shape[1] - wide
    spare = jnp.zeros((8, 2 * wide - x.shape[1] - half), F32)
    bottom = jnp.concatenate([first[:, wide:], rest, spare], axis=1)
    assert left + half + spare.shape[1] == wide
    packed = jnp.concatenate([first[:, :wide], bottom], axis=0).astype(BF)
    out_ref[...] = jnp.broadcast_to(packed[None], out_ref.shape)


def act_body(x_ref, w_ref, out_ref):
    v = x_ref[...].astype(F32)
    wide = v.shape[2]
    full = w_ref.shape[0]
    half = full // 2
    top, bottom = v[:, :8], v[:, 8:]
    left = full - wide
    first = jnp.concatenate([top, bottom[:, :, :left]], axis=2)
    rest = bottom[:, :, left : left + half].reshape(v.shape[0] // 2, 2, 8, half)
    even, odd = rest[:, 0], rest[:, 1]
    head = lax.broadcasted_iota(jnp.int32, even.shape, 1) < 4
    low = jnp.where(head, even, pltpu.roll(odd, 4, 1))
    high = jnp.where(head, pltpu.roll(even, 4, 1), odd)
    last = jnp.concatenate([low, high], axis=2)
    pairs = first.reshape(v.shape[0] // 2, 16, full)
    x = jnp.concatenate([pairs, last], axis=1).reshape(v.shape[0] * 12, full).astype(BF)
    out_ref[...] = dot(x, w_ref[...]).astype(BF)


def grad_body(g_ref, s_ref, w_ref, out_ref):
    w = w_ref[...]
    n = g_ref.shape[0]
    out_ref[:n] = dot(g_ref[...], w).astype(BF)
    s = dot(s_ref[...], w)
    spare = jnp.zeros((out_ref.shape[0] - n - s.shape[0], s.shape[1]), F32)
    out_ref[n:] = jnp.concatenate([s, spare], axis=0).astype(BF)


def scaled_body(a_ref, g_ref, e_ref, scaled_ref, out_ref):
    n = a_ref.shape[0]
    a = a_ref[...].T
    g = g_ref[:n]
    sk = g_ref[n : n + 80]
    odd = lax.broadcasted_iota(jnp.int32, g.shape, 0) % 2
    e = e_ref[...].astype(F32)
    parts = []
    for q in range(2):
        mine = jnp.where(odd == q, g.astype(F32), 0.0).astype(BF)
        s = (dot(a, mine) / e).astype(BF)
        scaled_ref[q] = s
        parts.append(dot(sk, s, 1, 1)[:72])
    to_tiles(jnp.concatenate(parts, axis=0), out_ref, out_ref.shape[1])


def range_body(r_ref, w_ref, out_ref):
    r = from_tiles(r_ref, 4, 9, 7)
    to_tiles(dot(r, w_ref[...], 1, 1), out_ref, 4)


def mapped_slot(t):
    return divmod(t, 6) if t < 42 else (7 + (t - 42) // 3, (t - 42) % 3)


def split3(x):
    hi = x.astype(BF)
    left = x - hi.astype(F32)
    mid = left.astype(BF)
    return hi, mid, (left - mid.astype(F32)).astype(BF)


def mapped_body(r_ref, w_ref, out_ref):
    r = from_tiles(r_ref, 4, 9, 14)
    y = dot(r, w_ref[...]).astype(BF)
    for t in range(69):
        p, s = mapped_slot(t)
        a, g = divmod(t, 7)
        tile = y[a * 16 : a * 16 + 16, g * 128 : g * 128 + 128] if t < 63 else jnp.zeros((16, 128), BF)
        out_ref[p, s] = tile
    wide = r.astype(F32)
    grams = []
    for q in range(2):
        rq = wide[q * 72 : q * 72 + 72].astype(BF)
        g = dot(rq, rq, 1, 1)
        grams.append(jnp.concatenate([g, jnp.zeros((72, 56), F32)], axis=1))
    gram = jnp.concatenate(grams, axis=0)
    for i, part in enumerate(split3(gram)):
        for a in range(9):
            out_ref[7 + a, 3 + i] = part[a * 16 : a * 16 + 16]


def gram_sum_body(flag_ref, x_ref, out_ref):
    total = jnp.sum(x_ref[...].astype(F32), axis=0)
    whole = total[3] + total[4] + total[5]
    plain = flag_ref[0, 0] < 7
    parts = split3(whole)
    for i in range(6):
        tile = total[i].astype(BF)
        if i >= 3:
            tile = jnp.where(plain, total[i], parts[i - 3].astype(F32)).astype(BF)
        out_ref[:, i] = jnp.broadcast_to(tile[None], (out_ref.shape[0], 16, 128))


def core_body(m_ref, s_ref, out_ref):
    tiles = [m_ref[mapped_slot(t)] for t in range(63)]
    m = jnp.concatenate(
        [jnp.concatenate(tiles[r * 7 : r * 7 + 7], axis=1) for r in range(9)], axis=0
    ).astype(F32)
    parts = [dot(m[q * 72 : q * 72 + 72].astype(BF), s_ref[q]) for q in range(2)]
    to_tiles(jnp.concatenate(parts, axis=0), out_ref, 2)


def inverse_body(m_ref, out_ref):
    gram = jnp.concatenate(
        [sum(m_ref[7 + a, 3 + i].astype(F32) for i in range(3)) for a in range(9)], axis=0
    )
    rows = lax.broadcasted_iota(jnp.int32, (72, 128), 0)
    lanes = lax.broadcasted_iota(jnp.int32, (72, 128), 1)
    below = lax.broadcasted_iota(jnp.int32, (72, 1), 0)
    eye = jnp.where(rows == lanes, 1.0, 0.0)
    left = [gram[q * 72 : q * 72 + 72] for q in range(2)]
    right = [eye, eye]
    for k in range(72):
        for q in range(2):
            pivot = left[q][k : k + 1]
            f = left[q][:, k : k + 1] / pivot[:, k : k + 1]
            f = jnp.where(below > k, f, 0.0)
            line = right[q][k : k + 1]
            left[q] = left[q] - f * pivot
            right[q] = right[q] - f * line
    for q in range(2):
        d = jnp.sum(jnp.where(rows == lanes, left[q], 0.0), axis=1, keepdims=True)
        out_ref[q] = right[q] / jnp.sqrt(d)


def basis_body(w_ref, r_ref, out_ref):
    r = from_tiles(r_ref, 4, 9, 14).astype(F32)
    for q in range(2):
        w = w_ref[q][:, :72]
        out_ref[q] = dot(w, r[q * 72 : q * 72 + 72], precision=lax.Precision.HIGHEST)


def project_body(c_ref, w_ref, out_ref):
    c = from_tiles(c_ref, 2, 9, 4)
    to_tiles(dot(c, w_ref[...], 1, 1), out_ref, 2)


def final_body(w_ref, p_ref, out_ref):
    p = from_tiles(p_ref, 2, 9, 2).astype(F32)
    for q in range(2):
        w = w_ref[q][:, :72]
        out_ref[q] = dot(w, p[q * 72 : q * 72 + 72], precision=lax.Precision.HIGHEST)


def on_device(acts, grads, basis_in, basis_out, eigen, sketch):
    g = grads.reshape(24, 256)
    g = jnp.concatenate([g[0:8], g[12:20], g[8:12], g[20:24]], axis=0)
    all_grads = swap(jnp.broadcast_to(g[None], (16, 24, 256)), ROW).reshape(384, 256)
    packed = call(pack_body, ((32, 16, 1408), BF), acts.reshape(12, 1792))
    all_acts = swap(packed, COL)
    g_part = call(grad_body, ((512, 512), BF), all_grads, sketch, basis_out)
    g_rot = sum_over(g_part.reshape(32, 16, 512), COL).reshape(512, 512)
    a_part = call(act_body, ((384, 896), BF), all_acts, basis_in)
    a_rot = sum_over(a_part.reshape(16, 24, 896), ROW).reshape(384, 896)
    scaled, red = call(
        scaled_body, [((2, 896, 512), BF), ((16, 4, 16, 128), BF)], a_rot, g_rot, eigen
    )
    reduced = sum_over(red, ROW)
    span = call(range_body, ((32, 4, 16, 128), BF), reduced, basis_in)
    span = sum_over(span, COL)
    mapped = swap(call(mapped_body, ((16, 6, 16, 128), BF), span, basis_in), ROW)
    flag = jnp.full((1, 1), lax.axis_index(ROW), jnp.int32)
    mapped = swap(call(gram_sum_body, ((16, 6, 16, 128), BF), flag, mapped), ROW)
    core = sum_over(call(core_body, ((32, 2, 16, 128), BF), mapped, scaled), COL)
    inverse = call(inverse_body, ((2, 72, 128), F32), mapped)
    basis = call(basis_body, ((2, 72, 1792), F32), inverse, span)
    proj = sum_over(call(project_body, ((16, 2, 16, 128), BF), core, basis_out), ROW)
    return basis, call(final_body, ((2, 72, 256), F32), inverse, proj)


def solution(mesh):
    split = Mesh(mesh.devices.reshape(8, 2, 8, 4), ("y", "core", "z", "x"))
    return jax.shard_map(
        on_device,
        mesh=split,
        in_specs=(
            P(COL, None, ROW),
            P(ROW, None, COL),
            P(ROW, COL),
            P(COL, ROW),
            P(COL, ROW),
            P(None, COL),
        ),
        out_specs=(P(None, None, ROW), P(None, None, COL)),
        check_vma=False,
    )
```

profile of v0, /device:TPU:1, one launch (start us, length us, event | category | flops | bytes accessed | tf_op | source)
XLA Modules:
  0.0 344.4 jit_solution(5516501921369359788)
XLA Ops:
  0.6 0.7 fusion
  1.3 0.7 fusion.1
  2.1 0.7 broadcast_in_dim.10
  2.8 10.8 %all-to-all-start.3 = ((bf16[16,24,256]{2,1,0:T(8,128)(2,1)}), bf16[16,24,256]{2,1,0:T(8,128)(2,1)}, u32[]{:S(2)}, u32[]{:S(2)}) async-start(bf16[16,24,256]{2,1,0:T(8,128)(2,1)} %broadcast_in_dim.10), calls=%async_computation.3 | async-start | bytes 393216 | tf_op jit(solution)/shard_map/all_to_all | solution.py:34
  13.6 0.8 reshape.28.x_ref
  14.4 0.0 copy-start.11
  14.4 0.0 copy-start.13
  14.4 0.1 shard_map.77
  14.5 0.0 copy-start.1
  14.5 1.1 copy-done.1
  15.6 8.4 %all-to-all-done.3 = bf16[16,24,256]{2,1,0:T(8,128)(2,1)} async-done(((bf16[16,24,256]{2,1,0:T(8,128)(2,1)}), bf16[16,24,256]{2,1,0:T(8,128)(2,1)}, u32[]{:S(2)}, u32[]{:S(2)}) %all-to-all-start.3) | async-done | bytes 196640 | tf_op jit(solution)/shard_map/all_to_all | solution.py:34
  24.1 10.8 %all-to-all-start = ((bf16[32,16,1408]{2,1,0:T(8,128)(2,1)}), bf16[32,16,1408]{2,1,0:T(8,128)(2,1)}, u32[]{:S(2)}, u32[]{:S(2)}) async-start(bf16[32,16,1408]{2,1,0:T(8,128)(2,1)} %copy-done.1), calls=%async_computation | async-start | bytes 2883584 | tf_op jit(solution)/shard_map/all_to_all | solution.py:34
  34.9 0.0 copy-done.11
  34.9 0.0 copy-done.13
  34.9 1.2 shard_map.80
  36.1 0.0 copy-start.6
  36.1 0.8 copy-done.6
  36.9 33.1 %all-to-all-done.x_ref = bf16[32,16,1408]{2,1,0:T(8,128)(2,1)} async-done(((bf16[32,16,1408]{2,1,0:T(8,128)(2,1)}), bf16[32,16,1408]{2,1,0:T(8,128)(2,1)}, u32[]{:S(2)}, u32[]{:S(2)}) %all-to-all-start) | async-done | bytes 1441824 | tf_op jit(solution)/shard_map/all_to_all | solution.py:34
  70.0 6.6 %all-to-all-start.4 = ((bf16[32,16,512]{2,1,0:T(8,128)(2,1)}), bf16[32,16,512]{2,1,0:T(8,128)(2,1)}, u32[]{:S(2)}, u32[]{:S(2)}) async-start(bf16[32,16,512]{2,1,0:T(8,128)(2,1)} %bitcast.8), calls=%async_computation.4 | async-start | bytes 1048576 | tf_op jit(solution)/shard_map/all_to_all | solution.py:34
  76.7 0.0 copy-done
  76.7 2.9 shard_map.78
  79.7 0.0 copy-start.5
  79.7 0.8 copy-done.5
  80.5 12.7 %all-to-all-done.4.x_ref = bf16[32,16,512]{2,1,0:T(8,128)(2,1)} async-done(((bf16[32,16,512]{2,1,0:T(8,128)(2,1)}), bf16[32,16,512]{2,1,0:T(8,128)(2,1)}, u32[]{:S(2)}, u32[]{:S(2)}) %all-to-all-start.4) | async-done | bytes 524320 | tf_op jit(solution)/shard_map/all_to_all | solution.py:34
  93.2 6.2 %all-to-all-start.1 = ((bf16[16,24,896]{2,1,0:T(8,128)(2,1)}), bf16[16,24,896]{2,1,0:T(8,128)(2,1)}, u32[]{:S(2)}, u32[]{:S(2)}) async-start(bf16[16,24,896]{2,1,0:T(8,128)(2,1)} %bitcast.7), calls=%async_computation.1 | async-start | bytes 1376256 | tf_op jit(solution)/shard_map/all_to_all | solution.py:34
  99.4 1.1 shard_map.81
  100.6 0.0 copy-start.7
  100.6 0.8 copy-done.7
  101.4 18.9 %all-to-all-done.1.x_ref = bf16[16,24,896]{2,1,0:T(8,128)(2,1)} async-done(((bf16[16,24,896]{2,1,0:T(8,128)(2,1)}), bf16[16,24,896]{2,1,0:T(8,128)(2,1)}, u32[]{:S(2)}, u32[]{:S(2)}) %all-to-all-start.1) | async-done | bytes 688160 | tf_op jit(solution)/shard_map/all_to_all | solution.py:34
  120.2 4.6 %all-to-all-start.5 = ((bf16[32,16,512]{2,1,0:T(8,128)(2,1)}), bf16[32,16,512]{2,1,0:T(8,128)(2,1)}, u32[]{:S(2)}, u32[]{:S(2)}) async-start(bf16[32,16,512]{2,1,0:T(8,128)(2,1)} %copy-done.7), calls=%async_computation.5 | async-start | bytes 1048576 | tf_op jit(solution)/shard_map/all_to_all | solution.py:34
  124.8 1.2 shard_map.79
  126.1 0.0 copy-start.4
  126.1 0.8 copy-done.4
  126.9 15.0 %all-to-all-done.5 = bf16[32,16,512]{2,1,0:T(8,128)(2,1)} async-done(((bf16[32,16,512]{2,1,0:T(8,128)(2,1)}), bf16[32,16,512]{2,1,0:T(8,128)(2,1)}, u32[]{:S(2)}, u32[]{:S(2)}) %all-to-all-start.5) | async-done | bytes 524320 | tf_op jit(solution)/shard_map/all_to_all | solution.py:34
  141.9 25.3 %all_to_all.80 = bf16[16,24,896]{2,1,0:T(8,128)(2,1)S(1)} all-to-all(bf16[16,24,896]{2,1,0:T(8,128)(2,1)} %copy-done.4), channel_id=1, replica_groups=mesh['y'=8,'core'=2,'z'=8,'x'=4] {'y','core'}, dimensions={0} | all-to-all | bytes 1376256 | tf_op jit(solution)/shard_map/all_to_all | solution.py:34
  167.2 2.6 shard_map.82
  169.8 1.3 copy-done.8
  171.1 14.4 %all_to_all.81.x_ref = bf16[16,4,16,128]{3,2,1,0:T(8,128)(2,1)S(1)} all-to-all(bf16[16,4,16,128]{3,2,1,0:T(8,128)(2,1)S(1)} %get-tuple-element.4), channel_id=1, replica_groups=mesh['y'=8,'core'=2,'z'=8,'x'=4] {'y','core'}, dimensions={0} | all-to-all | bytes 524288 | tf_op jit(solution)/shard_map/all_to_all | solution.py:34
  185.5 14.4 %all_to_all.82.r_ref = bf16[16,4,16,128]{3,2,1,0:T(8,128)(2,1)S(1)} all-to-all(bf16[16,4,16,128]{3,2,1,0:T(8,128)(2,1)S(1)} %shard_map.83), channel_id=1, replica_groups=mesh['y'=8,'core'=2,'z'=8,'x'=4] {'y','core'}, dimensions={0} | all-to-all | bytes 524288 | tf_op jit(solution)/shard_map/all_to_all | solution.py:34
  199.9 1.0 shard_map.84
  200.9 21.5 %all_to_all.83.x_ref = bf16[32,4,16,128]{3,2,1,0:T(8,128)(2,1)S(1)} all-to-all(bf16[32,4,16,128]{3,2,1,0:T(8,128)(2,1)S(1)} %shard_map.84), channel_id=1, replica_groups=mesh['y'=8,'core'=2,'z'=8,'x'=4] {'z','x'}, dimensions={0} | all-to-all | bytes 1048576 | tf_op jit(solution)/shard_map/all_to_all | solution.py:34
  222.4 0.1 shard_map.85
  222.5 20.0 %all_to_all.84.r_ref = bf16[32,4,16,128]{3,2,1,0:T(8,128)(2,1)S(1)} all-to-all(bf16[32,4,16,128]{3,2,1,0:T(8,128)(2,1)S(1)} %shard_map.85), channel_id=1, replica_groups=mesh['y'=8,'core'=2,'z'=8,'x'=4] {'z','x'}, dimensions={0} | all-to-all | bytes 1048576 | tf_op jit(solution)/shard_map/all_to_all | solution.py:34
  242.5 0.9 shard_map.86
  243.4 0.0 copy-start.2
  243.4 0.8 copy-done.2
  244.2 0.7 copy-done.10
  245.0 6.8 %all-to-all-start.10 = ((bf16[16,6,16,128]{3,2,1,0:T(8,128)(2,1)}), bf16[16,6,16,128]{3,2,1,0:T(8,128)(2,1)S(1)}, u32[]{:S(2)}, u32[]{:S(2)}) async-start(bf16[16,6,16,128]{3,2,1,0:T(8,128)(2,1)} %copy-done.10), calls=%async_computation.10 | async-start | bytes 786432 | tf_op jit(solution)/shard_map/all_to_all | solution.py:34
  251.8 14.6 %all-to-all-done.10.x_ref = bf16[16,6,16,128]{3,2,1,0:T(8,128)(2,1)S(1)} async-done(((bf16[16,6,16,128]{3,2,1,0:T(8,128)(2,1)}), bf16[16,6,16,128]{3,2,1,0:T(8,128)(2,1)S(1)}, u32[]{:S(2)}, u32[]{:S(2)}) %all-to-all-start.10) | async-done | bytes 393248 | tf_op jit(solution)/shard_map/all_to_all | solution.py:34
  266.3 0.1 shard_map.87
  266.4 17.3 %all_to_all.85.m_ref = bf16[16,6,16,128]{3,2,1,0:T(8,128)(2,1)S(1)} all-to-all(bf16[16,6,16,128]{3,2,1,0:T(8,128)(2,1)S(1)} %shard_map.87), channel_id=1, replica_groups=mesh['y'=8,'core'=2,'z'=8,'x'=4] {'y','core'}, dimensions={0} | all-to-all | bytes 786432 | tf_op jit(solution)/shard_map/all_to_all | solution.py:34
  283.6 0.4 shard_map.90
  284.1 0.0 copy-start.3
  284.1 17.2 %all_to_all.86.x_ref = bf16[32,2,16,128]{3,2,1,0:T(8,128)(2,1)S(1)} all-to-all(bf16[32,2,16,128]{3,2,1,0:T(8,128)(2,1)S(1)} %shard_map.90), channel_id=1, replica_groups=mesh['y'=8,'core'=2,'z'=8,'x'=4] {'z','x'}, dimensions={0} | all-to-all | bytes 524288 | tf_op jit(solution)/shard_map/all_to_all | solution.py:34
  301.3 0.1 shard_map.91
  301.3 15.2 %all_to_all.87.c_ref = bf16[32,2,16,128]{3,2,1,0:T(8,128)(2,1)S(1)} all-to-all(bf16[32,2,16,128]{3,2,1,0:T(8,128)(2,1)S(1)} %shard_map.91), channel_id=1, replica_groups=mesh['y'=8,'core'=2,'z'=8,'x'=4] {'z','x'}, dimensions={0} | all-to-all | bytes 524288 | tf_op jit(solution)/shard_map/all_to_all | solution.py:34
  316.6 0.2 shard_map.92
  316.8 13.9 %all_to_all.88.x_ref = bf16[16,2,16,128]{3,2,1,0:T(8,128)(2,1)S(1)} all-to-all(bf16[16,2,16,128]{3,2,1,0:T(8,128)(2,1)S(1)} %shard_map.92), channel_id=1, replica_groups=mesh['y'=8,'core'=2,'z'=8,'x'=4] {'y','core'}, dimensions={0} | all-to-all | bytes 262144 | tf_op jit(solution)/shard_map/all_to_all | solution.py:34
  330.8 0.7 shard_map.93
  331.4 3.6 %all-to-all-start.15 = ((bf16[16,2,16,128]{3,2,1,0:T(8,128)(2,1)}), bf16[16,2,16,128]{3,2,1,0:T(8,128)(2,1)S(1)}, u32[]{:S(2)}, u32[]{:S(2)}) async-start(bf16[16,2,16,128]{3,2,1,0:T(8,128)(2,1)} %shard_map.93), calls=%async_computation.15 | async-start | bytes 262144 | tf_op jit(solution)/shard_map/all_to_all | solution.py:34
  335.0 6.1 %shard_map.88.w_ref = f32[2,72,128]{2,1,0:T(8,128)S(1)} custom-call(bf16[16,6,16,128]{3,2,1,0:T(8,128)(2,1)S(1)} %all_to_all.85.m_ref), custom_call_target="tpu_custom_call" | custom-call | tf_op jit(solution)/shard_map/pallas_call | solution.py:21
  341.1 1.9 shard_map.89
  343.0 0.4 all-to-all-done.15.p_ref
  343.4 0.9 shard_map.94
  (14 shorter events, 0.1 us)
Async XLA Ops:
  2.8 21.3 %all-to-all-start.3 = ((bf16[16,24,256]{2,1,0:T(8,128)(2,1)}), bf16[16,24,256]{2,1,0:T(8,128)(2,1)}, u32[]{:S(2)}, u32[]{:S(2)}) async-start(bf16[16,24,256]{2,1,0:T(8,128)(2,1)} %broadcast_in_dim.10), calls=%async_computation.3 | async-start | bytes 393216 | tf_op jit(solution)/shard_map/all_to_all | solution.py:34
  14.4 20.5 %copy-start.11 = (bf16[256,512]{1,0:T(8,128)(2,1)S(1)}, bf16[256,512]{1,0:T(8,128)(2,1)}, u32[]{:S(2)}) copy-start(bf16[256,512]{1,0:T(8,128)(2,1)} %w_ref.9) | copy-start | bytes 786436
  14.4 20.5 %copy-start.13 = (bf16[72,256]{1,0:T(8,128)(2,1)S(1)}, bf16[72,256]{1,0:T(8,128)(2,1)}, u32[]{:S(2)}) copy-start(bf16[72,256]{1,0:T(8,128)(2,1)} %s_ref.1) | copy-start | bytes 110596
  14.5 1.1 copy-start.1
  15.6 61.1 %copy-start = (bf16[1792,896]{1,0:T(8,128)(2,1)S(1)}, bf16[1792,896]{1,0:T(8,128)(2,1)}, u32[]{:S(2)}) copy-start(bf16[1792,896]{1,0:T(8,128)(2,1)} %w_ref.8) | copy-start | bytes 9633796
  24.1 45.9 %all-to-all-start = ((bf16[32,16,1408]{2,1,0:T(8,128)(2,1)}), bf16[32,16,1408]{2,1,0:T(8,128)(2,1)}, u32[]{:S(2)}, u32[]{:S(2)}) async-start(bf16[32,16,1408]{2,1,0:T(8,128)(2,1)} %copy-done.1), calls=%async_computation | async-start | bytes 2883584 | tf_op jit(solution)/shard_map/all_to_all | solution.py:34
  36.1 0.8 copy-start.6
  70.0 23.2 %all-to-all-start.4 = ((bf16[32,16,512]{2,1,0:T(8,128)(2,1)}), bf16[32,16,512]{2,1,0:T(8,128)(2,1)}, u32[]{:S(2)}, u32[]{:S(2)}) async-start(bf16[32,16,512]{2,1,0:T(8,128)(2,1)} %bitcast.8), calls=%async_computation.4 | async-start | bytes 1048576 | tf_op jit(solution)/shard_map/all_to_all | solution.py:34
  79.7 0.8 copy-start.5
  93.2 27.0 %all-to-all-start.1 = ((bf16[16,24,896]{2,1,0:T(8,128)(2,1)}), bf16[16,24,896]{2,1,0:T(8,128)(2,1)}, u32[]{:S(2)}, u32[]{:S(2)}) async-start(bf16[16,24,896]{2,1,0:T(8,128)(2,1)} %bitcast.7), calls=%async_computation.1 | async-start | bytes 1376256 | tf_op jit(solution)/shard_map/all_to_all | solution.py:34
  100.6 0.8 copy-start.7
  120.2 21.6 %all-to-all-start.5 = ((bf16[32,16,512]{2,1,0:T(8,128)(2,1)}), bf16[32,16,512]{2,1,0:T(8,128)(2,1)}, u32[]{:S(2)}, u32[]{:S(2)}) async-start(bf16[32,16,512]{2,1,0:T(8,128)(2,1)} %copy-done.7), calls=%async_computation.5 | async-start | bytes 1048576 | tf_op jit(solution)/shard_map/all_to_all | solution.py:34
  126.1 0.8 copy-start.4
  141.9 25.3 %copy-start.12 = (bf16[896,512]{1,0:T(8,128)(2,1)S(1)}, bf16[896,512]{1,0:T(8,128)(2,1)}, u32[]{:S(2)}) copy-start(bf16[896,512]{1,0:T(8,128)(2,1)} %e_ref.1) | copy-start | bytes 2752516
  169.8 1.3 copy-start.8
  243.4 0.8 copy-start.2
  244.2 0.7 copy-start.10
  245.0 38.7 %copy-start.9 = (bf16[2,896,512]{2,1,0:T(8,128)(2,1)S(1)}, bf16[2,896,512]{2,1,0:T(8,128)(2,1)}, u32[]{:S(2)}) copy-start(bf16[2,896,512]{2,1,0:T(8,128)(2,1)} %copy-done.8) | copy-start | bytes 5505028
  245.0 21.4 %all-to-all-start.10 = ((bf16[16,6,16,128]{3,2,1,0:T(8,128)(2,1)}), bf16[16,6,16,128]{3,2,1,0:T(8,128)(2,1)S(1)}, u32[]{:S(2)}, u32[]{:S(2)}) async-start(bf16[16,6,16,128]{3,2,1,0:T(8,128)(2,1)} %copy-done.10), calls=%async_computation.10 | async-start | bytes 786432 | tf_op jit(solution)/shard_map/all_to_all | solution.py:34
  284.1 57.0 %copy-start.3 = (bf16[32,4,16,128]{3,2,1,0:T(8,128)(2,1)S(1)}, bf16[32,4,16,128]{3,2,1,0:T(8,128)(2,1)}, u32[]{:S(2)}) copy-start(bf16[32,4,16,128]{3,2,1,0:T(8,128)(2,1)} %copy-done.2) | copy-start | bytes 1572868
  331.4 12.0 %all-to-all-start.15 = ((bf16[16,2,16,128]{3,2,1,0:T(8,128)(2,1)}), bf16[16,2,16,128]{3,2,1,0:T(8,128)(2,1)S(1)}, u32[]{:S(2)}, u32[]{:S(2)}) async-start(bf16[16,2,16,128]{3,2,1,0:T(8,128)(2,1)} %shard_map.93), calls=%async_computation.15 | async-start | bytes 262144 | tf_op jit(solution)/shard_map/all_to_all | solution.py:34
where the time goes:
time: 346 us; the launch traced here: 344 us
  blocking collectives  159 us (46%)
  waiting for transfers between devices  103 us (30%)
  starting transfers between devices  49.4 us (14%)
  Pallas kernels  21.6 us (6%)
  local copies, waits for them, and re-layouts  10.1 us (3%)
    all_to_all x9, blocking collectives, swap(): return lax.all_to_all(x, axes, 0, 0, tiled=True)  159 us
    all_to_all x7, waiting for transfers between devices, swap(): return lax.all_to_all(x, axes, 0, 0, tiled=True)  103 us
    all_to_all x7, starting transfers between devices, swap(): return lax.all_to_all(x, axes, 0, 0, tiled=True)  49.4 us
    pallas_call x18, Pallas kernels, call(): pl.pallas_call(body, out_shape=shapes, in_specs=[pl.BlockSpec(memory_spac...  21.6 us
    unnamed x28, local copies, waits for them, and re-layouts  7.19 us
  transfers between devices with their start and end apart: 7, of which 7 were waited for; matrix products, arithmetic and copies ran while one was open for 0% of the time, Pallas kernels for 4%

commit v1 on v0

--- a/solution.py
+++ b/solution.py
@@ -21,9 +21,7 @@
     got = pl.pallas_call(
         body,
         out_shape=shapes,
-        in_specs=[
-            pl.BlockSpec(memory_space=pltpu.SMEM if a.size == 1 else pltpu.VMEM) for a in args
-        ],
+        in_specs=[pl.BlockSpec(memory_space=pltpu.VMEM)] * len(args),
         out_specs=[pl.BlockSpec(memory_space=pltpu.VMEM)] * len(shapes),
         compiler_params=pltpu.CompilerParams(vmem_limit_bytes=limit * MIB),
     )(*args)
@@ -64,42 +62,59 @@
     out_ref[...] = jnp.broadcast_to(total[None], out_ref.shape)
 
 
+def sum_one_body(x_ref, out_ref):
+    out_ref[...] = jnp.sum(x_ref[...].astype(F32), axis=0).astype(BF)
+
+
+def summed(pieces, axes):
+    own = swap(pieces, axes)
+    return call(sum_one_body, (own.shape[1:], BF), own)
+
+
 def sum_over(pieces, axes):
     own = swap(pieces, axes)
     return swap(call(sum_body, (own.shape, BF), own), axes)
 
 
-def pack_body(x_ref, out_ref):
+def join_body(own_ref, x_ref, out_ref):
+    g = jnp.sum(own_ref[...].astype(F32), axis=0)
     x = x_ref[...].astype(F32)
     half = x.shape[1] // 2
+    wide = out_ref.shape[2] - g.shape[1]
     first, rest = x[:8], x[8:]
-    low, high = rest[:, :half], rest[:, half:]
-    rest = jnp.concatenate([low, high], axis=0)
-    wide = out_ref.shape[2]
-    left = x.shape[1] - wide
+    rest = jnp.concatenate([rest[:, :half], rest[:, half:]], axis=0)
     spare = jnp.zeros((8, 2 * wide - x.shape[1] - half), F32)
     bottom = jnp.concatenate([first[:, wide:], rest, spare], axis=1)
-    assert left + half + spare.shape[1] == wide
-    packed = jnp.concatenate([first[:, :wide], bottom], axis=0).astype(BF)
-    out_ref[...] = jnp.broadcast_to(packed[None], out_ref.shape)
-
-
-def act_body(x_ref, w_ref, out_ref):
-    v = x_ref[...].astype(F32)
-    wide = v.shape[2]
+    packed = jnp.concatenate([first[:, :wide], bottom], axis=0)
+    joined = jnp.concatenate([packed, g], axis=1).astype(BF)
+    out_ref[...] = jnp.broadcast_to(joined[None], out_ref.shape)
+
+
+def act_body(x_ref, w_ref, out_ref, g_ref):
+    peers = [x_ref[c % 4, c // 4] for c in range(32)]
     full = w_ref.shape[0]
     half = full // 2
-    top, bottom = v[:, :8], v[:, 8:]
+    wide = x_ref.shape[3] - g_ref.shape[1]
     left = full - wide
-    first = jnp.concatenate([top, bottom[:, :, :left]], axis=2)
-    rest = bottom[:, :, left : left + half].reshape(v.shape[0] // 2, 2, 8, half)
-    even, odd = rest[:, 0], rest[:, 1]
-    head = lax.broadcasted_iota(jnp.int32, even.shape, 1) < 4
-    low = jnp.where(head, even, pltpu.roll(odd, 4, 1))
-    high = jnp.where(head, pltpu.roll(even, 4, 1), odd)
-    last = jnp.concatenate([low, high], axis=2)
-    pairs = first.reshape(v.shape[0] // 2, 16, full)
-    x = jnp.concatenate([pairs, last], axis=1).reshape(v.shape[0] * 12, full).astype(BF)
+    head = lax.broadcasted_iota(jnp.int32, (8, full), 0) < 4
+    near = lax.broadcasted_iota(jnp.int32, (8, half), 0) < 4
+    for c in range(32):
+        g_ref[c * 16 : c * 16 + 16] = peers[c][:, wide:]
+    lines = []
+    for core in range(2):
+        for y in range(8):
+            firsts, rests = [], []
+            for c in (4 * y + 2 * core, 4 * y + 2 * core + 1):
+                v = peers[c][:, :wide].astype(F32)
+                firsts.append(jnp.concatenate([v[:8], v[8:, :left]], axis=1))
+                rests.append(v[8:, left : left + half])
+            even, odd = rests
+            low = jnp.where(near, even, pltpu.roll(odd, 4, 0))
+            high = jnp.where(near, pltpu.roll(even, 4, 0), odd)
+            last = jnp.concatenate([low, high], axis=1)
+            turned = pltpu.roll(firsts[1], 4, 0)
+            lines += [firsts[0], jnp.where(head, last, turned), jnp.where(head, turned, last)]
+    x = jnp.concatenate(lines, axis=0).astype(BF)
     out_ref[...] = dot(x, w_ref[...]).astype(BF)
 
 
@@ -164,16 +179,16 @@
             out_ref[7 + a, 3 + i] = part[a * 16 : a * 16 + 16]
 
 
-def gram_sum_body(flag_ref, x_ref, out_ref):
+def gram_sum_body(x_ref, out_ref):
     total = jnp.sum(x_ref[...].astype(F32), axis=0)
     whole = total[3] + total[4] + total[5]
-    plain = flag_ref[0, 0] < 7
+    plain = lax.axis_index("y") * 2 + lax.axis_index("core") < 7
     parts = split3(whole)
     for i in range(6):
         tile = total[i].astype(BF)
         if i >= 3:
             tile = jnp.where(plain, total[i], parts[i - 3].astype(F32)).astype(BF)
-        out_ref[:, i] = jnp.broadcast_to(tile[None], (out_ref.shape[0], 16, 128))
+        out_ref[i] = tile
 
 
 def core_body(m_ref, s_ref, out_ref):
@@ -228,15 +243,16 @@
 
 
 def on_device(acts, grads, basis_in, basis_out, eigen, sketch):
-    g = grads.reshape(24, 256)
-    g = jnp.concatenate([g[0:8], g[12:20], g[8:12], g[20:24]], axis=0)
-    all_grads = swap(jnp.broadcast_to(g[None], (16, 24, 256)), ROW).reshape(384, 256)
-    packed = call(pack_body, ((32, 16, 1408), BF), acts.reshape(12, 1792))
-    all_acts = swap(packed, COL)
+    g = jnp.broadcast_to(grads.reshape(1, 24, 256), (16, 24, 256))
+    all_grads = swap(g, ROW).reshape(384, 256)
     g_part = call(grad_body, ((512, 512), BF), all_grads, sketch, basis_out)
-    g_rot = sum_over(g_part.reshape(32, 16, 512), COL).reshape(512, 512)
-    a_part = call(act_body, ((384, 896), BF), all_acts, basis_in)
-    a_rot = sum_over(a_part.reshape(16, 24, 896), ROW).reshape(384, 896)
+    own = swap(g_part.reshape(32, 16, 512), COL)
+    joined = call(join_body, ((8, 16, 1920), BF), own, acts.reshape(12, 1792))
+    near = swap(joined, "z")
+    both = swap(jnp.broadcast_to(near[None], (4, 8, 16, 1920)), "x")
+    a_part, g_rot = call(act_body, [((384, 896), BF), ((512, 512), BF)], both, basis_in)
+    a_own = summed(summed(a_part.reshape(2, 8, 24, 896), "core"), "y")
+    a_rot = lax.all_gather(a_own, ROW).reshape(384, 896)
     scaled, red = call(
         scaled_body, [((2, 896, 512), BF), ((16, 4, 16, 128), BF)], a_rot, g_rot, eigen
     )
@@ -244,8 +260,7 @@
     span = call(range_body, ((32, 4, 16, 128), BF), reduced, basis_in)
     span = sum_over(span, COL)
     mapped = swap(call(mapped_body, ((16, 6, 16, 128), BF), span, basis_in), ROW)
-    flag = jnp.full((1, 1), lax.axis_index(ROW), jnp.int32)
-    mapped = swap(call(gram_sum_body, ((16, 6, 16, 128), BF), flag, mapped), ROW)
+    mapped = lax.all_gather(call(gram_sum_body, ((6, 16, 128), BF), mapped), ROW)
     core = sum_over(call(core_body, ((32, 2, 16, 128), BF), mapped, scaled), COL)
     inverse = call(inverse_body, ((2, 72, 128), F32), mapped)
     basis = call(basis_body, ((2, 72, 1792), F32), inverse, span)

time: 346 us -> 314 us (0.908)
  blocking collectives: 159 us -> 259 us
  waiting for transfers between devices: 103 us -> 17.6 us
  starting transfers between devices: 49.4 us -> 15.5 us
  local copies, waits for them, and re-layouts: 10.1 us -> 2.64 us
  Pallas kernels: 21.6 us -> 16.9 us
    all_to_all x7 -> x2, waiting for transfers between devices: 103 us -> 17.6 us  [swap(): return lax.all_to_all(x, axes, 0, 0, tiled=True)]
    all_to_all x9 -> x13, blocking collectives: 159 us -> 227 us  [swap(): return lax.all_to_all(x, axes, 0, 0, tiled=True)]
    all_to_all x7 -> x2, starting transfers between devices: 49.4 us -> 15.5 us  [swap(): return lax.all_to_all(x, axes, 0, 0, tiled=True)]
    all_gather x0 -> x2, blocking collectives: none -> 32.4 us  [the longest x1 16.9 us: on_device(): a_rot = lax.all_gather(a_own, ROW).reshape(384, 896)]
    unnamed x28 -> x12, local copies, waits for them, and re-layouts: 7.19 us -> 1.74 us
    pallas_call x18, Pallas kernels: 21.6 us -> 16.9 us  [call(): pl.pallas_call(body, out_shape=shapes, in_specs=[pl.BlockSpec(memory_spac...]
  transfers between devices with their start and end apart: 7 -> 2, of which waited for: 7 -> 2; matrix products, arithmetic and copies ran while one was open for 0% -> 0% of each run, Pallas kernels for 4% -> 3%
where the time goes in v1:
time: 314 us; the launch traced here: 313 us
  blocking collectives  259 us (82%)
  waiting for transfers between devices  17.6 us (6%)
  Pallas kernels  16.9 us (5%)
  starting transfers between devices  15.5 us (5%)
    all_to_all x13, blocking collectives, swap(): return lax.all_to_all(x, axes, 0, 0, tiled=True)  227 us
    all_to_all x2, waiting for transfers between devices, swap(): return lax.all_to_all(x, axes, 0, 0, tiled=True)  17.6 us
    pallas_call x18, Pallas kernels, call(): pl.pallas_call(body, out_shape=shapes, in_specs=[pl.BlockSpec(memory_spac...  16.9 us
    all_gather x1, blocking collectives, on_device(): a_rot = lax.all_gather(a_own, ROW).reshape(384, 896)  16.9 us
    all_to_all x2, starting transfers between devices, swap(): return lax.all_to_all(x, axes, 0, 0, tiled=True)  15.5 us
    all_gather x1, blocking collectives, on_device(): lax.all_gather(call(gram_sum_body, ((6, 16, 128), BF), mapped), ROW)  15.5 us
  transfers between devices with their start and end apart: 2, of which 2 were waited for; matrix products, arithmetic and copies ran while one was open for 0% of the time, Pallas kernels for 3%

profile of v1, /device:TPU:1, one launch (start us, length us, event | category | flops | bytes accessed | tf_op | source)
XLA Modules:
  0.0 312.7 jit_solution(4578812535684798684)
XLA Ops:
  0.6 0.0 copy-start.5
  0.6 0.7 broadcast_in_dim.6
  1.4 19.7 %all_to_all.75 = bf16[16,24,256]{2,1,0:T(8,128)(2,1)S(1)} all-to-all(bf16[16,24,256]{2,1,0:T(8,128)(2,1)S(1)} %broadcast_in_dim.14), channel_id=1, replica_groups=mesh['y'=8,'core'=2,'z'=8,'x'=4] {'y','core'}, dimensions={0} | all-to-all | bytes 393216 | tf_op jit(solution)/shard_map/all_to_all | solution.py:32
  21.1 0.0 copy-start.1
  21.1 0.9 copy-done.1
  22.0 0.0 copy-start.4
  22.0 0.8 copy-done.4
  22.8 1.1 shard_map.77
  23.9 12.0 %all-to-all-start.1 = ((bf16[32,16,512]{2,1,0:T(8,128)(2,1)}), bf16[32,16,512]{2,1,0:T(8,128)(2,1)S(1)}, u32[]{:S(2)}, u32[]{:S(2)}) async-start(bf16[32,16,512]{2,1,0:T(8,128)(2,1)} %bitcast.1), calls=%async_computation.1 | async-start | bytes 1048576 | tf_op jit(solution)/shard_map/all_to_all | solution.py:32
  35.8 0.0 copy-done.5
  35.9 17.3 %all-to-all-done.1.own_ref = bf16[32,16,512]{2,1,0:T(8,128)(2,1)S(1)} async-done(((bf16[32,16,512]{2,1,0:T(8,128)(2,1)}), bf16[32,16,512]{2,1,0:T(8,128)(2,1)S(1)}, u32[]{:S(2)}, u32[]{:S(2)}) %all-to-all-start.1) | async-done | bytes 524320 | tf_op jit(solution)/shard_map/all_to_all | solution.py:32
  53.1 0.1 shard_map.78
  53.2 17.4 %all_to_all.76 = bf16[8,16,1920]{2,1,0:T(8,128)(2,1)S(1)} all-to-all(bf16[8,16,1920]{2,1,0:T(8,128)(2,1)S(1)} %shard_map.78), channel_id=1, replica_groups=mesh['y'=8,'core'=2,'z'=8,'x'=4] {'z'}, dimensions={0} | all-to-all | bytes 983040 | tf_op jit(solution)/shard_map/all_to_all | solution.py:32
  70.6 0.1 broadcast_in_dim.15
  70.8 0.0 copy-start
  70.8 27.2 %all_to_all.77.x_ref = bf16[4,8,16,1920]{3,2,1,0:T(8,128)(2,1)S(1)} all-to-all(bf16[4,8,16,1920]{3,2,1,0:T(8,128)(2,1)S(1)} %broadcast_in_dim.15), channel_id=1, replica_groups=mesh['y'=8,'core'=2,'z'=8,'x'=4] {'x'}, dimensions={0} | all-to-all | bytes 3932160 | tf_op jit(solution)/shard_map/all_to_all | solution.py:32
  98.0 0.0 copy-done
  98.0 1.6 shard_map.79
  99.6 0.0 copy-start.3
  99.6 7.3 %all_to_all.78.x_ref = bf16[2,8,24,896]{3,2,1,0:T(8,128)(2,1)S(1)} all-to-all(bf16[2,8,24,896]{3,2,1,0:T(8,128)(2,1)S(1)} %bitcast.7), channel_id=1, replica_groups=mesh['y'=8,'core'=2,'z'=8,'x'=4] {'core'}, dimensions={0} | all-to-all | bytes 1376256 | tf_op jit(solution)/shard_map/all_to_all | solution.py:32
  107.0 0.1 shard_map.80
  107.1 16.5 %all_to_all.79.x_ref = bf16[8,24,896]{2,1,0:T(8,128)(2,1)S(1)} all-to-all(bf16[8,24,896]{2,1,0:T(8,128)(2,1)S(1)} %shard_map.80), channel_id=1, replica_groups=mesh['y'=8,'core'=2,'z'=8,'x'=4] {'y'}, dimensions={0} | all-to-all | bytes 688128 | tf_op jit(solution)/shard_map/all_to_all | solution.py:32
  123.6 16.9 %all-gather.a_ref = bf16[384,896]{1,0:T(8,128)(2,1)S(1)} all-gather(bf16[24,896]{1,0:T(8,128)(2,1)S(1)} %shard_map.81), channel_id=2, replica_groups=mesh['y'=8,'core'=2,'z'=8,'x'=4] {'y','core'}, dimensions={0}, use_global_device_ids=true | all-gather | bytes 731136 | tf_op jit(solution)/shard_map/all_gather | solution.py:255
  140.5 0.0 copy-done.3
  140.5 1.6 shard_map.82
  142.1 15.4 %all_to_all.80.x_ref = bf16[16,4,16,128]{3,2,1,0:T(8,128)(2,1)S(1)} all-to-all(bf16[16,4,16,128]{3,2,1,0:T(8,128)(2,1)S(1)} %get-tuple-element.8), channel_id=1, replica_groups=mesh['y'=8,'core'=2,'z'=8,'x'=4] {'y','core'}, dimensions={0} | all-to-all | bytes 524288 | tf_op jit(solution)/shard_map/all_to_all | solution.py:32
  157.5 14.4 %all_to_all.81.r_ref = bf16[16,4,16,128]{3,2,1,0:T(8,128)(2,1)S(1)} all-to-all(bf16[16,4,16,128]{3,2,1,0:T(8,128)(2,1)S(1)} %shard_map.83), channel_id=1, replica_groups=mesh['y'=8,'core'=2,'z'=8,'x'=4] {'y','core'}, dimensions={0} | all-to-all | bytes 524288 | tf_op jit(solution)/shard_map/all_to_all | solution.py:32
  171.9 1.0 shard_map.84
  173.0 20.6 %all_to_all.82.x_ref = bf16[32,4,16,128]{3,2,1,0:T(8,128)(2,1)S(1)} all-to-all(bf16[32,4,16,128]{3,2,1,0:T(8,128)(2,1)S(1)} %shard_map.84), channel_id=1, replica_groups=mesh['y'=8,'core'=2,'z'=8,'x'=4] {'z','x'}, dimensions={0} | all-to-all | bytes 1048576 | tf_op jit(solution)/shard_map/all_to_all | solution.py:32
  193.5 0.1 shard_map.85
  193.7 20.0 %all_to_all.83.r_ref = bf16[32,4,16,128]{3,2,1,0:T(8,128)(2,1)S(1)} all-to-all(bf16[32,4,16,128]{3,2,1,0:T(8,128)(2,1)S(1)} %shard_map.85), channel_id=1, replica_groups=mesh['y'=8,'core'=2,'z'=8,'x'=4] {'z','x'}, dimensions={0} | all-to-all | bytes 1048576 | tf_op jit(solution)/shard_map/all_to_all | solution.py:32
  213.7 0.9 shard_map.86
  214.5 20.3 %all_to_all.84.x_ref = bf16[16,6,16,128]{3,2,1,0:T(8,128)(2,1)S(1)} all-to-all(bf16[16,6,16,128]{3,2,1,0:T(8,128)(2,1)S(1)} %shard_map.86), channel_id=1, replica_groups=mesh['y'=8,'core'=2,'z'=8,'x'=4] {'y','core'}, dimensions={0} | all-to-all | bytes 786432 | tf_op jit(solution)/shard_map/all_to_all | solution.py:32
  234.8 0.1 shard_map.87
  234.9 15.5 %all-gather.1 = bf16[96,16,128]{2,1,0:T(8,128)(2,1)S(1)} all-gather(bf16[6,16,128]{2,1,0:T(8,128)(2,1)S(1)} %shard_map.87), channel_id=3, replica_groups=mesh['y'=8,'core'=2,'z'=8,'x'=4] {'y','core'}, dimensions={0}, use_global_device_ids=true | all-gather | bytes 417792 | tf_op jit(solution)/shard_map/all_gather | solution.py:263
  250.4 0.0 copy-start.2
  250.5 0.4 shard_map.90
  250.9 15.9 %all_to_all.85.x_ref = bf16[32,2,16,128]{3,2,1,0:T(8,128)(2,1)S(1)} all-to-all(bf16[32,2,16,128]{3,2,1,0:T(8,128)(2,1)S(1)} %shard_map.90), channel_id=1, replica_groups=mesh['y'=8,'core'=2,'z'=8,'x'=4] {'z','x'}, dimensions={0} | all-to-all | bytes 524288 | tf_op jit(solution)/shard_map/all_to_all | solution.py:32
  266.8 0.1 shard_map.91
  266.9 14.8 %all_to_all.86.c_ref = bf16[32,2,16,128]{3,2,1,0:T(8,128)(2,1)S(1)} all-to-all(bf16[32,2,16,128]{3,2,1,0:T(8,128)(2,1)S(1)} %shard_map.91), channel_id=1, replica_groups=mesh['y'=8,'core'=2,'z'=8,'x'=4] {'z','x'}, dimensions={0} | all-to-all | bytes 524288 | tf_op jit(solution)/shard_map/all_to_all | solution.py:32
  281.6 0.0 copy-done.2
  281.7 0.2 shard_map.92
  281.9 17.2 %all_to_all.87.x_ref = bf16[16,2,16,128]{3,2,1,0:T(8,128)(2,1)S(1)} all-to-all(bf16[16,2,16,128]{3,2,1,0:T(8,128)(2,1)S(1)} %shard_map.92), channel_id=1, replica_groups=mesh['y'=8,'core'=2,'z'=8,'x'=4] {'y','core'}, dimensions={0} | all-to-all | bytes 262144 | tf_op jit(solution)/shard_map/all_to_all | solution.py:32
  299.1 0.7 shard_map.93
  299.8 3.6 %all-to-all-start.14 = ((bf16[16,2,16,128]{3,2,1,0:T(8,128)(2,1)}), bf16[16,2,16,128]{3,2,1,0:T(8,128)(2,1)S(1)}, u32[]{:S(2)}, u32[]{:S(2)}) async-start(bf16[16,2,16,128]{3,2,1,0:T(8,128)(2,1)} %shard_map.93), calls=%async_computation.14 | async-start | bytes 262144 | tf_op jit(solution)/shard_map/all_to_all | solution.py:32
  303.4 6.1 %shard_map.88.w_ref = f32[2,72,128]{2,1,0:T(8,128)S(1)} custom-call(bf16[16,6,16,128]{3,2,1,0:T(8,128)(2,1)S(1)} %bitcast.5), custom_call_target="tpu_custom_call" | custom-call | tf_op jit(solution)/shard_map/pallas_call | solution.py:21
  309.4 1.9 shard_map.89
  311.3 0.4 all-to-all-done.14.p_ref
  311.7 0.9 shard_map.94
  (4 shorter events, 0.1 us)
Async XLA Ops:
  0.6 35.2 %copy-start.5 = (bf16[6,2,1792]{2,1,0:T(2,128)(2,1)S(1)}, bf16[6,2,1792]{2,1,0:T(2,128)(2,1)}, u32[]{:S(2)}) copy-start(bf16[6,2,1792]{2,1,0:T(2,128)(2,1)} %param.6) | copy-start | bytes 129028
  21.1 1.0 copy-start.1
  22.0 0.8 copy-start.4
  23.9 29.3 %all-to-all-start.1 = ((bf16[32,16,512]{2,1,0:T(8,128)(2,1)}), bf16[32,16,512]{2,1,0:T(8,128)(2,1)S(1)}, u32[]{:S(2)}, u32[]{:S(2)}) async-start(bf16[32,16,512]{2,1,0:T(8,128)(2,1)} %bitcast.1), calls=%async_computation.1 | async-start | bytes 1048576 | tf_op jit(solution)/shard_map/all_to_all | solution.py:32
  70.8 27.2 %copy-start = (bf16[1792,896]{1,0:T(8,128)(2,1)S(1)}, bf16[1792,896]{1,0:T(8,128)(2,1)}, u32[]{:S(2)}) copy-start(bf16[1792,896]{1,0:T(8,128)(2,1)} %w_ref.8) | copy-start | bytes 9633796
  99.6 40.9 %copy-start.3 = (bf16[896,512]{1,0:T(8,128)(2,1)S(1)}, bf16[896,512]{1,0:T(8,128)(2,1)}, u32[]{:S(2)}) copy-start(bf16[896,512]{1,0:T(8,128)(2,1)} %e_ref.1) | copy-start | bytes 2752516
  250.4 31.2 %copy-start.2 = (bf16[256,512]{1,0:T(8,128)(2,1)S(1)}, bf16[256,512]{1,0:T(8,128)(2,1)}, u32[]{:S(2)}) copy-start(bf16[256,512]{1,0:T(8,128)(2,1)} %w_ref.9) | copy-start | bytes 786436
  299.8 12.0 %all-to-all-start.14 = ((bf16[16,2,16,128]{3,2,1,0:T(8,128)(2,1)}), bf16[16,2,16,128]{3,2,1,0:T(8,128)(2,1)S(1)}, u32[]{:S(2)}, u32[]{:S(2)}) async-start(bf16[16,2,16,128]{3,2,1,0:T(8,128)(2,1)} %shard_map.93), calls=%async_computation.14 | async-start | bytes 262144 | tf_op jit(solution)/shard_map/all_to_all | solution.py:32

commit v2 on v1

--- a/solution.py
+++ b/solution.py
@@ -71,41 +71,41 @@
     return call(sum_one_body, (own.shape[1:], BF), own)
 
 
+def add_body(a_ref, b_ref, out_ref):
+    out_ref[...] = (a_ref[...].astype(F32) + b_ref[...].astype(F32)).astype(BF)
+
+
 def sum_over(pieces, axes):
     own = swap(pieces, axes)
     return swap(call(sum_body, (own.shape, BF), own), axes)
 
 
-def join_body(own_ref, x_ref, out_ref):
-    g = jnp.sum(own_ref[...].astype(F32), axis=0)
+def pack_body(x_ref, out_ref):
     x = x_ref[...].astype(F32)
     half = x.shape[1] // 2
-    wide = out_ref.shape[2] - g.shape[1]
+    wide = out_ref.shape[2]
     first, rest = x[:8], x[8:]
     rest = jnp.concatenate([rest[:, :half], rest[:, half:]], axis=0)
     spare = jnp.zeros((8, 2 * wide - x.shape[1] - half), F32)
     bottom = jnp.concatenate([first[:, wide:], rest, spare], axis=1)
-    packed = jnp.concatenate([first[:, :wide], bottom], axis=0)
-    joined = jnp.concatenate([packed, g], axis=1).astype(BF)
-    out_ref[...] = jnp.broadcast_to(joined[None], out_ref.shape)
-
-
-def act_body(x_ref, w_ref, out_ref, g_ref):
+    packed = jnp.concatenate([first[:, :wide], bottom], axis=0).astype(BF)
+    out_ref[...] = jnp.broadcast_to(packed[None], out_ref.shape)
+
+
+def act_body(x_ref, w_ref, keep_ref, out_ref):
     peers = [x_ref[c % 4, c // 4] for c in range(32)]
     full = w_ref.shape[0]
     half = full // 2
-    wide = x_ref.shape[3] - g_ref.shape[1]
+    wide = x_ref.shape[3]
     left = full - wide
     head = lax.broadcasted_iota(jnp.int32, (8, full), 0) < 4
     near = lax.broadcasted_iota(jnp.int32, (8, half), 0) < 4
-    for c in range(32):
-        g_ref[c * 16 : c * 16 + 16] = peers[c][:, wide:]
     lines = []
     for core in range(2):
         for y in range(8):
             firsts, rests = [], []
             for c in (4 * y + 2 * core, 4 * y + 2 * core + 1):
-                v = peers[c][:, :wide].astype(F32)
+                v = peers[c].astype(F32)
                 firsts.append(jnp.concatenate([v[:8], v[8:, :left]], axis=1))
                 rests.append(v[8:, left : left + half])
             even, odd = rests
@@ -115,7 +115,11 @@
             turned = pltpu.roll(firsts[1], 4, 0)
             lines += [firsts[0], jnp.where(head, last, turned), jnp.where(head, turned, last)]
     x = jnp.concatenate(lines, axis=0).astype(BF)
-    out_ref[...] = dot(x, w_ref[...]).astype(BF)
+    y = dot(x, w_ref[...])
+    n = out_ref.shape[0]
+    first = lax.axis_index("core") == 0
+    keep_ref[...] = jnp.where(first, y[:n], y[n:]).astype(BF)
+    out_ref[...] = jnp.where(first, y[n:], y[:n]).astype(BF)
 
 
 def grad_body(g_ref, s_ref, w_ref, out_ref):
@@ -243,15 +247,21 @@
 
 
 def on_device(acts, grads, basis_in, basis_out, eigen, sketch):
-    g = jnp.broadcast_to(grads.reshape(1, 24, 256), (16, 24, 256))
-    all_grads = swap(g, ROW).reshape(384, 256)
+    packed = call(pack_body, ((8, 16, 1408), BF), acts.reshape(12, 1792))
+    near = swap(packed, "z")
+    all_grads = lax.all_gather(grads.reshape(24, 256), ROW).reshape(384, 256)
+    near, all_grads = lax.optimization_barrier((near, all_grads))
     g_part = call(grad_body, ((512, 512), BF), all_grads, sketch, basis_out)
-    own = swap(g_part.reshape(32, 16, 512), COL)
-    joined = call(join_body, ((8, 16, 1920), BF), own, acts.reshape(12, 1792))
-    near = swap(joined, "z")
-    both = swap(jnp.broadcast_to(near[None], (4, 8, 16, 1920)), "x")
-    a_part, g_rot = call(act_body, [((384, 896), BF), ((512, 512), BF)], both, basis_in)
-    a_own = summed(summed(a_part.reshape(2, 8, 24, 896), "core"), "y")
+    both = swap(jnp.broadcast_to(near[None], (4, 8, 16, 1408)), "x")
+    both, g_part = lax.optimization_barrier((both, g_part))
+    g_own = summed(g_part.reshape(32, 16, 512), COL)
+    keep, give = call(act_body, [((192, 896), BF), ((192, 896), BF)], both, basis_in)
+    give = lax.ppermute(give, "core", [(0, 1), (1, 0)])
+    a_pair = call(add_body, ((192, 896), BF), keep, give)
+    a_pair, g_own = lax.optimization_barrier((a_pair, g_own))
+    a_own = summed(a_pair.reshape(8, 24, 896), "y")
+    a_own, g_own = lax.optimization_barrier((a_own, g_own))
+    g_rot = swap(jnp.broadcast_to(g_own[None], (32, 16, 512)), COL).reshape(512, 512)
     a_rot = lax.all_gather(a_own, ROW).reshape(384, 896)
     scaled, red = call(
         scaled_body, [((2, 896, 512), BF), ((16, 4, 16, 128), BF)], a_rot, g_rot, eigen

time: 314 us -> 310 us (0.987)
  blocking collectives: 259 us -> 215 us
  starting transfers between devices: 15.5 us -> 38.2 us
  waiting for transfers between devices: 17.6 us -> 26.8 us
  local copies, waits for them, and re-layouts: 2.64 us -> 7.61 us
  Pallas kernels: 16.9 us -> 20.3 us
    all_to_all x13 -> x9, blocking collectives: 227 us -> 159 us  [swap(): return lax.all_to_all(x, axes, 0, 0, tiled=True)]
    all_gather x0 -> x1, blocking collectives: none -> 20.3 us  [on_device(): all_grads = lax.all_gather(grads.reshape(24, 256), ROW).reshape(384, 256)]
    all_to_all x2 -> x5, starting transfers between devices: 15.5 us -> 35 us  [swap(): return lax.all_to_all(x, axes, 0, 0, tiled=True)]
    all_to_all x2 -> x5, waiting for transfers between devices: 17.6 us -> 25.5 us  [swap(): return lax.all_to_all(x, axes, 0, 0, tiled=True)]
    all_gather x1, blocking collectives: 16.9 us -> 20.8 us  [on_device(): a_rot = lax.all_gather(a_own, ROW).reshape(384, 896)]
    pallas_call x18 -> x19, Pallas kernels: 16.9 us -> 20.3 us  [call(): pl.pallas_call(body, out_shape=shapes, in_specs=[pl.BlockSpec(memory_spac...]
    ppermute x0 -> x1, starting transfers between devices: none -> 3.16 us  [on_device(): give = lax.ppermute(give, 'core', [(0, 1), (1, 0)])]
  transfers between devices with their start and end apart: 2 -> 6, of which waited for: 2 -> 4; matrix products, arithmetic and copies ran while one was open for 0% -> 0% of each run, Pallas kernels for 3% -> 4%
where the time goes in v2:
time: 310 us; the launch traced here: 309 us
  blocking collectives  215 us (69%)
  starting transfers between devices  38.2 us (12%)
  waiting for transfers between devices  26.8 us (9%)
  Pallas kernels  20.3 us (7%)
  local copies, waits for them, and re-layouts  7.61 us (2%)
    all_to_all x9, blocking collectives, swap(): return lax.all_to_all(x, axes, 0, 0, tiled=True)  159 us
    all_to_all x5, starting transfers between devices, swap(): return lax.all_to_all(x, axes, 0, 0, tiled=True)  35 us
    all_to_all x5, waiting for transfers between devices, swap(): return lax.all_to_all(x, axes, 0, 0, tiled=True)  25.5 us
    all_gather x1, blocking collectives, on_device(): a_rot = lax.all_gather(a_own, ROW).reshape(384, 896)  20.8 us
    all_gather x1, blocking collectives, on_device(): all_grads = lax.all_gather(grads.reshape(24, 256), ROW).reshape(384, 256)  20.3 us
    pallas_call x19, Pallas kernels, call(): pl.pallas_call(body, out_shape=shapes, in_specs=[pl.BlockSpec(memory_spac...  20.3 us
    all_gather x1, blocking collectives, on_device(): lax.all_gather(call(gram_sum_body, ((6, 16, 128), BF), mapped), ROW)  15.5 us
  transfers between devices with their start and end apart: 6, of which 4 were waited for; matrix products, arithmetic and copies ran while one was open for 0% of the time, Pallas kernels for 4%

profile of v2, /device:TPU:1, one launch (start us, length us, event | category | flops | bytes accessed | tf_op | source)
XLA Modules:
  0.0 309.1 jit_solution(2179597329720240983)
XLA Ops:
  0.6 0.8 reshape.24.x_ref
  1.4 0.8 shard_map.77
  2.2 10.9 %all-to-all-start = ((bf16[8,16,1408]{2,1,0:T(8,128)(2,1)}), bf16[8,16,1408]{2,1,0:T(8,128)(2,1)S(1)}, u32[]{:S(2)}, u32[]{:S(2)}) async-start(bf16[8,16,1408]{2,1,0:T(8,128)(2,1)} %shard_map.77), calls=%async_computation | async-start | bytes 720896 | tf_op jit(solution)/shard_map/all_to_all | solution.py:32
  13.1 0.7 all_gather_reshape.3
  13.8 20.3 %all_gather.15 = bf16[16,24,256]{2,1,0:T(8,128)(2,1)} all-gather(bf16[1,24,256]{2,1,0:T(8,128)(2,1)S(1)} %all_gather_reshape.3), channel_id=1, replica_groups=mesh['y'=8,'core'=2,'z'=8,'x'=4] {'y','core'}, dimensions={0}, use_global_device_ids=true | all-gather | bytes 208896 | tf_op jit(solution)/shard_map/all_gather | solution.py:252
  34.1 0.0 all-to-all-done
  34.1 0.0 copy-start.5
  34.1 0.0 copy-start.9
  34.1 1.2 broadcast_in_dim.4
  35.3 0.0 copy-start
  35.3 4.6 %all-to-all-start.1 = ((bf16[4,8,16,1408]{3,2,1,0:T(8,128)(2,1)}), bf16[4,8,16,1408]{3,2,1,0:T(8,128)(2,1)}, u32[]{:S(2)}, u32[]{:S(2)}) async-start(bf16[4,8,16,1408]{3,2,1,0:T(8,128)(2,1)} %broadcast_in_dim.4), calls=%async_computation.1 | async-start | bytes 2883584 | tf_op jit(solution)/shard_map/all_to_all | solution.py:32
  39.9 0.0 copy-done.5
  39.9 0.0 copy-done.9
  39.9 0.0 copy-start.8
  39.9 0.9 copy-done.8
  40.9 0.3 shard_map.78
  41.1 0.0 copy-start.4
  41.2 0.8 copy-done.4
  41.9 17.3 %all-to-all-done.1.x_ref = bf16[4,8,16,1408]{3,2,1,0:T(8,128)(2,1)} async-done(((bf16[4,8,16,1408]{3,2,1,0:T(8,128)(2,1)}), bf16[4,8,16,1408]{3,2,1,0:T(8,128)(2,1)}, u32[]{:S(2)}, u32[]{:S(2)}) %all-to-all-start.1) | async-done | bytes 1441824 | tf_op jit(solution)/shard_map/all_to_all | solution.py:32
  59.3 8.0 %all-to-all-start.2 = ((bf16[32,16,512]{2,1,0:T(8,128)(2,1)}), bf16[32,16,512]{2,1,0:T(8,128)(2,1)}, u32[]{:S(2)}, u32[]{:S(2)}) async-start(bf16[32,16,512]{2,1,0:T(8,128)(2,1)} %bitcast.7), calls=%async_computation.2 | async-start | bytes 1048576 | tf_op jit(solution)/shard_map/all_to_all | solution.py:32
  67.3 0.0 copy-done
  67.3 3.0 shard_map.79
  70.3 3.2 %collective-permute-start = (bf16[192,896]{1,0:T(8,128)(2,1)S(1)}, bf16[192,896]{1,0:T(8,128)(2,1)S(1)}, u32[]{:S(2)}, u32[]{:S(2)}) collective-permute-start(bf16[192,896]{1,0:T(8,128)(2,1)S(1)} %get-tuple-element.18), channel_id=1, source_target_pairs={{0,32},{32,0},{1,33},{33,1},{2,34},{34,2},{3,35},{35,3},{4,36},{36... | collective-permute-start | bytes 1032200 | tf_op jit(solution)/shard_map/ppermute | solution.py:259
  73.5 1.3 collective-permute-done.b_ref
  74.7 0.1 shard_map.80
  74.8 7.9 %all-to-all-done.2.x_ref = bf16[32,16,512]{2,1,0:T(8,128)(2,1)} async-done(((bf16[32,16,512]{2,1,0:T(8,128)(2,1)}), bf16[32,16,512]{2,1,0:T(8,128)(2,1)}, u32[]{:S(2)}, u32[]{:S(2)}) %all-to-all-start.2) | async-done | bytes 524320 | tf_op jit(solution)/shard_map/all_to_all | solution.py:32
  82.7 1.1 shard_map.81
  83.8 14.1 %all_to_all.70.x_ref = bf16[8,24,896]{2,1,0:T(8,128)(2,1)S(1)} all-to-all(bf16[8,24,896]{2,1,0:T(8,128)(2,1)S(1)} %bitcast.8), channel_id=1, replica_groups=mesh['y'=8,'core'=2,'z'=8,'x'=4] {'y'}, dimensions={0} | all-to-all | bytes 688128 | tf_op jit(solution)/shard_map/all_to_all | solution.py:32
  97.9 0.9 broadcast_in_dim.5
  98.8 7.9 %all-to-all-start.4 = ((bf16[32,16,512]{2,1,0:T(8,128)(2,1)}), bf16[32,16,512]{2,1,0:T(8,128)(2,1)}, u32[]{:S(2)}, u32[]{:S(2)}) async-start(bf16[32,16,512]{2,1,0:T(8,128)(2,1)} %broadcast_in_dim.5), calls=%async_computation.4 | async-start | bytes 1048576 | tf_op jit(solution)/shard_map/all_to_all | solution.py:32
  106.7 20.8 %all-gather.a_ref = bf16[384,896]{1,0:T(8,128)(2,1)} all-gather(bf16[24,896]{1,0:T(8,128)(2,1)S(1)} %shard_map.82), channel_id=2, replica_groups=mesh['y'=8,'core'=2,'z'=8,'x'=4] {'y','core'}, dimensions={0}, use_global_device_ids=true | all-gather | bytes 731136 | tf_op jit(solution)/shard_map/all_gather | solution.py:265
  127.4 0.0 all-to-all-done.4
  127.4 0.0 copy-start.3
  127.4 1.1 copy-done.3
  128.5 0.0 copy-start.7
  128.5 1.2 copy-done.7
  129.7 2.6 shard_map.83
  132.3 15.4 %all_to_all.71.x_ref = bf16[16,4,16,128]{3,2,1,0:T(8,128)(2,1)S(1)} all-to-all(bf16[16,4,16,128]{3,2,1,0:T(8,128)(2,1)S(1)} %get-tuple-element.24), channel_id=1, replica_groups=mesh['y'=8,'core'=2,'z'=8,'x'=4] {'y','core'}, dimensions={0} | all-to-all | bytes 524288 | tf_op jit(solution)/shard_map/all_to_all | solution.py:32
  147.8 14.4 %all_to_all.72.r_ref = bf16[16,4,16,128]{3,2,1,0:T(8,128)(2,1)S(1)} all-to-all(bf16[16,4,16,128]{3,2,1,0:T(8,128)(2,1)S(1)} %shard_map.84), channel_id=1, replica_groups=mesh['y'=8,'core'=2,'z'=8,'x'=4] {'y','core'}, dimensions={0} | all-to-all | bytes 524288 | tf_op jit(solution)/shard_map/all_to_all | solution.py:32
  162.2 1.0 shard_map.85
  163.2 26.6 %all_to_all.73.x_ref = bf16[32,4,16,128]{3,2,1,0:T(8,128)(2,1)S(1)} all-to-all(bf16[32,4,16,128]{3,2,1,0:T(8,128)(2,1)S(1)} %shard_map.85), channel_id=1, replica_groups=mesh['y'=8,'core'=2,'z'=8,'x'=4] {'z','x'}, dimensions={0} | all-to-all | bytes 1048576 | tf_op jit(solution)/shard_map/all_to_all | solution.py:32
  189.8 0.1 shard_map.86
  189.9 20.0 %all_to_all.74.r_ref = bf16[32,4,16,128]{3,2,1,0:T(8,128)(2,1)S(1)} all-to-all(bf16[32,4,16,128]{3,2,1,0:T(8,128)(2,1)S(1)} %shard_map.86), channel_id=1, replica_groups=mesh['y'=8,'core'=2,'z'=8,'x'=4] {'z','x'}, dimensions={0} | all-to-all | bytes 1048576 | tf_op jit(solution)/shard_map/all_to_all | solution.py:32
  209.9 0.0 copy-start.1
  209.9 0.9 shard_map.87
  210.8 0.0 copy-done.1
  210.8 20.3 %all_to_all.75.x_ref = bf16[16,6,16,128]{3,2,1,0:T(8,128)(2,1)S(1)} all-to-all(bf16[16,6,16,128]{3,2,1,0:T(8,128)(2,1)S(1)} %shard_map.87), channel_id=1, replica_groups=mesh['y'=8,'core'=2,'z'=8,'x'=4] {'y','core'}, dimensions={0} | all-to-all | bytes 786432 | tf_op jit(solution)/shard_map/all_to_all | solution.py:32
  231.1 0.1 shard_map.88
  231.2 15.5 %all-gather.1 = bf16[96,16,128]{2,1,0:T(8,128)(2,1)S(1)} all-gather(bf16[6,16,128]{2,1,0:T(8,128)(2,1)S(1)} %shard_map.88), channel_id=3, replica_groups=mesh['y'=8,'core'=2,'z'=8,'x'=4] {'y','core'}, dimensions={0}, use_global_device_ids=true | all-gather | bytes 417792 | tf_op jit(solution)/shard_map/all_gather | solution.py:273
  246.7 0.4 shard_map.91
  247.2 0.0 copy-start.2
  247.2 16.1 %all_to_all.76.x_ref = bf16[32,2,16,128]{3,2,1,0:T(8,128)(2,1)S(1)} all-to-all(bf16[32,2,16,128]{3,2,1,0:T(8,128)(2,1)S(1)} %shard_map.91), channel_id=1, replica_groups=mesh['y'=8,'core'=2,'z'=8,'x'=4] {'z','x'}, dimensions={0} | all-to-all | bytes 524288 | tf_op jit(solution)/shard_map/all_to_all | solution.py:32
  263.3 0.1 shard_map.92
  263.3 14.8 %all_to_all.77.c_ref = bf16[32,2,16,128]{3,2,1,0:T(8,128)(2,1)S(1)} all-to-all(bf16[32,2,16,128]{3,2,1,0:T(8,128)(2,1)S(1)} %shard_map.92), channel_id=1, replica_groups=mesh['y'=8,'core'=2,'z'=8,'x'=4] {'z','x'}, dimensions={0} | all-to-all | bytes 524288 | tf_op jit(solution)/shard_map/all_to_all | solution.py:32
  278.1 0.0 copy-done.6
  278.1 0.2 shard_map.93
  278.3 17.2 %all_to_all.78.x_ref = bf16[16,2,16,128]{3,2,1,0:T(8,128)(2,1)S(1)} all-to-all(bf16[16,2,16,128]{3,2,1,0:T(8,128)(2,1)S(1)} %shard_map.93), channel_id=1, replica_groups=mesh['y'=8,'core'=2,'z'=8,'x'=4] {'y','core'}, dimensions={0} | all-to-all | bytes 262144 | tf_op jit(solution)/shard_map/all_to_all | solution.py:32
  295.5 0.7 shard_map.94
  296.2 3.6 %all-to-all-start.13 = ((bf16[16,2,16,128]{3,2,1,0:T(8,128)(2,1)}), bf16[16,2,16,128]{3,2,1,0:T(8,128)(2,1)S(1)}, u32[]{:S(2)}, u32[]{:S(2)}) async-start(bf16[16,2,16,128]{3,2,1,0:T(8,128)(2,1)} %shard_map.94), calls=%async_computation.13 | async-start | bytes 262144 | tf_op jit(solution)/shard_map/all_to_all | solution.py:32
  299.8 6.1 %shard_map.89.w_ref = f32[2,72,128]{2,1,0:T(8,128)S(1)} custom-call(bf16[16,6,16,128]{3,2,1,0:T(8,128)(2,1)S(1)} %bitcast.6), custom_call_target="tpu_custom_call" | custom-call | tf_op jit(solution)/shard_map/pallas_call | solution.py:21
  305.9 0.0 copy-done.2
  305.9 1.9 shard_map.90
  307.8 0.4 all-to-all-done.13.p_ref
  308.2 0.9 shard_map.95
  (3 shorter events, 0.1 us)
Async XLA Ops:
  2.2 31.9 %all-to-all-start = ((bf16[8,16,1408]{2,1,0:T(8,128)(2,1)}), bf16[8,16,1408]{2,1,0:T(8,128)(2,1)S(1)}, u32[]{:S(2)}, u32[]{:S(2)}) async-start(bf16[8,16,1408]{2,1,0:T(8,128)(2,1)} %shard_map.77), calls=%async_computation | async-start | bytes 720896 | tf_op jit(solution)/shard_map/all_to_all | solution.py:32
  34.1 5.8 %copy-start.5 = (bf16[256,512]{1,0:T(8,128)(2,1)S(1)}, bf16[256,512]{1,0:T(8,128)(2,1)}, u32[]{:S(2)}) copy-start(bf16[256,512]{1,0:T(8,128)(2,1)} %w_ref.9) | copy-start | bytes 786436
  34.1 5.8 %copy-start.9 = (bf16[72,256]{1,0:T(8,128)(2,1)S(1)}, bf16[72,256]{1,0:T(8,128)(2,1)}, u32[]{:S(2)}) copy-start(bf16[72,256]{1,0:T(8,128)(2,1)} %s_ref.1) | copy-start | bytes 110596
  35.3 32.0 %copy-start = (bf16[1792,896]{1,0:T(8,128)(2,1)S(1)}, bf16[1792,896]{1,0:T(8,128)(2,1)}, u32[]{:S(2)}) copy-start(bf16[1792,896]{1,0:T(8,128)(2,1)} %w_ref.8) | copy-start | bytes 9633796
  35.3 23.9 %all-to-all-start.1 = ((bf16[4,8,16,1408]{3,2,1,0:T(8,128)(2,1)}), bf16[4,8,16,1408]{3,2,1,0:T(8,128)(2,1)}, u32[]{:S(2)}, u32[]{:S(2)}) async-start(bf16[4,8,16,1408]{3,2,1,0:T(8,128)(2,1)} %broadcast_in_dim.4), calls=%async_computation.1 | async-start | bytes 2883584 | tf_op jit(solution)/shard_map/all_to_all | solution.py:32
  39.9 0.9 copy-start.8
  41.1 0.8 copy-start.4
  59.3 23.4 %all-to-all-start.2 = ((bf16[32,16,512]{2,1,0:T(8,128)(2,1)}), bf16[32,16,512]{2,1,0:T(8,128)(2,1)}, u32[]{:S(2)}, u32[]{:S(2)}) async-start(bf16[32,16,512]{2,1,0:T(8,128)(2,1)} %bitcast.7), calls=%async_computation.2 | async-start | bytes 1048576 | tf_op jit(solution)/shard_map/all_to_all | solution.py:32
  70.3 4.4 %collective-permute-start = (bf16[192,896]{1,0:T(8,128)(2,1)S(1)}, bf16[192,896]{1,0:T(8,128)(2,1)S(1)}, u32[]{:S(2)}, u32[]{:S(2)}) collective-permute-start(bf16[192,896]{1,0:T(8,128)(2,1)S(1)} %get-tuple-element.18), channel_id=1, source_target_pairs={{0,32},{32,0},{1,33},{33,1},{2,34},{34,2},{3,35},{35,3},{4,36},{36... | collective-permute-start | bytes 1032200 | tf_op jit(solution)/shard_map/ppermute | solution.py:259
  98.8 28.7 %all-to-all-start.4 = ((bf16[32,16,512]{2,1,0:T(8,128)(2,1)}), bf16[32,16,512]{2,1,0:T(8,128)(2,1)}, u32[]{:S(2)}, u32[]{:S(2)}) async-start(bf16[32,16,512]{2,1,0:T(8,128)(2,1)} %broadcast_in_dim.5), calls=%async_computation.4 | async-start | bytes 1048576 | tf_op jit(solution)/shard_map/all_to_all | solution.py:32
  127.4 1.1 copy-start.3
  128.5 1.2 copy-start.7
  209.9 0.9 copy-start.1
  246.7 31.4 %copy-start.6 = (bf16[256,512]{1,0:T(8,128)(2,1)S(1)}, bf16[256,512]{1,0:T(8,128)(2,1)}, u32[]{:S(2)}) copy-start(bf16[256,512]{1,0:T(8,128)(2,1)} %w_ref.9) | copy-start | bytes 786436
  247.2 58.7 %copy-start.2 = (bf16[32,4,16,128]{3,2,1,0:T(8,128)(2,1)S(1)}, bf16[32,4,16,128]{3,2,1,0:T(8,128)(2,1)}, u32[]{:S(2)}) copy-start(bf16[32,4,16,128]{3,2,1,0:T(8,128)(2,1)} %copy-done.1) | copy-start | bytes 1572868
  296.2 12.0 %all-to-all-start.13 = ((bf16[16,2,16,128]{3,2,1,0:T(8,128)(2,1)}), bf16[16,2,16,128]{3,2,1,0:T(8,128)(2,1)S(1)}, u32[]{:S(2)}, u32[]{:S(2)}) async-start(bf16[16,2,16,128]{3,2,1,0:T(8,128)(2,1)} %shard_map.94), calls=%async_computation.13 | async-start | bytes 262144 | tf_op jit(solution)/shard_map/all_to_all | solution.py:32

commit v3 on v2

--- a/solution.py
+++ b/solution.py
@@ -36,24 +36,25 @@
     return lax.dot_general(a, b, (((ca,), (cb,)), ((), ())), preferred_element_type=F32, **kw)
 
 
-def to_tiles(y, out_ref, slots):
+def to_tiles(y, out_ref):
+    slots, high = out_ref.shape[1:3]
     lanes = y.shape[1] // 128
-    count = (y.shape[0] // 16) * lanes
-    y = y.astype(BF)
+    count = (y.shape[0] // high) * lanes
     for t in range(out_ref.shape[0] * slots):
         if t < count:
             r, g = divmod(t, lanes)
-            tile = y[r * 16 : r * 16 + 16, g * 128 : g * 128 + 128]
+            tile = y[r * high : r * high + high, g * 128 : g * 128 + 128]
         else:
-            tile = jnp.zeros((16, 128), BF)
-        out_ref[t // slots, t % slots] = tile
-
-
-def from_tiles(ref, slots, rows, lanes):
+            tile = jnp.zeros((high, 128), F32)
+        out_ref[t // slots, t % slots] = tile.astype(BF)
+
+
+def from_tiles(ref, lanes):
+    slots, high = ref.shape[1:3]
     lines = []
-    for r in range(rows):
+    for r in range(144 // high):
         at = [divmod(r * lanes + g, slots) for g in range(lanes)]
-        lines.append(jnp.concatenate([ref[p, s] for p, s in at], axis=1))
+        lines.append(jnp.concatenate([ref[p, s].astype(F32) for p, s in at], axis=1))
     return jnp.concatenate(lines, axis=0)
 
 
@@ -144,75 +145,35 @@
         s = (dot(a, mine) / e).astype(BF)
         scaled_ref[q] = s
         parts.append(dot(sk, s, 1, 1)[:72])
-    to_tiles(jnp.concatenate(parts, axis=0), out_ref, out_ref.shape[1])
+    to_tiles(jnp.concatenate(parts, axis=0), out_ref)
 
 
 def range_body(r_ref, w_ref, out_ref):
-    r = from_tiles(r_ref, 4, 9, 7)
-    to_tiles(dot(r, w_ref[...], 1, 1), out_ref, 4)
-
-
-def mapped_slot(t):
-    return divmod(t, 6) if t < 42 else (7 + (t - 42) // 3, (t - 42) % 3)
-
-
-def split3(x):
-    hi = x.astype(BF)
-    left = x - hi.astype(F32)
-    mid = left.astype(BF)
-    return hi, mid, (left - mid.astype(F32)).astype(BF)
-
-
-def mapped_body(r_ref, w_ref, out_ref):
-    r = from_tiles(r_ref, 4, 9, 14)
-    y = dot(r, w_ref[...]).astype(BF)
-    for t in range(69):
-        p, s = mapped_slot(t)
-        a, g = divmod(t, 7)
-        tile = y[a * 16 : a * 16 + 16, g * 128 : g * 128 + 128] if t < 63 else jnp.zeros((16, 128), BF)
-        out_ref[p, s] = tile
-    wide = r.astype(F32)
-    grams = []
-    for q in range(2):
-        rq = wide[q * 72 : q * 72 + 72].astype(BF)
-        g = dot(rq, rq, 1, 1)
-        grams.append(jnp.concatenate([g, jnp.zeros((72, 56), F32)], axis=1))
-    gram = jnp.concatenate(grams, axis=0)
-    for i, part in enumerate(split3(gram)):
-        for a in range(9):
-            out_ref[7 + a, 3 + i] = part[a * 16 : a * 16 + 16]
-
-
-def gram_sum_body(x_ref, out_ref):
-    total = jnp.sum(x_ref[...].astype(F32), axis=0)
-    whole = total[3] + total[4] + total[5]
-    plain = lax.axis_index("y") * 2 + lax.axis_index("core") < 7
-    parts = split3(whole)
-    for i in range(6):
-        tile = total[i].astype(BF)
-        if i >= 3:
-            tile = jnp.where(plain, total[i], parts[i - 3].astype(F32)).astype(BF)
-        out_ref[i] = tile
+    r = from_tiles(r_ref, 7).astype(BF)
+    to_tiles(dot(r, w_ref[...], 1, 1), out_ref)
+
+
+def mapped_body(r_ref, w_ref, out_ref, gram_ref):
+    r = from_tiles(r_ref, 14)
+    to_tiles(dot(r.astype(BF), w_ref[...]), out_ref)
+    for q in range(2):
+        rq = r[q * 72 : q * 72 + 72].astype(BF)
+        gram_ref[q] = dot(rq, rq, 1, 1)
 
 
 def core_body(m_ref, s_ref, out_ref):
-    tiles = [m_ref[mapped_slot(t)] for t in range(63)]
-    m = jnp.concatenate(
-        [jnp.concatenate(tiles[r * 7 : r * 7 + 7], axis=1) for r in range(9)], axis=0
-    ).astype(F32)
+    m = from_tiles(m_ref, 7)
     parts = [dot(m[q * 72 : q * 72 + 72].astype(BF), s_ref[q]) for q in range(2)]
-    to_tiles(jnp.concatenate(parts, axis=0), out_ref, 2)
+    to_tiles(jnp.concatenate(parts, axis=0), out_ref)
 
 
 def inverse_body(m_ref, out_ref):
-    gram = jnp.concatenate(
-        [sum(m_ref[7 + a, 3 + i].astype(F32) for i in range(3)) for a in range(9)], axis=0
-    )
     rows = lax.broadcasted_iota(jnp.int32, (72, 128), 0)
     lanes = lax.broadcasted_iota(jnp.int32, (72, 128), 1)
     below = lax.broadcasted_iota(jnp.int32, (72, 1), 0)
     eye = jnp.where(rows == lanes, 1.0, 0.0)
-    left = [gram[q * 72 : q * 72 + 72] for q in range(2)]
+    spare = jnp.zeros((72, 56), F32)
+    left = [jnp.concatenate([jnp.sum(m_ref[:, q], axis=0), spare], axis=1) for q in range(2)]
     right = [eye, eye]
     for k in range(72):
         for q in range(2):
@@ -228,29 +189,34 @@
 
 
 def basis_body(w_ref, r_ref, out_ref):
-    r = from_tiles(r_ref, 4, 9, 14).astype(F32)
+    r = from_tiles(r_ref, 14)
     for q in range(2):
         w = w_ref[q][:, :72]
         out_ref[q] = dot(w, r[q * 72 : q * 72 + 72], precision=lax.Precision.HIGHEST)
 
 
 def project_body(c_ref, w_ref, out_ref):
-    c = from_tiles(c_ref, 2, 9, 4)
-    to_tiles(dot(c, w_ref[...], 1, 1), out_ref, 2)
+    c = from_tiles(c_ref, 4).astype(BF)
+    out_ref[...] = dot(c, w_ref[...], 1, 1).astype(BF)
+
+
+def query_body(p_ref, out_ref):
+    p = p_ref[0].astype(F32) + p_ref[1].astype(F32)
+    mine = jnp.where(lax.axis_index("core") == 0, p[:72], p[72:]).astype(BF)
+    out_ref[...] = jnp.broadcast_to(mine[None], out_ref.shape)
 
 
 def final_body(w_ref, p_ref, out_ref):
-    p = from_tiles(p_ref, 2, 9, 2).astype(F32)
-    for q in range(2):
-        w = w_ref[q][:, :72]
-        out_ref[q] = dot(w, p[q * 72 : q * 72 + 72], precision=lax.Precision.HIGHEST)
+    p = jnp.sum(p_ref[...].astype(F32), axis=0)
+    w = jnp.where(lax.axis_index("core") == 0, w_ref[0], w_ref[1])[:, :72]
+    out_ref[...] = dot(w, p, precision=lax.Precision.HIGHEST)
 
 
 def on_device(acts, grads, basis_in, basis_out, eigen, sketch):
     packed = call(pack_body, ((8, 16, 1408), BF), acts.reshape(12, 1792))
     near = swap(packed, "z")
-    all_grads = lax.all_gather(grads.reshape(24, 256), ROW).reshape(384, 256)
-    near, all_grads = lax.optimization_barrier((near, all_grads))
+    near, own_grads = lax.optimization_barrier((near, grads.reshape(24, 256)))
+    all_grads = lax.all_gather(own_grads, ROW).reshape(384, 256)
     g_part = call(grad_body, ((512, 512), BF), all_grads, sketch, basis_out)
     both = swap(jnp.broadcast_to(near[None], (4, 8, 16, 1408)), "x")
     both, g_part = lax.optimization_barrier((both, g_part))
@@ -269,13 +235,21 @@
     reduced = sum_over(red, ROW)
     span = call(range_body, ((32, 4, 16, 128), BF), reduced, basis_in)
     span = sum_over(span, COL)
-    mapped = swap(call(mapped_body, ((16, 6, 16, 128), BF), span, basis_in), ROW)
-    mapped = lax.all_gather(call(gram_sum_body, ((6, 16, 128), BF), mapped), ROW)
-    core = sum_over(call(core_body, ((32, 2, 16, 128), BF), mapped, scaled), COL)
-    inverse = call(inverse_body, ((2, 72, 128), F32), mapped)
+    pieces, gram = call(
+        mapped_body, [((16, 4, 16, 128), BF), ((2, 72, 72), F32)], span, basis_in
+    )
+    mapped = sum_over(pieces, ROW)
+    core = call(core_body, ((32, 3, 8, 128), BF), mapped, scaled)
+    core, gram = lax.optimization_barrier((core, gram))
+    grams = lax.all_gather(gram, ROW)
+    core, grams = lax.optimization_barrier((summed(core, COL), grams))
+    core = swap(jnp.broadcast_to(core[None], (32, 3, 8, 128)), COL)
+    inverse = call(inverse_body, ((2, 72, 128), F32), grams)
     basis = call(basis_body, ((2, 72, 1792), F32), inverse, span)
-    proj = sum_over(call(project_body, ((16, 2, 16, 128), BF), core, basis_out), ROW)
-    return basis, call(final_body, ((2, 72, 256), F32), inverse, proj)
+    part = call(project_body, ((144, 256), BF), core, basis_out)
+    mine = call(query_body, ((8, 72, 256), BF), lax.all_gather(part, "core"))
+    mine = call(final_body, ((72, 256), F32), inverse, swap(mine, "y"))
+    return basis, lax.all_gather(mine, "core")
 
 
 def solution(mesh):

time: 310 us -> 304 us (0.981)
  blocking collectives: 215 us -> 206 us
    all_to_all x9 -> x8, blocking collectives: 159 us -> 141 us  [swap(): return lax.all_to_all(x, axes, 0, 0, tiled=True)]
    all_gather x2 -> x4, blocking collectives: 35.8 us -> 44.1 us  [the longest x1 20 us: on_device(): all_grads = lax.all_gather(own_grads, ROW).reshape(384, 256)]
    all_to_all x5 -> x6, starting transfers between devices: 35 us -> 37.4 us  [swap(): return lax.all_to_all(x, axes, 0, 0, tiled=True)]
    all_to_all x5 -> x6, waiting for transfers between devices: 25.5 us -> 26.7 us  [swap(): return lax.all_to_all(x, axes, 0, 0, tiled=True)]
  transfers between devices with their start and end apart: 6 -> 7, of which waited for: 4 -> 4; matrix products, arithmetic and copies ran while one was open for 0% -> 0% of each run, Pallas kernels for 4% -> 4%
where the time goes in v3:
time: 304 us; the launch traced here: 302 us
  blocking collectives  206 us (68%)
  starting transfers between devices  39.7 us (13%)
  waiting for transfers between devices  27.9 us (9%)
  Pallas kernels  20.3 us (7%)
  local copies, waits for them, and re-layouts  7.37 us (2%)
    all_to_all x8, blocking collectives, swap(): return lax.all_to_all(x, axes, 0, 0, tiled=True)  141 us
    all_to_all x6, starting transfers between devices, swap(): return lax.all_to_all(x, axes, 0, 0, tiled=True)  37.4 us
    all_to_all x6, waiting for transfers between devices, swap(): return lax.all_to_all(x, axes, 0, 0, tiled=True)  26.7 us
    all_gather x1, blocking collectives, on_device(): a_rot = lax.all_gather(a_own, ROW).reshape(384, 896)  20.8 us
    pallas_call x19, Pallas kernels, call(): pl.pallas_call(body, out_shape=shapes, in_specs=[pl.BlockSpec(memory_spac...  20.3 us
    all_gather x1, blocking collectives, on_device(): all_grads = lax.all_gather(own_grads, ROW).reshape(384, 256)  20 us
    all_gather x1, blocking collectives, on_device(): grams = lax.all_gather(gram, ROW)  17.9 us
  transfers between devices with their start and end apart: 7, of which 4 were waited for; matrix products, arithmetic and copies ran while one was open for 0% of the time, Pallas kernels for 4%

profile of v3, /device:TPU:1, one launch (start us, length us, event | category | flops | bytes accessed | tf_op | source)
XLA Modules:
  0.0 302.2 jit_solution(10548974272078997870)
XLA Ops:
  0.6 0.8 reshape.28.x_ref
  1.4 0.8 shard_map.77
  2.2 10.9 %all-to-all-start = ((bf16[8,16,1408]{2,1,0:T(8,128)(2,1)}), bf16[8,16,1408]{2,1,0:T(8,128)(2,1)S(1)}, u32[]{:S(2)}, u32[]{:S(2)}) async-start(bf16[8,16,1408]{2,1,0:T(8,128)(2,1)} %shard_map.77), calls=%async_computation | async-start | bytes 720896 | tf_op jit(solution)/shard_map/all_to_all | solution.py:32
  13.1 0.7 reshape.29
  13.8 12.2 %all-to-all-done = bf16[8,16,1408]{2,1,0:T(8,128)(2,1)S(1)} async-done(((bf16[8,16,1408]{2,1,0:T(8,128)(2,1)}), bf16[8,16,1408]{2,1,0:T(8,128)(2,1)S(1)}, u32[]{:S(2)}, u32[]{:S(2)}) %all-to-all-start) | async-done | bytes 360480 | tf_op jit(solution)/shard_map/all_to_all | solution.py:32
  26.0 0.0 copy-start.5
  26.0 0.0 copy-start.8
  26.0 1.2 broadcast_in_dim.6
  27.2 0.0 copy-start
  27.2 4.6 %all-to-all-start.1 = ((bf16[4,8,16,1408]{3,2,1,0:T(8,128)(2,1)}), bf16[4,8,16,1408]{3,2,1,0:T(8,128)(2,1)}, u32[]{:S(2)}, u32[]{:S(2)}) async-start(bf16[4,8,16,1408]{3,2,1,0:T(8,128)(2,1)} %broadcast_in_dim.6), calls=%async_computation.1 | async-start | bytes 2883584 | tf_op jit(solution)/shard_map/all_to_all | solution.py:32
  31.8 20.0 %all-gather.g_ref = bf16[384,256]{1,0:T(8,128)(2,1)S(1)} all-gather(bf16[24,256]{1,0:T(8,128)(2,1)S(1)} %reshape.29), channel_id=2, replica_groups=mesh['y'=8,'core'=2,'z'=8,'x'=4] {'y','core'}, dimensions={0}, use_global_device_ids=true | all-gather | bytes 208896 | tf_op jit(solution)/shard_map/all_gather | solution.py:219
  51.8 0.0 copy-done.5
  51.8 0.0 copy-done.8
  51.8 0.3 shard_map.78
  52.1 0.0 copy-start.4
  52.1 0.8 copy-done.4
  52.9 0.0 all-to-all-done.1.x_ref
  52.9 5.0 %all-to-all-start.2 = ((bf16[32,16,512]{2,1,0:T(8,128)(2,1)}), bf16[32,16,512]{2,1,0:T(8,128)(2,1)}, u32[]{:S(2)}, u32[]{:S(2)}) async-start(bf16[32,16,512]{2,1,0:T(8,128)(2,1)} %bitcast.7), calls=%async_computation.2 | async-start | bytes 1048576 | tf_op jit(solution)/shard_map/all_to_all | solution.py:32
  57.9 0.0 copy-done
  57.9 3.0 shard_map.79
  60.8 2.3 collective-permute-start
  63.2 1.3 collective-permute-done.b_ref
  64.5 0.1 shard_map.80
  64.5 10.0 %all-to-all-done.2.x_ref = bf16[32,16,512]{2,1,0:T(8,128)(2,1)} async-done(((bf16[32,16,512]{2,1,0:T(8,128)(2,1)}), bf16[32,16,512]{2,1,0:T(8,128)(2,1)}, u32[]{:S(2)}, u32[]{:S(2)}) %all-to-all-start.2) | async-done | bytes 524320 | tf_op jit(solution)/shard_map/all_to_all | solution.py:32
  74.6 1.1 shard_map.81
  75.7 13.2 %all_to_all.70.x_ref = bf16[8,24,896]{2,1,0:T(8,128)(2,1)S(1)} all-to-all(bf16[8,24,896]{2,1,0:T(8,128)(2,1)S(1)} %bitcast.8), channel_id=1, replica_groups=mesh['y'=8,'core'=2,'z'=8,'x'=4] {'y'}, dimensions={0} | all-to-all | bytes 688128 | tf_op jit(solution)/shard_map/all_to_all | solution.py:32
  89.0 0.9 broadcast_in_dim.7
  89.8 7.4 %all-to-all-start.4 = ((bf16[32,16,512]{2,1,0:T(8,128)(2,1)}), bf16[32,16,512]{2,1,0:T(8,128)(2,1)}, u32[]{:S(2)}, u32[]{:S(2)}) async-start(bf16[32,16,512]{2,1,0:T(8,128)(2,1)} %broadcast_in_dim.7), calls=%async_computation.4 | async-start | bytes 1048576 | tf_op jit(solution)/shard_map/all_to_all | solution.py:32
  97.2 20.8 %all-gather.1.a_ref = bf16[384,896]{1,0:T(8,128)(2,1)} all-gather(bf16[24,896]{1,0:T(8,128)(2,1)S(1)} %shard_map.82), channel_id=3, replica_groups=mesh['y'=8,'core'=2,'z'=8,'x'=4] {'y','core'}, dimensions={0}, use_global_device_ids=true | all-gather | bytes 731136 | tf_op jit(solution)/shard_map/all_gather | solution.py:231
  118.0 0.0 all-to-all-done.4
  118.0 0.0 copy-start.3
  118.0 1.1 copy-done.3
  119.1 0.0 copy-start.7
  119.1 1.2 copy-done.7
  120.3 2.6 shard_map.83
  122.9 15.4 %all_to_all.71.x_ref = bf16[16,4,16,128]{3,2,1,0:T(8,128)(2,1)S(1)} all-to-all(bf16[16,4,16,128]{3,2,1,0:T(8,128)(2,1)S(1)} %get-tuple-element.30), channel_id=1, replica_groups=mesh['y'=8,'core'=2,'z'=8,'x'=4] {'y','core'}, dimensions={0} | all-to-all | bytes 524288 | tf_op jit(solution)/shard_map/all_to_all | solution.py:32
  138.3 14.4 %all_to_all.72.r_ref = bf16[16,4,16,128]{3,2,1,0:T(8,128)(2,1)S(1)} all-to-all(bf16[16,4,16,128]{3,2,1,0:T(8,128)(2,1)S(1)} %shard_map.84), channel_id=1, replica_groups=mesh['y'=8,'core'=2,'z'=8,'x'=4] {'y','core'}, dimensions={0} | all-to-all | bytes 524288 | tf_op jit(solution)/shard_map/all_to_all | solution.py:32
  152.7 1.0 shard_map.85
  153.8 26.6 %all_to_all.73.x_ref = bf16[32,4,16,128]{3,2,1,0:T(8,128)(2,1)S(1)} all-to-all(bf16[32,4,16,128]{3,2,1,0:T(8,128)(2,1)S(1)} %shard_map.85), channel_id=1, replica_groups=mesh['y'=8,'core'=2,'z'=8,'x'=4] {'z','x'}, dimensions={0} | all-to-all | bytes 1048576 | tf_op jit(solution)/shard_map/all_to_all | solution.py:32
  180.4 0.1 shard_map.86
  180.5 20.0 %all_to_all.74.r_ref = bf16[32,4,16,128]{3,2,1,0:T(8,128)(2,1)S(1)} all-to-all(bf16[32,4,16,128]{3,2,1,0:T(8,128)(2,1)S(1)} %shard_map.86), channel_id=1, replica_groups=mesh['y'=8,'core'=2,'z'=8,'x'=4] {'z','x'}, dimensions={0} | all-to-all | bytes 1048576 | tf_op jit(solution)/shard_map/all_to_all | solution.py:32
  200.5 0.0 copy-start.1
  200.5 0.8 shard_map.87
  201.3 0.0 copy-done.1
  201.4 17.6 %all_to_all.75.x_ref = bf16[16,4,16,128]{3,2,1,0:T(8,128)(2,1)S(1)} all-to-all(bf16[16,4,16,128]{3,2,1,0:T(8,128)(2,1)S(1)} %get-tuple-element.31), channel_id=1, replica_groups=mesh['y'=8,'core'=2,'z'=8,'x'=4] {'y','core'}, dimensions={0} | all-to-all | bytes 524288 | tf_op jit(solution)/shard_map/all_to_all | solution.py:32
  219.0 14.3 %all_to_all.76.m_ref = bf16[16,4,16,128]{3,2,1,0:T(8,128)(2,1)S(1)} all-to-all(bf16[16,4,16,128]{3,2,1,0:T(8,128)(2,1)S(1)} %shard_map.88), channel_id=1, replica_groups=mesh['y'=8,'core'=2,'z'=8,'x'=4] {'y','core'}, dimensions={0} | all-to-all | bytes 524288 | tf_op jit(solution)/shard_map/all_to_all | solution.py:32
  233.3 1.1 shard_map.89
  234.4 0.0 copy-start.6
  234.4 4.4 %all-to-all-start.11 = ((bf16[32,3,8,128]{3,2,1,0:T(8,128)(2,1)}), bf16[32,3,8,128]{3,2,1,0:T(8,128)(2,1)S(1)}, u32[]{:S(2)}, u32[]{:S(2)}) async-start(bf16[32,3,8,128]{3,2,1,0:T(8,128)(2,1)} %shard_map.89), calls=%async_computation.11 | async-start | bytes 393216 | tf_op jit(solution)/shard_map/all_to_all | solution.py:32
  238.9 17.9 %all-gather.2 = f32[32,72,72]{2,1,0:T(8,128)S(1)} all-gather(f32[2,72,72]{2,1,0:T(8,128)S(1)} %get-tuple-element.35), channel_id=4, replica_groups=mesh['y'=8,'core'=2,'z'=8,'x'=4] {'y','core'}, dimensions={0}, use_global_device_ids=true | all-gather | bytes 705024 | tf_op jit(solution)/shard_map/all_gather | solution.py:244
  256.7 0.0 all-to-all-done.11.x_ref
  256.8 19.7 %all_to_all.77.c_ref = bf16[32,3,8,128]{3,2,1,0:T(8,128)(2,1)S(1)} all-to-all(bf16[32,3,8,128]{3,2,1,0:T(8,128)(2,1)S(1)} %broadcast_in_dim.8), channel_id=1, replica_groups=mesh['y'=8,'core'=2,'z'=8,'x'=4] {'z','x'}, dimensions={0} | all-to-all | bytes 393216 | tf_op jit(solution)/shard_map/all_to_all | solution.py:32
  276.5 0.0 copy-done.6
  276.5 0.2 shard_map.93
  276.8 3.6 %all-gather.3 = bf16[288,256]{1,0:T(8,128)(2,1)S(1)} all-gather(bf16[144,256]{1,0:T(8,128)(2,1)S(1)} %shard_map.93), channel_id=5, replica_groups=mesh['y'=8,'core'=2,'z'=8,'x'=4] {'core'}, dimensions={0}, use_global_device_ids=true | all-gather | bytes 221184 | tf_op jit(solution)/shard_map/all_gather | solution.py:250
  280.3 0.7 shard_map.94
  281.1 5.1 %all-to-all-start.13 = ((bf16[8,72,256]{2,1,0:T(8,128)(2,1)}), bf16[8,72,256]{2,1,0:T(8,128)(2,1)S(1)}, u32[]{:S(2)}, u32[]{:S(2)}) async-start(bf16[8,72,256]{2,1,0:T(8,128)(2,1)} %shard_map.94), calls=%async_computation.13 | async-start | bytes 589824 | tf_op jit(solution)/shard_map/all_to_all | solution.py:32
  286.2 6.1 %shard_map.91.w_ref = f32[2,72,128]{2,1,0:T(8,128)S(1)} custom-call(f32[16,2,72,72]{3,2,1,0:T(8,128)S(1)} %bitcast.6), custom_call_target="tpu_custom_call" | custom-call | tf_op jit(solution)/shard_map/pallas_call | solution.py:21
  292.3 0.0 copy-done.2
  292.3 1.9 shard_map.92
  294.2 4.4 %all-to-all-done.13.p_ref = bf16[8,72,256]{2,1,0:T(8,128)(2,1)S(1)} async-done(((bf16[8,72,256]{2,1,0:T(8,128)(2,1)}), bf16[8,72,256]{2,1,0:T(8,128)(2,1)S(1)}, u32[]{:S(2)}, u32[]{:S(2)}) %all-to-all-start.13) | async-done | bytes 294944 | tf_op jit(solution)/shard_map/all_to_all | solution.py:32
  298.7 0.2 shard_map.95
  298.9 2.6 all-gather.4
  301.6 0.7 copy.9
  (6 shorter events, 0.2 us)
Async XLA Ops:
  2.2 23.8 %all-to-all-start = ((bf16[8,16,1408]{2,1,0:T(8,128)(2,1)}), bf16[8,16,1408]{2,1,0:T(8,128)(2,1)S(1)}, u32[]{:S(2)}, u32[]{:S(2)}) async-start(bf16[8,16,1408]{2,1,0:T(8,128)(2,1)} %shard_map.77), calls=%async_computation | async-start | bytes 720896 | tf_op jit(solution)/shard_map/all_to_all | solution.py:32
  26.0 25.8 %copy-start.5 = (bf16[256,512]{1,0:T(8,128)(2,1)S(1)}, bf16[256,512]{1,0:T(8,128)(2,1)}, u32[]{:S(2)}) copy-start(bf16[256,512]{1,0:T(8,128)(2,1)} %w_ref.9) | copy-start | bytes 786436
  26.0 25.8 %copy-start.8 = (bf16[72,256]{1,0:T(8,128)(2,1)S(1)}, bf16[72,256]{1,0:T(8,128)(2,1)}, u32[]{:S(2)}) copy-start(bf16[72,256]{1,0:T(8,128)(2,1)} %s_ref.1) | copy-start | bytes 110596
  27.2 30.7 %copy-start = (bf16[1792,896]{1,0:T(8,128)(2,1)S(1)}, bf16[1792,896]{1,0:T(8,128)(2,1)}, u32[]{:S(2)}) copy-start(bf16[1792,896]{1,0:T(8,128)(2,1)} %w_ref.8) | copy-start | bytes 9633796
  27.2 25.7 %all-to-all-start.1 = ((bf16[4,8,16,1408]{3,2,1,0:T(8,128)(2,1)}), bf16[4,8,16,1408]{3,2,1,0:T(8,128)(2,1)}, u32[]{:S(2)}, u32[]{:S(2)}) async-start(bf16[4,8,16,1408]{3,2,1,0:T(8,128)(2,1)} %broadcast_in_dim.6), calls=%async_computation.1 | async-start | bytes 2883584 | tf_op jit(solution)/shard_map/all_to_all | solution.py:32
  52.1 0.8 copy-start.4
  52.9 21.7 %all-to-all-start.2 = ((bf16[32,16,512]{2,1,0:T(8,128)(2,1)}), bf16[32,16,512]{2,1,0:T(8,128)(2,1)}, u32[]{:S(2)}, u32[]{:S(2)}) async-start(bf16[32,16,512]{2,1,0:T(8,128)(2,1)} %bitcast.7), calls=%async_computation.2 | async-start | bytes 1048576 | tf_op jit(solution)/shard_map/all_to_all | solution.py:32
  60.8 3.6 %collective-permute-start = (bf16[192,896]{1,0:T(8,128)(2,1)S(1)}, bf16[192,896]{1,0:T(8,128)(2,1)S(1)}, u32[]{:S(2)}, u32[]{:S(2)}) collective-permute-start(bf16[192,896]{1,0:T(8,128)(2,1)S(1)} %get-tuple-element.24), channel_id=1, source_target_pairs={{0,32},{32,0},{1,33},{33,1},{2,34},{34,2},{3,35},{35,3},{4,36},{36... | collective-permute-start | bytes 1032200 | tf_op jit(solution)/shard_map/ppermute | solution.py:225
  89.8 28.1 %all-to-all-start.4 = ((bf16[32,16,512]{2,1,0:T(8,128)(2,1)}), bf16[32,16,512]{2,1,0:T(8,128)(2,1)}, u32[]{:S(2)}, u32[]{:S(2)}) async-start(bf16[32,16,512]{2,1,0:T(8,128)(2,1)} %broadcast_in_dim.7), calls=%async_computation.4 | async-start | bytes 1048576 | tf_op jit(solution)/shard_map/all_to_all | solution.py:32
  118.0 1.1 copy-start.3
  119.1 1.2 copy-start.7
  200.5 0.9 copy-start.1
  234.4 42.1 %copy-start.6 = (bf16[256,512]{1,0:T(8,128)(2,1)S(1)}, bf16[256,512]{1,0:T(8,128)(2,1)}, u32[]{:S(2)}) copy-start(bf16[256,512]{1,0:T(8,128)(2,1)} %w_ref.9) | copy-start | bytes 786436
  234.4 22.3 %all-to-all-start.11 = ((bf16[32,3,8,128]{3,2,1,0:T(8,128)(2,1)}), bf16[32,3,8,128]{3,2,1,0:T(8,128)(2,1)S(1)}, u32[]{:S(2)}, u32[]{:S(2)}) async-start(bf16[32,3,8,128]{3,2,1,0:T(8,128)(2,1)} %shard_map.89), calls=%async_computation.11 | async-start | bytes 393216 | tf_op jit(solution)/shard_map/all_to_all | solution.py:32
  276.5 15.8 %copy-start.2 = (bf16[32,4,16,128]{3,2,1,0:T(8,128)(2,1)S(1)}, bf16[32,4,16,128]{3,2,1,0:T(8,128)(2,1)}, u32[]{:S(2)}) copy-start(bf16[32,4,16,128]{3,2,1,0:T(8,128)(2,1)} %copy-done.1) | copy-start | bytes 1572868
  281.1 17.6 %all-to-all-start.13 = ((bf16[8,72,256]{2,1,0:T(8,128)(2,1)}), bf16[8,72,256]{2,1,0:T(8,128)(2,1)S(1)}, u32[]{:S(2)}, u32[]{:S(2)}) async-start(bf16[8,72,256]{2,1,0:T(8,128)(2,1)} %shard_map.94), calls=%async_computation.13 | async-start | bytes 589824 | tf_op jit(solution)/shard_map/all_to_all | solution.py:32

commit v4 on v3

v4 whole, which is shorter than its diff:
```python
import jax
import jax.numpy as jnp
import numpy as np
from jax import lax
from jax.experimental import pallas as pl
from jax.experimental.pallas import tpu as pltpu
from jax.sharding import Mesh
from jax.sharding import PartitionSpec as P

COL = ("z", "x")
ROW = ("y", "core")
BF = jnp.bfloat16
F32 = jnp.float32
MIB = 1024 * 1024


def call(body, out, *args, limit=40):
    many = isinstance(out, list)
    shapes = [jax.ShapeDtypeStruct(s, d) for s, d in (out if many else [out])]
    got = pl.pallas_call(
        body,
        out_shape=shapes,
        in_specs=[pl.BlockSpec(memory_space=pltpu.VMEM)] * len(args),
        out_specs=[pl.BlockSpec(memory_space=pltpu.VMEM)] * len(shapes),
        compiler_params=pltpu.CompilerParams(vmem_limit_bytes=limit * MIB),
    )(*args)
    return got if many else got[0]


def swap(x, axes):
    return lax.all_to_all(x, axes, 0, 0, tiled=True)


def from_sibling(x):
    return lax.ppermute(x, "core", [(0, 1), (1, 0)])


def dot(a, b, ca=1, cb=0, **kw):
    return lax.dot_general(a, b, (((ca,), (cb,)), ((), ())), preferred_element_type=F32, **kw)


def to_tiles(y, out_ref, slots=None):
    slots = slots or out_ref.shape[1]
    lanes = y.shape[1] // 128
    count = (y.shape[0] // 8) * lanes
    for t in range(out_ref.shape[0] * slots):
        if t < count:
            r, g = divmod(t, lanes)
            tile = y[r * 8 : r * 8 + 8, g * 128 : g * 128 + 128]
        else:
            tile = jnp.zeros((8, 128), F32)
        out_ref[t // slots, t % slots] = tile.astype(BF)


def from_tiles(ref, lanes, rows=72, slots=None):
    slots = slots or ref.shape[1]
    lines = []
    for r in range(rows // 8):
        at = [divmod(r * lanes + g, slots) for g in range(lanes)]
        lines.append(jnp.concatenate([ref[p, s].astype(F32) for p, s in at], axis=1))
    return jnp.concatenate(lines, axis=0)


def sum_one_body(x_ref, out_ref):
    out_ref[...] = jnp.sum(x_ref[...].astype(F32), axis=0).astype(BF)


def summed(pieces, axes):
    own = swap(pieces, axes)
    return call(sum_one_body, (own.shape[1:], BF), own)


def sum_body(x_ref, out_ref):
    total = jnp.sum(x_ref[...].astype(F32), axis=0).astype(BF)
    out_ref[...] = jnp.broadcast_to(total[None], out_ref.shape)


def sum_over(pieces, axes):
    own = swap(pieces, axes)
    return swap(call(sum_body, (own.shape, BF), own), axes)


def picked(rows, x):
    lanes = lax.broadcasted_iota(jnp.int32, (rows.shape[0], x.shape[0]), 1)
    return dot(jnp.where(lanes == rows, 1.0, 0.0).astype(BF), x).astype(BF)


def pack_body(x_ref, out_ref):
    core = lax.axis_index("core")
    t = lax.broadcasted_iota(jnp.int32, (8, 1), 0)
    x = x_ref[...]
    parts = []
    for other in range(2):
        at = jnp.where(core == other, 0, 16) + 2 * t + core
        parts.append(picked(jnp.where(t < 6, at, -1), x))
    packed = jnp.concatenate(parts, axis=1)
    out_ref[...] = jnp.broadcast_to(packed[None], out_ref.shape)


def dense_body(rows_ref, x_ref, out_ref):
    y = picked(rows_ref[...], x_ref[...])
    out_ref[...] = jnp.broadcast_to(y[None], out_ref.shape)


def act_body(x_ref, w_ref, v_ref, out_ref):
    n = w_ref.shape[0]
    y = dot(x_ref[:, :n], w_ref[...]) + dot(x_ref[:, n:], v_ref[...])
    out_ref[...] = y.astype(BF)


def grad_body(rows_ref, g_ref, s_ref, w_ref, v_ref, out_ref):
    g = picked(rows_ref[...] + lax.axis_index("core"), g_ref[...])
    s = s_ref[...]
    w, v = w_ref[...], v_ref[...]
    top = jnp.concatenate([dot(g, w), dot(g, v)], axis=1)
    low = jnp.concatenate([dot(s, w), dot(s, v)], axis=1)
    to_tiles(jnp.concatenate([top, low], axis=0), out_ref)


def scaled_body(a_ref, g_ref, e_ref, f_ref, scaled_ref, out_ref):
    core = lax.axis_index("core")
    a = jnp.concatenate([a_ref[y, core].astype(F32) for y in range(8)], axis=0).astype(BF)
    g = from_tiles(g_ref, 8, 264)
    both = dot(a.T, g[:192].astype(BF))
    n = e_ref.shape[1]
    left = (both[:, :n] / e_ref[...].astype(F32)).astype(BF)
    right = (both[:, n:] / f_ref[...].astype(F32)).astype(BF)
    s = jnp.concatenate([left, right], axis=1)
    scaled_ref[...] = s
    to_tiles(dot(g[192:].astype(BF), s, 1, 1), out_ref)


def range_body(r_ref, w_ref, v_ref, out_ref):
    r = from_tiles(r_ref, 7).astype(BF)
    both = [dot(r, w_ref[...], 1, 1), dot(r, v_ref[...], 1, 1)]
    to_tiles(jnp.concatenate(both, axis=1), out_ref)


def split3(x):
    hi = x.astype(BF)
    left = x - hi.astype(F32)
    mid = left.astype(BF)
    return hi, mid, (left - mid.astype(F32)).astype(BF)


def gram_at(g):
    return (g, 9) if g < 8 else (7, 6)


def mapped_body(r_ref, w_ref, v_ref, out_ref, keep_ref, give_ref):
    r = from_tiles(r_ref, 28).astype(BF)
    n = w_ref.shape[0]
    keep_ref[...] = r[:, :n]
    give_ref[...] = r[:, n:]
    to_tiles(dot(r[:, :n], w_ref[...]) + dot(r[:, n:], v_ref[...]), out_ref, 9)
    gram = jnp.concatenate([dot(r, r, 1, 1), jnp.zeros((72, 56), F32)], axis=1)
    for g in range(9):
        p, s = gram_at(g)
        for i, part in enumerate(split3(gram[g * 8 : g * 8 + 8])):
            out_ref[p, s + i] = part


def gram_sum_body(x_ref, out_ref):
    total = jnp.sum(x_ref[...].astype(F32), axis=0)
    last = lax.axis_index("y") == 7
    parts = split3(total[9] + total[10] + total[11])
    spare = split3(total[6] + total[7] + total[8])
    for i in range(12):
        tile = total[i].astype(BF)
        if i >= 9:
            tile = parts[i - 9]
        elif i >= 6:
            tile = jnp.where(last, spare[i - 6].astype(F32), total[i]).astype(BF)
        out_ref[:, i] = jnp.broadcast_to(tile[None], (out_ref.shape[0], 8, 128))


def core_body(m_ref, s_ref, out_ref):
    m = from_tiles(m_ref, 7, slots=9).astype(BF)
    to_tiles(dot(m, s_ref[...]), out_ref)


def inverse_body(m_ref, out_ref):
    tiles = []
    for g in range(9):
        p, s = gram_at(g)
        tiles.append(sum(m_ref[p, s + i].astype(F32) for i in range(3)))
    left = jnp.concatenate(tiles, axis=0)
    rows = lax.broadcasted_iota(jnp.int32, (72, 128), 0)
    lanes = lax.broadcasted_iota(jnp.int32, (72, 128), 1)
    below = lax.broadcasted_iota(jnp.int32, (72, 1), 0)
    right = jnp.where(rows == lanes, 1.0, 0.0)
    for k in range(72):
        pivot = left[k : k + 1]
        f = left[:, k : k + 1] / pivot[:, k : k + 1]
        f = jnp.where(below > k, f, 0.0)
        line = right[k : k + 1]
        left = left - f * pivot
        right = right - f * line
    d = jnp.sum(jnp.where(rows == lanes, left, 0.0), axis=1, keepdims=True)
    out_ref[...] = right / jnp.sqrt(d)


def basis_body(w_ref, keep_ref, got_ref, out_ref):
    core = lax.axis_index("core")
    for q, ref in ((core, keep_ref), (1 - core, got_ref)):
        w = w_ref[q][:, :72]
        out_ref[q] = dot(w, ref[...].astype(F32), precision=lax.Precision.HIGHEST)


def project_body(c_ref, w_ref, v_ref, out_ref):
    c = from_tiles(c_ref, 8).astype(BF)
    n = w_ref.shape[1]
    y = dot(c[:, :n], w_ref[...], 1, 1) + dot(c[:, n:], v_ref[...], 1, 1)
    out_ref[...] = jnp.broadcast_to(y.astype(BF)[None], out_ref.shape)


def final_body(w_ref, p_ref, out_ref):
    p = jnp.sum(p_ref[...].astype(F32), axis=0)
    out_ref[...] = dot(w_ref[...][:, :72], p, precision=lax.Precision.HIGHEST)


DENSE = np.array([[8 * z + t] for z in range(8) for t in range(6)], np.int32)
TOKENS = np.array(
    [[2 * ((z * 4 + x) * 6 + t)] for x in range(4) for z in range(8) for t in range(6)], np.int32
)


def on_device(acts, grads, basis_in, basis_out, eigen, sketch):
    lines = jnp.pad(acts.reshape(12, 1792), ((0, 4), (0, 0)))
    lines = lax.all_gather(lines, "core").reshape(32, 1792)
    packed = call(pack_body, ((8, 8, 3584), BF), lines)
    packed, away = lax.optimization_barrier((packed, (basis_in, basis_out, eigen)))
    far_in, far_out, far_eigen = [from_sibling(w) for w in away]
    near = swap(packed, "z").reshape(64, 3584)
    near, own_grads = lax.optimization_barrier((near, grads.reshape(24, 256)))
    dense = call(dense_body, ((4, 48, 3584), BF), jnp.asarray(DENSE), near)
    all_grads = lax.all_gather(own_grads, ROW).reshape(384, 256)
    g_part = call(
        grad_body, ((32, 9, 8, 128), BF),
        jnp.asarray(TOKENS), all_grads, sketch, basis_out, far_out,
    )
    both = swap(dense, "x").reshape(192, 3584)
    both, g_part = lax.optimization_barrier((both, g_part))
    g_own = summed(g_part, COL)
    a_part = call(act_body, ((192, 896), BF), both, basis_in, far_in)
    a_part, g_own = lax.optimization_barrier((a_part, g_own))
    a_own = summed(a_part.reshape(8, 24, 896), "y")
    a_own, g_own = lax.optimization_barrier((a_own, g_own))
    g_rot = swap(jnp.broadcast_to(g_own[None], (32, 9, 8, 128)), COL)
    a_rot = lax.all_gather(a_own, ROW).reshape(8, 2, 24, 896)
    scaled, red = call(
        scaled_body, [((896, 1024), BF), ((8, 8, 8, 128), BF)], a_rot, g_rot, eigen, far_eigen
    )
    reduced = sum_over(red, "y")
    span = sum_over(call(range_body, ((32, 8, 8, 128), BF), reduced, basis_in, far_in), COL)
    mapped, keep, give = call(
        mapped_body,
        [((8, 12, 8, 128), BF), ((72, 1792), BF), ((72, 1792), BF)],
        span, basis_in, far_in,
    )
    mapped = swap(call(gram_sum_body, ((8, 12, 8, 128), BF), swap(mapped, "y")), "y")
    core = sum_over(call(core_body, ((32, 3, 8, 128), BF), mapped, scaled), COL)
    part = call(project_body, ((8, 72, 256), BF), core, basis_out, far_out)
    inverse = call(inverse_body, ((72, 128), F32), mapped)
    basis = call(
        basis_body, ((2, 72, 1792), F32),
        lax.all_gather(inverse, "core"), keep, from_sibling(give),
    )
    mine = call(final_body, ((72, 256), F32), inverse, swap(part, "y"))
    return basis, lax.all_gather(mine, "core")


def solution(mesh):
    split = Mesh(mesh.devices.reshape(8, 2, 8, 4), ("y", "core", "z", "x"))
    return jax.shard_map(
        on_device,
        mesh=split,
        in_specs=(
            P(COL, None, ROW),
            P(ROW, None, COL),
            P(ROW, COL),
            P(COL, ROW),
            P(COL, ROW),
            P(None, COL),
        ),
        out_specs=(P(None, None, ROW), P(None, None, COL)),
        check_vma=False,
    )
```

time: 304 us -> 296 us (0.974)
  waiting for transfers between devices: 27.9 us -> 16.6 us
  blocking collectives: 206 us -> 200 us
  Pallas kernels: 20.3 us -> 26.2 us
  local copies, waits for them, and re-layouts: 7.37 us -> 10.6 us
    ppermute x1 -> x4, starting transfers between devices: 2.35 us -> 21.2 us  [from_sibling(): return lax.ppermute(x, 'core', [(0, 1), (1, 0)])]
    all_to_all x6 -> x4, starting transfers between devices: 37.4 us -> 18.9 us  [swap(): return lax.all_to_all(x, axes, 0, 0, tiled=True)]
    all_gather x3, blocking collectives: 42.2 us -> 28.1 us  [the longest x1 17.8 us: on_device(): a_rot = lax.all_gather(a_own, ROW).reshape(8, 2, 24, 896)]
    all_to_all x8 -> x10, blocking collectives: 141 us -> 152 us  [swap(): return lax.all_to_all(x, axes, 0, 0, tiled=True)]
    all_to_all x6 -> x4, waiting for transfers between devices: 26.7 us -> 16.5 us  [swap(): return lax.all_to_all(x, axes, 0, 0, tiled=True)]
    pallas_call x19 -> x18, Pallas kernels: 20.3 us -> 26.2 us  [call(): pl.pallas_call(body, out_shape=shapes, in_specs=[pl.BlockSpec(memory_spac...]
    unnamed x19 -> x35, local copies, waits for them, and re-layouts: 3.75 us -> 8.88 us
  transfers between devices with their start and end apart: 7 -> 8, of which waited for: 4 -> 1; matrix products, arithmetic and copies ran while one was open for 0% -> 0% of each run, Pallas kernels for 4% -> 3%
where the time goes in v4:
time: 296 us; the launch traced here: 294 us
  blocking collectives  200 us (68%)
  starting transfers between devices  40 us (14%)
  Pallas kernels  26.2 us (9%)
  waiting for transfers between devices  16.6 us (6%)
  local copies, waits for them, and re-layouts  10.6 us (4%)
    all_to_all x10, blocking collectives, swap(): return lax.all_to_all(x, axes, 0, 0, tiled=True)  152 us
    pallas_call x18, Pallas kernels, call(): pl.pallas_call(body, out_shape=shapes, in_specs=[pl.BlockSpec(memory_spac...  26.2 us
    ppermute x4, starting transfers between devices, from_sibling(): return lax.ppermute(x, 'core', [(0, 1), (1, 0)])  21.2 us
    all_to_all x4, starting transfers between devices, swap(): return lax.all_to_all(x, axes, 0, 0, tiled=True)  18.9 us
    all_gather x1, blocking collectives, on_device(): all_grads = lax.all_gather(own_grads, ROW).reshape(384, 256)  18 us
    all_gather x1, blocking collectives, on_device(): a_rot = lax.all_gather(a_own, ROW).reshape(8, 2, 24, 896)  17.8 us
    all_to_all x4, waiting for transfers between devices, swap(): return lax.all_to_all(x, axes, 0, 0, tiled=True)  16.5 us
    unnamed x35, local copies, waits for them, and re-layouts  8.88 us
  transfers between devices with their start and end apart: 8, of which 1 were waited for; matrix products, arithmetic and copies ran while one was open for 0% of the time, Pallas kernels for 3%

profile of v4, /device:TPU:1, one launch (start us, length us, event | category | flops | bytes accessed | tf_op | source)
XLA Modules:
  0.0 294.5 jit_solution(9166184346396265946)
XLA Ops:
  0.6 0.0 copy-start.13
  0.7 0.8 reshape.29
  1.5 8.4 %all-gather.x_ref = bf16[32,1792]{1,0:T(8,128)(2,1)S(1)} all-gather(bf16[16,1792]{1,0:T(8,128)(2,1)S(1)} %pad.4), channel_id=2, replica_groups=mesh['y'=8,'core'=2,'z'=8,'x'=4] {'core'}, dimensions={0}, use_global_device_ids=true | all-gather | bytes 172032 | tf_op jit(solution)/shard_map/all_gather | solution.py:230
  9.9 0.9 shard_map.95
  10.8 2.3 collective-permute-start.1
  13.1 4.7 %all-to-all-start = ((bf16[8,8,3584]{2,1,0:T(8,128)(2,1)}), bf16[8,8,3584]{2,1,0:T(8,128)(2,1)S(1)}, u32[]{:S(2)}, u32[]{:S(2)}) async-start(bf16[8,8,3584]{2,1,0:T(8,128)(2,1)} %shard_map.95), calls=%async_computation | async-start | bytes 917504 | tf_op jit(solution)/shard_map/all_to_all | solution.py:31
  17.8 0.0 copy-done.16
  17.8 16.5 %all-to-all-done = bf16[8,8,3584]{2,1,0:T(8,128)(2,1)S(1)} async-done(((bf16[8,8,3584]{2,1,0:T(8,128)(2,1)}), bf16[8,8,3584]{2,1,0:T(8,128)(2,1)S(1)}, u32[]{:S(2)}, u32[]{:S(2)}) %all-to-all-start) | async-done | bytes 458784 | tf_op jit(solution)/shard_map/all_to_all | solution.py:31
  34.3 0.0 copy-done.13
  34.3 1.4 shard_map.96
  35.8 4.4 %all-to-all-start.1 = ((bf16[4,48,3584]{2,1,0:T(8,128)(2,1)}), bf16[4,48,3584]{2,1,0:T(8,128)(2,1)}, u32[]{:S(2)}, u32[]{:S(2)}) async-start(bf16[4,48,3584]{2,1,0:T(8,128)(2,1)} %shard_map.96), calls=%async_computation.1 | async-start | bytes 2752512 | tf_op jit(solution)/shard_map/all_to_all | solution.py:31
  40.2 0.0 copy-start
  40.2 2.7 collective-permute-start
  42.9 18.0 %all-gather.1.g_ref = bf16[384,256]{1,0:T(8,128)(2,1)S(1)} all-gather(bf16[24,256]{1,0:T(8,128)(2,1)S(1)} %reshape.32), channel_id=3, replica_groups=mesh['y'=8,'core'=2,'z'=8,'x'=4] {'y','core'}, dimensions={0}, use_global_device_ids=true | all-gather | bytes 208896 | tf_op jit(solution)/shard_map/all_gather | solution.py:237
  60.9 0.0 collective-permute-done.v_ref
  60.9 0.9 copy-done.11
  61.8 0.6 shard_map.97
  62.4 0.0 copy-start.2
  62.4 0.8 copy-done.2
  63.2 0.7 copy-done.4
  63.9 0.0 all-to-all-done.1
  63.9 22.7 %all_to_all.70.x_ref = bf16[32,9,8,128]{3,2,1,0:T(8,128)(2,1)S(1)} all-to-all(bf16[32,9,8,128]{3,2,1,0:T(8,128)(2,1)} %copy-done.2), channel_id=1, replica_groups=mesh['y'=8,'core'=2,'z'=8,'x'=4] {'z','x'}, dimensions={0} | all-to-all | bytes 1179648 | tf_op jit(solution)/shard_map/all_to_all | solution.py:31
  86.6 0.1 shard_map.99
  86.7 0.0 collective-permute-done.1.v_ref
  86.7 3.9 %shard_map.98 = bf16[192,896]{1,0:T(8,128)(2,1)S(1)} custom-call(bf16[192,3584]{1,0:T(8,128)(2,1)} %bitcast.1.x_ref, bf16[1792,896]{1,0:T(8,128)(2,1)S(1)} %copy-done, bf16[1792,896]{1,0:T(8,128)(2,1)} %collective-permute-done.1.v_ref), custom_call_target="tpu_custom_call" | custom-call | tf_op jit(solution)/shard_map/pallas_call | solution.py:20
  90.7 14.4 %all_to_all.71.x_ref = bf16[8,24,896]{2,1,0:T(8,128)(2,1)S(1)} all-to-all(bf16[8,24,896]{2,1,0:T(8,128)(2,1)S(1)} %bitcast.8), channel_id=1, replica_groups=mesh['y'=8,'core'=2,'z'=8,'x'=4] {'y'}, dimensions={0} | all-to-all | bytes 688128 | tf_op jit(solution)/shard_map/all_to_all | solution.py:31
  105.2 0.9 broadcast_in_dim.2
  106.1 6.3 %all-to-all-start.4 = ((bf16[32,9,8,128]{3,2,1,0:T(8,128)(2,1)}), bf16[32,9,8,128]{3,2,1,0:T(8,128)(2,1)}, u32[]{:S(2)}, u32[]{:S(2)}) async-start(bf16[32,9,8,128]{3,2,1,0:T(8,128)(2,1)} %broadcast_in_dim.2), calls=%async_computation.4 | async-start | bytes 1179648 | tf_op jit(solution)/shard_map/all_to_all | solution.py:31
  112.4 5.2 %collective-permute-start.2 = (bf16[896,512]{1,0:T(8,128)(2,1)}, bf16[896,512]{1,0:T(8,128)(2,1)S(1)}, u32[]{:S(2)}, u32[]{:S(2)}) collective-permute-start(bf16[896,512]{1,0:T(8,128)(2,1)} %e_ref.1), channel_id=1, source_target_pairs={{0,32},{32,0},{1,33},{33,1},{2,34},{34,2},{3,35},{35,3},{4,36},{36... | collective-permute-start | bytes 2752520 | tf_op jit(solution)/shard_map/ppermute | solution.py:35
  117.6 17.8 %all-gather.2 = bf16[384,896]{1,0:T(8,128)(2,1)} all-gather(bf16[24,896]{1,0:T(8,128)(2,1)S(1)} %shard_map.100), channel_id=4, replica_groups=mesh['y'=8,'core'=2,'z'=8,'x'=4] {'y','core'}, dimensions={0}, use_global_device_ids=true | all-gather | bytes 731136 | tf_op jit(solution)/shard_map/all_gather | solution.py:250
  135.4 0.0 collective-permute-done.2.f_ref
  135.4 0.9 copy-done.7
  136.3 0.0 all-to-all-done.4.g_ref
  136.3 1.1 copy-done.1
  137.4 1.2 copy-done.6
  138.6 1.2 copy-done.8
  139.8 2.2 shard_map.101
  142.0 11.7 %all_to_all.72.x_ref = bf16[8,8,8,128]{3,2,1,0:T(8,128)(2,1)S(1)} all-to-all(bf16[8,8,8,128]{3,2,1,0:T(8,128)(2,1)S(1)} %get-tuple-element.31), channel_id=1, replica_groups=mesh['y'=8,'core'=2,'z'=8,'x'=4] {'y'}, dimensions={0} | all-to-all | bytes 262144 | tf_op jit(solution)/shard_map/all_to_all | solution.py:31
  153.7 10.3 %all_to_all.73.r_ref = bf16[8,8,8,128]{3,2,1,0:T(8,128)(2,1)S(1)} all-to-all(bf16[8,8,8,128]{3,2,1,0:T(8,128)(2,1)S(1)} %shard_map.102), channel_id=1, replica_groups=mesh['y'=8,'core'=2,'z'=8,'x'=4] {'y'}, dimensions={0} | all-to-all | bytes 262144 | tf_op jit(solution)/shard_map/all_to_all | solution.py:31
  164.1 4.0 %shard_map.103 = bf16[32,8,8,128]{3,2,1,0:T(8,128)(2,1)S(1)} custom-call(bf16[8,8,8,128]{3,2,1,0:T(8,128)(2,1)S(1)} %all_to_all.73.r_ref, bf16[1792,896]{1,0:T(8,128)(2,1)S(1)} %copy-done, bf16[1792,896]{1,0:T(8,128)(2,1)} %collective-permute-done.1.v_ref), custom_call_target="tpu_custom_call" | custom-call | tf_op jit(solution)/shard_map/pallas_call | solution.py:20
  168.0 22.7 %all_to_all.74.x_ref = bf16[32,8,8,128]{3,2,1,0:T(8,128)(2,1)S(1)} all-to-all(bf16[32,8,8,128]{3,2,1,0:T(8,128)(2,1)S(1)} %shard_map.103), channel_id=1, replica_groups=mesh['y'=8,'core'=2,'z'=8,'x'=4] {'z','x'}, dimensions={0} | all-to-all | bytes 1048576 | tf_op jit(solution)/shard_map/all_to_all | solution.py:31
  190.7 0.1 shard_map.104
  190.8 18.9 %all_to_all.75.r_ref = bf16[32,8,8,128]{3,2,1,0:T(8,128)(2,1)S(1)} all-to-all(bf16[32,8,8,128]{3,2,1,0:T(8,128)(2,1)S(1)} %shard_map.104), channel_id=1, replica_groups=mesh['y'=8,'core'=2,'z'=8,'x'=4] {'z','x'}, dimensions={0} | all-to-all | bytes 1048576 | tf_op jit(solution)/shard_map/all_to_all | solution.py:31
  209.8 3.2 %shard_map.105 = (bf16[8,12,8,128]{3,2,1,0:T(8,128)(2,1)S(1)}, bf16[72,1792]{1,0:T(8,128)(2,1)S(1)}, bf16[72,1792]{1,0:T(8,128)(2,1)S(1)}) custom-call(bf16[32,8,8,128]{3,2,1,0:T(8,128)(2,1)S(1)} %all_to_all.75.r_ref, bf16[1792,896]{1,0:T(8,128)(2,1)S(1)} %copy-done, bf16[1792,896]{1,0:T(8,128)(2,1)} %collective-permute-done.1.v_ref), custom_call_target="tpu_custom_call" | custom-call | tf_op jit(solution)/shard_map/pallas_call | solution.py:20
  213.0 0.0 copy-start.9
  213.0 0.7 copy-done.9
  213.7 0.7 copy-done.14
  214.4 11.3 %all_to_all.76.x_ref = bf16[8,12,8,128]{3,2,1,0:T(8,128)(2,1)S(1)} all-to-all(bf16[8,12,8,128]{3,2,1,0:T(8,128)(2,1)S(1)} %get-tuple-element.32), channel_id=1, replica_groups=mesh['y'=8,'core'=2,'z'=8,'x'=4] {'y'}, dimensions={0} | all-to-all | bytes 393216 | tf_op jit(solution)/shard_map/all_to_all | solution.py:31
  225.8 11.2 %all_to_all.77.m_ref = bf16[8,12,8,128]{3,2,1,0:T(8,128)(2,1)S(1)} all-to-all(bf16[8,12,8,128]{3,2,1,0:T(8,128)(2,1)S(1)} %shard_map.106), channel_id=1, replica_groups=mesh['y'=8,'core'=2,'z'=8,'x'=4] {'y'}, dimensions={0} | all-to-all | bytes 393216 | tf_op jit(solution)/shard_map/all_to_all | solution.py:31
  236.9 0.5 shard_map.109
  237.4 0.0 copy-start.10
  237.4 15.9 %all_to_all.78.x_ref = bf16[32,3,8,128]{3,2,1,0:T(8,128)(2,1)S(1)} all-to-all(bf16[32,3,8,128]{3,2,1,0:T(8,128)(2,1)S(1)} %shard_map.109), channel_id=1, replica_groups=mesh['y'=8,'core'=2,'z'=8,'x'=4] {'z','x'}, dimensions={0} | all-to-all | bytes 393216 | tf_op jit(solution)/shard_map/all_to_all | solution.py:31
  253.3 13.1 %all_to_all.79.c_ref = bf16[32,3,8,128]{3,2,1,0:T(8,128)(2,1)S(1)} all-to-all(bf16[32,3,8,128]{3,2,1,0:T(8,128)(2,1)S(1)} %shard_map.110), channel_id=1, replica_groups=mesh['y'=8,'core'=2,'z'=8,'x'=4] {'z','x'}, dimensions={0} | all-to-all | bytes 393216 | tf_op jit(solution)/shard_map/all_to_all | solution.py:31
  266.4 1.0 shard_map.111
  267.4 3.4 %all-to-all-start.13 = ((bf16[8,72,256]{2,1,0:T(8,128)(2,1)}), bf16[8,72,256]{2,1,0:T(8,128)(2,1)S(1)}, u32[]{:S(2)}, u32[]{:S(2)}) async-start(bf16[8,72,256]{2,1,0:T(8,128)(2,1)} %shard_map.111), calls=%async_computation.13 | async-start | bytes 589824 | tf_op jit(solution)/shard_map/all_to_all | solution.py:31
  270.8 11.1 %collective-permute-start.3 = (bf16[72,1792]{1,0:T(8,128)(2,1)S(1)}, bf16[72,1792]{1,0:T(8,128)(2,1)S(1)}, u32[]{:S(2)}, u32[]{:S(2)}) collective-permute-start(bf16[72,1792]{1,0:T(8,128)(2,1)S(1)} %copy-done.15), channel_id=1, source_target_pairs={{0,32},{32,0},{1,33},{33,1},{2,34},{34,2},{3,35},{35,3},{4,36},{36... | collective-permute-start | bytes 774152 | tf_op jit(solution)/shard_map/ppermute | solution.py:35
  281.9 6.0 %shard_map.107.w_ref = f32[72,128]{1,0:T(8,128)S(1)} custom-call(bf16[8,12,8,128]{3,2,1,0:T(8,128)(2,1)S(1)} %all_to_all.77.m_ref), custom_call_target="tpu_custom_call" | custom-call | tf_op jit(solution)/shard_map/pallas_call | solution.py:20
  287.9 1.9 all-gather.3
  289.8 0.0 collective-permute-done.3.got_ref
  289.8 1.9 shard_map.108
  291.7 0.0 all-to-all-done.13.p_ref
  291.7 0.2 shard_map.112
  291.9 1.9 all-gather.4
  293.8 0.7 copy.11
  (24 shorter events, 0.2 us)
Async XLA Ops:
  0.6 33.7 %copy-start.13 = (s32[48,1]{1,0:T(8,128)S(1)}, s32[48,1]{1,0:T(8,128)}, u32[]{:S(2)}) copy-start(s32[48,1]{1,0:T(8,128)} %constant.7.clone.rows_ref) | copy-start | bytes 580
  0.6 17.1 %copy-start.16 = (bf16[12,2,256]{2,1,0:T(2,128)(2,1)S(1)}, bf16[12,2,256]{2,1,0:T(2,128)(2,1)}, u32[]{:S(2)}) copy-start(bf16[12,2,256]{2,1,0:T(2,128)(2,1)} %param.9) | copy-start | bytes 36868
  10.8 75.9 %collective-permute-start.1 = (bf16[1792,896]{1,0:T(8,128)(2,1)}, bf16[1792,896]{1,0:T(8,128)(2,1)}, u32[]{:S(2)}, u32[]{:S(2)}) collective-permute-start(bf16[1792,896]{1,0:T(8,128)(2,1)} %w_ref.8), channel_id=1, source_target_pairs={{0,32},{32,0},{1,33},{33,1},{2,34},{34,2},{3,35},{35,3},{4,36},{36... | collective-permute-start | bytes 9633800 | tf_op jit(solution)/shard_map/ppermute | solution.py:35
  13.1 21.2 %all-to-all-start = ((bf16[8,8,3584]{2,1,0:T(8,128)(2,1)}), bf16[8,8,3584]{2,1,0:T(8,128)(2,1)S(1)}, u32[]{:S(2)}, u32[]{:S(2)}) async-start(bf16[8,8,3584]{2,1,0:T(8,128)(2,1)} %shard_map.95), calls=%async_computation | async-start | bytes 917504 | tf_op jit(solution)/shard_map/all_to_all | solution.py:31
  35.8 4.4 %copy-start.3 = (bf16[256,512]{1,0:T(8,128)(2,1)S(1)}, bf16[256,512]{1,0:T(8,128)(2,1)}, u32[]{:S(2)}) copy-start(bf16[256,512]{1,0:T(8,128)(2,1)} %w_ref.9) | copy-start | bytes 786436
  35.8 25.1 %copy-start.12 = (bf16[72,256]{1,0:T(8,128)(2,1)S(1)}, bf16[72,256]{1,0:T(8,128)(2,1)}, u32[]{:S(2)}) copy-start(bf16[72,256]{1,0:T(8,128)(2,1)} %s_ref.1) | copy-start | bytes 110596
  35.8 28.1 %all-to-all-start.1 = ((bf16[4,48,3584]{2,1,0:T(8,128)(2,1)}), bf16[4,48,3584]{2,1,0:T(8,128)(2,1)}, u32[]{:S(2)}, u32[]{:S(2)}) async-start(bf16[4,48,3584]{2,1,0:T(8,128)(2,1)} %shard_map.96), calls=%async_computation.1 | async-start | bytes 2752512 | tf_op jit(solution)/shard_map/all_to_all | solution.py:31
  40.2 46.5 %copy-start = (bf16[1792,896]{1,0:T(8,128)(2,1)S(1)}, bf16[1792,896]{1,0:T(8,128)(2,1)}, u32[]{:S(2)}) copy-start(bf16[1792,896]{1,0:T(8,128)(2,1)} %w_ref.8) | copy-start | bytes 9633796
  40.2 20.6 %collective-permute-start = (bf16[256,512]{1,0:T(8,128)(2,1)S(1)}, bf16[256,512]{1,0:T(8,128)(2,1)S(1)}, u32[]{:S(2)}, u32[]{:S(2)}) collective-permute-start(bf16[256,512]{1,0:T(8,128)(2,1)S(1)} %copy-done.3), channel_id=1, source_target_pairs={{0,32},{32,0},{1,33},{33,1},{2,34},{34,2},{3,35},{35,3},{4,36},{36... | collective-permute-start | bytes 786440 | tf_op jit(solution)/shard_map/ppermute | solution.py:35
  60.9 0.9 copy-start.11
  62.4 0.8 copy-start.2
  63.2 0.7 copy-start.4
  106.1 30.3 %all-to-all-start.4 = ((bf16[32,9,8,128]{3,2,1,0:T(8,128)(2,1)}), bf16[32,9,8,128]{3,2,1,0:T(8,128)(2,1)}, u32[]{:S(2)}, u32[]{:S(2)}) async-start(bf16[32,9,8,128]{3,2,1,0:T(8,128)(2,1)} %broadcast_in_dim.2), calls=%async_computation.4 | async-start | bytes 1179648 | tf_op jit(solution)/shard_map/all_to_all | solution.py:31
  112.4 23.0 %collective-permute-start.2 = (bf16[896,512]{1,0:T(8,128)(2,1)}, bf16[896,512]{1,0:T(8,128)(2,1)S(1)}, u32[]{:S(2)}, u32[]{:S(2)}) collective-permute-start(bf16[896,512]{1,0:T(8,128)(2,1)} %e_ref.1), channel_id=1, source_target_pairs={{0,32},{32,0},{1,33},{33,1},{2,34},{34,2},{3,35},{35,3},{4,36},{36... | collective-permute-start | bytes 2752520 | tf_op jit(solution)/shard_map/ppermute | solution.py:35
  135.4 0.9 copy-start.7
  136.3 1.1 copy-start.1
  137.4 1.2 copy-start.6
  138.6 1.2 copy-start.8
  213.0 0.7 copy-start.9
  213.7 0.7 copy-start.14
  225.8 40.6 %copy-start.5 = (bf16[256,512]{1,0:T(8,128)(2,1)S(1)}, bf16[256,512]{1,0:T(8,128)(2,1)}, u32[]{:S(2)}) copy-start(bf16[256,512]{1,0:T(8,128)(2,1)} %copy-done.4) | copy-start | bytes 786436
  237.4 33.4 %copy-start.15 = (bf16[72,1792]{1,0:T(8,128)(2,1)S(1)}, bf16[72,1792]{1,0:T(8,128)(2,1)}, u32[]{:S(2)}) copy-start(bf16[72,1792]{1,0:T(8,128)(2,1)} %copy-done.14) | copy-start | bytes 774148
  237.4 52.3 %copy-start.10 = (bf16[72,1792]{1,0:T(8,128)(2,1)S(1)}, bf16[72,1792]{1,0:T(8,128)(2,1)}, u32[]{:S(2)}) copy-start(bf16[72,1792]{1,0:T(8,128)(2,1)} %copy-done.9) | copy-start | bytes 774148
  267.4 24.3 %all-to-all-start.13 = ((bf16[8,72,256]{2,1,0:T(8,128)(2,1)}), bf16[8,72,256]{2,1,0:T(8,128)(2,1)S(1)}, u32[]{:S(2)}, u32[]{:S(2)}) async-start(bf16[8,72,256]{2,1,0:T(8,128)(2,1)} %shard_map.111), calls=%async_computation.13 | async-start | bytes 589824 | tf_op jit(solution)/shard_map/all_to_all | solution.py:31
  270.8 18.9 %collective-permute-start.3 = (bf16[72,1792]{1,0:T(8,128)(2,1)S(1)}, bf16[72,1792]{1,0:T(8,128)(2,1)S(1)}, u32[]{:S(2)}, u32[]{:S(2)}) collective-permute-start(bf16[72,1792]{1,0:T(8,128)(2,1)S(1)} %copy-done.15), channel_id=1, source_target_pairs={{0,32},{32,0},{1,33},{33,1},{2,34},{34,2},{3,35},{35,3},{4,36},{36... | collective-permute-start | bytes 774152 | tf_op jit(solution)/shard_map/ppermute | solution.py:35

commit v5 on v4

--- a/solution.py
+++ b/solution.py
@@ -1,6 +1,5 @@
 import jax
 import jax.numpy as jnp
-import numpy as np
 from jax import lax
 from jax.experimental import pallas as pl
 from jax.experimental.pallas import tpu as pltpu
@@ -14,7 +13,7 @@
 MIB = 1024 * 1024
 
 
-def call(body, out, *args, limit=40):
+def call(body, out, *args, limit=32):
     many = isinstance(out, list)
     shapes = [jax.ShapeDtypeStruct(s, d) for s, d in (out if many else [out])]
     got = pl.pallas_call(
@@ -52,6 +51,19 @@
         out_ref[t // slots, t % slots] = tile.astype(BF)
 
 
+def to_flat_tiles(y, out_ref):
+    lanes = y.shape[1] // 128
+    count = (y.shape[0] // 8) * lanes
+
+    def tile(t):
+        r, g = divmod(t, lanes)
+        return y[r * 8 : r * 8 + 8, g * 128 : g * 128 + 128] if t < count else jnp.zeros((8, 128), F32)
+
+    for t in range(0, out_ref.shape[0] // 8, 2):
+        pair = jnp.concatenate([tile(t), tile(t + 1)], axis=0)
+        out_ref[t * 8 : t * 8 + 16] = pair.astype(BF)
+
+
 def from_tiles(ref, lanes, rows=72, slots=None):
     slots = slots or ref.shape[1]
     lines = []
@@ -75,30 +87,44 @@
     out_ref[...] = jnp.broadcast_to(total[None], out_ref.shape)
 
 
+def sum_flat_body(x_ref, out_ref):
+    total = jnp.sum(x_ref[...].astype(F32), axis=0).reshape(-1, 128)
+    peers = jnp.broadcast_to(total[None], (x_ref.shape[0], *total.shape))
+    out_ref[...] = peers.reshape(out_ref.shape).astype(BF)
+
+
 def sum_over(pieces, axes):
     own = swap(pieces, axes)
     return swap(call(sum_body, (own.shape, BF), own), axes)
 
 
-def picked(rows, x):
-    lanes = lax.broadcasted_iota(jnp.int32, (rows.shape[0], x.shape[0]), 1)
-    return dot(jnp.where(lanes == rows, 1.0, 0.0).astype(BF), x).astype(BF)
+def picked(n, to, x):
+    rows = lax.broadcasted_iota(jnp.int32, (n, x.shape[0]), 0)
+    return dot(jnp.where(rows == to, 1.0, 0.0).astype(BF), x).astype(BF)
+
+
+def row_numbers(n):
+    return lax.broadcasted_iota(jnp.int32, (1, n), 1)
 
 
 def pack_body(x_ref, out_ref):
     core = lax.axis_index("core")
-    t = lax.broadcasted_iota(jnp.int32, (8, 1), 0)
-    x = x_ref[...]
+    m = row_numbers(32)
+    token = (m & 15) >> 1
     parts = []
     for other in range(2):
-        at = jnp.where(core == other, 0, 16) + 2 * t + core
-        parts.append(picked(jnp.where(t < 6, at, -1), x))
-    packed = jnp.concatenate(parts, axis=1)
-    out_ref[...] = jnp.broadcast_to(packed[None], out_ref.shape)
-
-
-def dense_body(rows_ref, x_ref, out_ref):
-    y = picked(rows_ref[...], x_ref[...])
+        block = core if other == 0 else 1 - core
+        mine = jnp.logical_and((m >> 4) == block, (m & 1) == core)
+        parts.append(picked(8, jnp.where(mine, token, -1), x_ref[...]))
+    packed = jnp.concatenate(parts, axis=1).astype(F32)
+    peers = jnp.broadcast_to(packed[None], (8, *packed.shape))
+    out_ref[...] = peers.reshape(out_ref.shape).astype(BF)
+
+
+def dense_body(x_ref, out_ref):
+    m = row_numbers(64)
+    token = m & 7
+    y = picked(48, jnp.where(token < 6, (m >> 3) * 6 + token, -1), x_ref[...])
     out_ref[...] = jnp.broadcast_to(y[None], out_ref.shape)
 
 
@@ -108,13 +134,17 @@
     out_ref[...] = y.astype(BF)
 
 
-def grad_body(rows_ref, g_ref, s_ref, w_ref, v_ref, out_ref):
-    g = picked(rows_ref[...] + lax.axis_index("core"), g_ref[...])
+def grad_body(g_ref, s_ref, w_ref, v_ref, out_ref):
+    m = row_numbers(384)
+    token = m >> 1
+    peer = jnp.floor((token.astype(F32) + 0.5) * (1.0 / 6.0)).astype(jnp.int32)
+    to = (peer & 3) * 48 + (peer >> 2) * 6 + token - peer * 6
+    g = picked(192, jnp.where((m & 1) == lax.axis_index("core"), to, -1), g_ref[...])
     s = s_ref[...]
     w, v = w_ref[...], v_ref[...]
     top = jnp.concatenate([dot(g, w), dot(g, v)], axis=1)
     low = jnp.concatenate([dot(s, w), dot(s, v)], axis=1)
-    to_tiles(jnp.concatenate([top, low], axis=0), out_ref)
+    to_flat_tiles(jnp.concatenate([top, low], axis=0), out_ref)
 
 
 def scaled_body(a_ref, g_ref, e_ref, f_ref, scaled_ref, out_ref):
@@ -176,7 +206,7 @@
 
 def core_body(m_ref, s_ref, out_ref):
     m = from_tiles(m_ref, 7, slots=9).astype(BF)
-    to_tiles(dot(m, s_ref[...]), out_ref)
+    to_flat_tiles(dot(m, s_ref[...]), out_ref)
 
 
 def inverse_body(m_ref, out_ref):
@@ -211,7 +241,8 @@
     c = from_tiles(c_ref, 8).astype(BF)
     n = w_ref.shape[1]
     y = dot(c[:, :n], w_ref[...], 1, 1) + dot(c[:, n:], v_ref[...], 1, 1)
-    out_ref[...] = jnp.broadcast_to(y.astype(BF)[None], out_ref.shape)
+    peers = jnp.broadcast_to(y[None], (8, *y.shape))
+    out_ref[...] = peers.reshape(out_ref.shape).astype(BF)
 
 
 def final_body(w_ref, p_ref, out_ref):
@@ -219,54 +250,55 @@
     out_ref[...] = dot(w_ref[...][:, :72], p, precision=lax.Precision.HIGHEST)
 
 
-DENSE = np.array([[8 * z + t] for z in range(8) for t in range(6)], np.int32)
-TOKENS = np.array(
-    [[2 * ((z * 4 + x) * 6 + t)] for x in range(4) for z in range(8) for t in range(6)], np.int32
-)
-
-
 def on_device(acts, grads, basis_in, basis_out, eigen, sketch):
     lines = jnp.pad(acts.reshape(12, 1792), ((0, 4), (0, 0)))
     lines = lax.all_gather(lines, "core").reshape(32, 1792)
-    packed = call(pack_body, ((8, 8, 3584), BF), lines)
-    packed, away = lax.optimization_barrier((packed, (basis_in, basis_out, eigen)))
-    far_in, far_out, far_eigen = [from_sibling(w) for w in away]
-    near = swap(packed, "z").reshape(64, 3584)
-    near, own_grads = lax.optimization_barrier((near, grads.reshape(24, 256)))
-    dense = call(dense_body, ((4, 48, 3584), BF), jnp.asarray(DENSE), near)
+    packed = call(pack_body, ((64, 3584), BF), lines, limit=62)
+    packed, own_grads, away_out = lax.optimization_barrier((packed, grads, basis_out))
+    own_grads = own_grads.reshape(24, 256)
+    own_grads, away_in = lax.optimization_barrier((own_grads, basis_in))
+    far_out, far_in = from_sibling(away_out), from_sibling(away_in)
+    near = swap(packed.reshape(8, 8, 3584), "z").reshape(64, 3584)
+    near, own_grads, far_out, far_in = lax.optimization_barrier((near, own_grads, far_out, far_in))
+    dense = call(dense_body, ((4, 48, 3584), BF), near, limit=62)
     all_grads = lax.all_gather(own_grads, ROW).reshape(384, 256)
     g_part = call(
-        grad_body, ((32, 9, 8, 128), BF),
-        jnp.asarray(TOKENS), all_grads, sketch, basis_out, far_out,
+        grad_body, ((2304, 128), BF), all_grads, sketch, basis_out, far_out, limit=62
     )
     both = swap(dense, "x").reshape(192, 3584)
-    both, g_part = lax.optimization_barrier((both, g_part))
-    g_own = summed(g_part, COL)
+    both, g_part, away = lax.optimization_barrier((both, g_part, eigen))
+    g_pieces = swap(g_part.reshape(32, 9, 8, 128), COL)
     a_part = call(act_body, ((192, 896), BF), both, basis_in, far_in)
-    a_part, g_own = lax.optimization_barrier((a_part, g_own))
+    a_part, g_pieces, far_eigen = lax.optimization_barrier((a_part, g_pieces, from_sibling(away)))
+    g_own = call(sum_flat_body, ((2304, 128), BF), g_pieces, limit=62)
     a_own = summed(a_part.reshape(8, 24, 896), "y")
     a_own, g_own = lax.optimization_barrier((a_own, g_own))
-    g_rot = swap(jnp.broadcast_to(g_own[None], (32, 9, 8, 128)), COL)
+    g_rot = swap(g_own.reshape(32, 9, 8, 128), COL)
     a_rot = lax.all_gather(a_own, ROW).reshape(8, 2, 24, 896)
     scaled, red = call(
-        scaled_body, [((896, 1024), BF), ((8, 8, 8, 128), BF)], a_rot, g_rot, eigen, far_eigen
+        scaled_body, [((896, 1024), BF), ((8, 8, 8, 128), BF)],
+        a_rot, g_rot, eigen, far_eigen,
     )
     reduced = sum_over(red, "y")
-    span = sum_over(call(range_body, ((32, 8, 8, 128), BF), reduced, basis_in, far_in), COL)
+    span = call(range_body, ((32, 8, 8, 128), BF), reduced, basis_in, far_in)
+    span = sum_over(span, COL)
     mapped, keep, give = call(
         mapped_body,
         [((8, 12, 8, 128), BF), ((72, 1792), BF), ((72, 1792), BF)],
         span, basis_in, far_in,
     )
     mapped = swap(call(gram_sum_body, ((8, 12, 8, 128), BF), swap(mapped, "y")), "y")
-    core = sum_over(call(core_body, ((32, 3, 8, 128), BF), mapped, scaled), COL)
-    part = call(project_body, ((8, 72, 256), BF), core, basis_out, far_out)
+    core = call(core_body, ((768, 128), BF), mapped, scaled)
+    core = swap(core.reshape(32, 3, 8, 128), COL)
     inverse = call(inverse_body, ((72, 128), F32), mapped)
-    basis = call(
-        basis_body, ((2, 72, 1792), F32),
-        lax.all_gather(inverse, "core"), keep, from_sibling(give),
-    )
-    mine = call(final_body, ((72, 256), F32), inverse, swap(part, "y"))
+    core, inverse, give = lax.optimization_barrier((core, inverse, give))
+    core = call(sum_flat_body, ((768, 128), BF), core)
+    core = swap(core.reshape(32, 3, 8, 128), COL)
+    both_inverses = lax.all_gather(inverse, "core")
+    core, both_inverses, got = lax.optimization_barrier((core, both_inverses, from_sibling(give)))
+    part = call(project_body, ((576, 256), BF), core, basis_out, far_out)
+    basis = call(basis_body, ((2, 72, 1792), F32), both_inverses, keep, got)
+    mine = call(final_body, ((72, 256), F32), inverse, swap(part.reshape(8, 72, 256), "y"))
     return basis, lax.all_gather(mine, "core")
 
 

time: 296 us -> 285 us (0.963)
  blocking collectives: 200 us -> 146 us
  waiting for transfers between devices: 16.6 us -> 42.6 us
  starting transfers between devices: 40 us -> 54.7 us
    all_to_all x10 -> x6, blocking collectives: 152 us -> 85.9 us  [swap(): return lax.all_to_all(x, axes, 0, 0, tiled=True)]
    all_to_all x4 -> x8, waiting for transfers between devices: 16.5 us -> 41.4 us  [swap(): return lax.all_to_all(x, axes, 0, 0, tiled=True)]
    all_to_all x4 -> x8, starting transfers between devices: 18.9 us -> 38.8 us  [swap(): return lax.all_to_all(x, axes, 0, 0, tiled=True)]
    all_gather x1, blocking collectives: 1.91 us -> 9.94 us  [on_device(): return (basis, lax.all_gather(mine, 'core'))]
    ppermute x4, starting transfers between devices: 21.2 us -> 15.8 us  [from_sibling(): return lax.ppermute(x, 'core', [(0, 1), (1, 0)])]
    unnamed x35 -> x25, local copies, waits for them, and re-layouts: 8.88 us -> 10.2 us
  transfers between devices with their start and end apart: 8 -> 12, of which waited for: 1 -> 6; matrix products, arithmetic and copies ran while one was open for 0% -> 0% of each run, Pallas kernels for 3% -> 5%
where the time goes in v5:
time: 285 us; the launch traced here: 284 us
  blocking collectives  146 us (51%)
  starting transfers between devices  54.7 us (19%)
  waiting for transfers between devices  42.6 us (15%)
  Pallas kernels  27.9 us (10%)
  local copies, waits for them, and re-layouts  11.7 us (4%)
    all_to_all x6, blocking collectives, swap(): return lax.all_to_all(x, axes, 0, 0, tiled=True)  85.9 us
    all_to_all x8, waiting for transfers between devices, swap(): return lax.all_to_all(x, axes, 0, 0, tiled=True)  41.4 us
    all_to_all x8, starting transfers between devices, swap(): return lax.all_to_all(x, axes, 0, 0, tiled=True)  38.8 us
    pallas_call x18, Pallas kernels, call(): pl.pallas_call(body, out_shape=shapes, in_specs=[pl.BlockSpec(memory_spac...  27.9 us
    all_gather x1, blocking collectives, on_device(): all_grads = lax.all_gather(own_grads, ROW).reshape(384, 256)  20.1 us
    all_gather x1, blocking collectives, on_device(): a_rot = lax.all_gather(a_own, ROW).reshape(8, 2, 24, 896)  19.8 us
    ppermute x4, starting transfers between devices, from_sibling(): return lax.ppermute(x, 'core', [(0, 1), (1, 0)])  15.8 us
    unnamed x25, local copies, waits for them, and re-layouts  10.2 us
  transfers between devices with their start and end apart: 12, of which 6 were waited for; matrix products, arithmetic and copies ran while one was open for 0% of the time, Pallas kernels for 5%

profile of v5, /device:TPU:1, one launch (start us, length us, event | category | flops | bytes accessed | tf_op | source)
XLA Modules:
  0.0 283.8 jit_solution(2982595603760873030)
XLA Ops:
  0.6 0.0 copy-start.6
  0.6 0.8 reshape.46
  1.5 8.5 %all-gather.x_ref = bf16[32,1792]{1,0:T(8,128)(2,1)} all-gather(bf16[16,1792]{1,0:T(8,128)(2,1)S(1)} %pad.4), channel_id=2, replica_groups=mesh['y'=8,'core'=2,'z'=8,'x'=4] {'core'}, dimensions={0}, use_global_device_ids=true | all-gather | bytes 172032 | tf_op jit(solution)/shard_map/all_gather | solution.py:255
  10.1 1.8 shard_map.77
  11.9 0.7 reshape.50
  12.6 2.3 collective-permute-start.1
  14.9 4.7 %all-to-all-start = ((bf16[8,8,3584]{2,1,0:T(8,128)(2,1)}), bf16[8,8,3584]{2,1,0:T(8,128)(2,1)}, u32[]{:S(2)}, u32[]{:S(2)}) async-start(bf16[8,8,3584]{2,1,0:T(8,128)(2,1)} %bitcast.17), calls=%async_computation | async-start | bytes 917504 | tf_op jit(solution)/shard_map/all_to_all | solution.py:30
  19.5 2.3 collective-permute-start
  21.9 1.3 collective-permute-done.v_ref
  23.2 13.0 %all-to-all-done = bf16[8,8,3584]{2,1,0:T(8,128)(2,1)} async-done(((bf16[8,8,3584]{2,1,0:T(8,128)(2,1)}), bf16[8,8,3584]{2,1,0:T(8,128)(2,1)}, u32[]{:S(2)}, u32[]{:S(2)}) %all-to-all-start) | async-done | bytes 458784 | tf_op jit(solution)/shard_map/all_to_all | solution.py:30
  36.2 0.0 collective-permute-done.1.v_ref
  36.2 1.6 copy-done.2
  37.9 2.3 shard_map.78
  40.2 4.0 %all-to-all-start.1 = ((bf16[4,48,3584]{2,1,0:T(8,128)(2,1)}), bf16[4,48,3584]{2,1,0:T(8,128)(2,1)S(1)}, u32[]{:S(2)}, u32[]{:S(2)}) async-start(bf16[4,48,3584]{2,1,0:T(8,128)(2,1)} %shard_map.78), calls=%async_computation.1 | async-start | bytes 2752512 | tf_op jit(solution)/shard_map/all_to_all | solution.py:30
  44.2 20.1 %all-gather.1.g_ref = bf16[384,256]{1,0:T(8,128)(2,1)} all-gather(bf16[24,256]{1,0:T(8,128)(2,1)S(1)} %reshape.50), channel_id=3, replica_groups=mesh['y'=8,'core'=2,'z'=8,'x'=4] {'y','core'}, dimensions={0}, use_global_device_ids=true | all-gather | bytes 208896 | tf_op jit(solution)/shard_map/all_gather | solution.py:264
  64.3 2.6 shard_map.79
  66.8 0.0 all-to-all-done.1
  66.8 4.9 %all-to-all-start.2 = ((bf16[32,9,8,128]{3,2,1,0:T(8,128)(2,1)}), bf16[32,9,8,128]{3,2,1,0:T(8,128)(2,1)S(1)}, u32[]{:S(2)}, u32[]{:S(2)}) async-start(bf16[32,9,8,128]{3,2,1,0:T(8,128)(2,1)} %bitcast.16), calls=%async_computation.2 | async-start | bytes 1179648 | tf_op jit(solution)/shard_map/all_to_all | solution.py:30
  71.8 2.4 collective-permute-start.2
  74.1 0.0 copy-start
  74.1 1.9 copy-done
  76.0 1.9 copy-done.3
  78.0 2.3 shard_map.80
  80.3 0.0 collective-permute-done.2.f_ref
  80.3 0.9 copy-done.9
  81.2 8.4 %all-to-all-done.2.x_ref = bf16[32,9,8,128]{3,2,1,0:T(8,128)(2,1)S(1)} async-done(((bf16[32,9,8,128]{3,2,1,0:T(8,128)(2,1)}), bf16[32,9,8,128]{3,2,1,0:T(8,128)(2,1)S(1)}, u32[]{:S(2)}, u32[]{:S(2)}) %all-to-all-start.2) | async-done | bytes 589856 | tf_op jit(solution)/shard_map/all_to_all | solution.py:30
  89.6 4.0 %all-to-all-start.3 = ((bf16[8,24,896]{2,1,0:T(8,128)(2,1)}), bf16[8,24,896]{2,1,0:T(8,128)(2,1)S(1)}, u32[]{:S(2)}, u32[]{:S(2)}) async-start(bf16[8,24,896]{2,1,0:T(8,128)(2,1)} %bitcast.4), calls=%async_computation.3 | async-start | bytes 688128 | tf_op jit(solution)/shard_map/all_to_all | solution.py:30
  93.7 0.0 copy-done.11
  93.7 0.0 copy-start.8
  93.7 2.1 shard_map.82
  95.8 8.5 %all-to-all-done.3.x_ref = bf16[8,24,896]{2,1,0:T(8,128)(2,1)S(1)} async-done(((bf16[8,24,896]{2,1,0:T(8,128)(2,1)}), bf16[8,24,896]{2,1,0:T(8,128)(2,1)S(1)}, u32[]{:S(2)}, u32[]{:S(2)}) %all-to-all-start.3) | async-done | bytes 344096 | tf_op jit(solution)/shard_map/all_to_all | solution.py:30
  104.3 6.2 %all-to-all-start.4 = ((bf16[32,9,8,128]{3,2,1,0:T(8,128)(2,1)}), bf16[32,9,8,128]{3,2,1,0:T(8,128)(2,1)S(1)}, u32[]{:S(2)}, u32[]{:S(2)}) async-start(bf16[32,9,8,128]{3,2,1,0:T(8,128)(2,1)} %bitcast.15), calls=%async_computation.4 | async-start | bytes 1179648 | tf_op jit(solution)/shard_map/all_to_all | solution.py:30
  110.5 19.8 %all-gather.2 = bf16[384,896]{1,0:T(8,128)(2,1)S(1)} all-gather(bf16[24,896]{1,0:T(8,128)(2,1)S(1)} %shard_map.81), channel_id=4, replica_groups=mesh['y'=8,'core'=2,'z'=8,'x'=4] {'y','core'}, dimensions={0}, use_global_device_ids=true | all-gather | bytes 731136 | tf_op jit(solution)/shard_map/all_gather | solution.py:277
  130.3 0.0 all-to-all-done.4.g_ref
  130.3 1.2 copy-done.10
  131.5 1.2 shard_map.83
  132.6 11.5 %all_to_all.70.x_ref = bf16[8,8,8,128]{3,2,1,0:T(8,128)(2,1)S(1)} all-to-all(bf16[8,8,8,128]{3,2,1,0:T(8,128)(2,1)S(1)} %get-tuple-element.47), channel_id=1, replica_groups=mesh['y'=8,'core'=2,'z'=8,'x'=4] {'y'}, dimensions={0} | all-to-all | bytes 262144 | tf_op jit(solution)/shard_map/all_to_all | solution.py:30
  144.2 10.3 %all_to_all.71.r_ref = bf16[8,8,8,128]{3,2,1,0:T(8,128)(2,1)S(1)} all-to-all(bf16[8,8,8,128]{3,2,1,0:T(8,128)(2,1)S(1)} %shard_map.84), channel_id=1, replica_groups=mesh['y'=8,'core'=2,'z'=8,'x'=4] {'y'}, dimensions={0} | all-to-all | bytes 262144 | tf_op jit(solution)/shard_map/all_to_all | solution.py:30
  154.5 0.0 copy-done.1
  154.5 1.9 copy-done.4
  156.4 2.1 shard_map.85
  158.5 22.7 %all_to_all.72.x_ref = bf16[32,8,8,128]{3,2,1,0:T(8,128)(2,1)S(1)} all-to-all(bf16[32,8,8,128]{3,2,1,0:T(8,128)(2,1)S(1)} %shard_map.85), channel_id=1, replica_groups=mesh['y'=8,'core'=2,'z'=8,'x'=4] {'z','x'}, dimensions={0} | all-to-all | bytes 1048576 | tf_op jit(solution)/shard_map/all_to_all | solution.py:30
  181.2 0.1 shard_map.86
  181.3 18.9 %all_to_all.73.r_ref = bf16[32,8,8,128]{3,2,1,0:T(8,128)(2,1)S(1)} all-to-all(bf16[32,8,8,128]{3,2,1,0:T(8,128)(2,1)S(1)} %shard_map.86), channel_id=1, replica_groups=mesh['y'=8,'core'=2,'z'=8,'x'=4] {'z','x'}, dimensions={0} | all-to-all | bytes 1048576 | tf_op jit(solution)/shard_map/all_to_all | solution.py:30
  200.3 1.4 shard_map.87
  201.7 11.3 %all_to_all.74.x_ref = bf16[8,12,8,128]{3,2,1,0:T(8,128)(2,1)S(1)} all-to-all(bf16[8,12,8,128]{3,2,1,0:T(8,128)(2,1)S(1)} %get-tuple-element.48), channel_id=1, replica_groups=mesh['y'=8,'core'=2,'z'=8,'x'=4] {'y'}, dimensions={0} | all-to-all | bytes 393216 | tf_op jit(solution)/shard_map/all_to_all | solution.py:30
  213.1 11.0 %all_to_all.75.m_ref = bf16[8,12,8,128]{3,2,1,0:T(8,128)(2,1)S(1)} all-to-all(bf16[8,12,8,128]{3,2,1,0:T(8,128)(2,1)S(1)} %shard_map.88), channel_id=1, replica_groups=mesh['y'=8,'core'=2,'z'=8,'x'=4] {'y'}, dimensions={0} | all-to-all | bytes 393216 | tf_op jit(solution)/shard_map/all_to_all | solution.py:30
  224.1 1.1 shard_map.89
  225.2 6.2 %all-to-all-start.11 = ((bf16[32,3,8,128]{3,2,1,0:T(8,128)(2,1)}), bf16[32,3,8,128]{3,2,1,0:T(8,128)(2,1)S(1)}, u32[]{:S(2)}, u32[]{:S(2)}) async-start(bf16[32,3,8,128]{3,2,1,0:T(8,128)(2,1)} %bitcast.7), calls=%async_computation.11 | async-start | bytes 393216 | tf_op jit(solution)/shard_map/all_to_all | solution.py:30
  231.5 6.0 %shard_map.90.w_ref = f32[72,128]{1,0:T(8,128)S(1)} custom-call(bf16[8,12,8,128]{3,2,1,0:T(8,128)(2,1)S(1)} %all_to_all.75.m_ref), custom_call_target="tpu_custom_call" | custom-call | tf_op jit(solution)/shard_map/pallas_call | solution.py:19
  237.5 3.7 %all-to-all-done.11.x_ref = bf16[32,3,8,128]{3,2,1,0:T(8,128)(2,1)S(1)} async-done(((bf16[32,3,8,128]{3,2,1,0:T(8,128)(2,1)}), bf16[32,3,8,128]{3,2,1,0:T(8,128)(2,1)S(1)}, u32[]{:S(2)}, u32[]{:S(2)}) %all-to-all-start.11) | async-done | bytes 196640 | tf_op jit(solution)/shard_map/all_to_all | solution.py:30
  241.2 0.7 shard_map.91
  241.9 5.3 %all-to-all-start.12 = ((bf16[32,3,8,128]{3,2,1,0:T(8,128)(2,1)}), bf16[32,3,8,128]{3,2,1,0:T(8,128)(2,1)S(1)}, u32[]{:S(2)}, u32[]{:S(2)}) async-start(bf16[32,3,8,128]{3,2,1,0:T(8,128)(2,1)} %bitcast.8), calls=%async_computation.12 | async-start | bytes 393216 | tf_op jit(solution)/shard_map/all_to_all | solution.py:30
  247.2 8.9 %collective-permute-start.3 = (bf16[72,1792]{1,0:T(8,128)(2,1)S(1)}, bf16[72,1792]{1,0:T(8,128)(2,1)S(1)}, u32[]{:S(2)}, u32[]{:S(2)}) collective-permute-start(bf16[72,1792]{1,0:T(8,128)(2,1)S(1)} %get-tuple-element.53), channel_id=1, source_target_pairs={{0,32},{32,0},{1,33},{33,1},{2,34},{34,2},{3,35},{35,3},{4,36},{36... | collective-permute-start | bytes 774152 | tf_op jit(solution)/shard_map/ppermute | solution.py:34
  256.1 1.9 all-gather.3
  258.0 0.0 collective-permute-done.3.got_ref
  258.0 0.0 all-to-all-done.12.c_ref
  258.0 1.9 shard_map.93
  259.9 3.4 %all-to-all-start.13 = ((bf16[8,72,256]{2,1,0:T(8,128)(2,1)}), bf16[8,72,256]{2,1,0:T(8,128)(2,1)S(1)}, u32[]{:S(2)}, u32[]{:S(2)}) async-start(bf16[8,72,256]{2,1,0:T(8,128)(2,1)} %bitcast.10), calls=%async_computation.13 | async-start | bytes 589824 | tf_op jit(solution)/shard_map/all_to_all | solution.py:30
  263.4 1.9 shard_map.92
  265.3 7.7 %all-to-all-done.13.p_ref = bf16[8,72,256]{2,1,0:T(8,128)(2,1)S(1)} async-done(((bf16[8,72,256]{2,1,0:T(8,128)(2,1)}), bf16[8,72,256]{2,1,0:T(8,128)(2,1)S(1)}, u32[]{:S(2)}, u32[]{:S(2)}) %all-to-all-start.13) | async-done | bytes 294944 | tf_op jit(solution)/shard_map/all_to_all | solution.py:30
  273.0 0.2 shard_map.94
  273.2 9.9 %all-gather.4 = f32[144,256]{1,0:T(8,128)S(1)} all-gather(f32[72,256]{1,0:T(8,128)S(1)} %shard_map.94), channel_id=6, replica_groups=mesh['y'=8,'core'=2,'z'=8,'x'=4] {'core'}, dimensions={0}, use_global_device_ids=true | all-gather | bytes 221184 | tf_op jit(solution)/shard_map/all_gather | solution.py:302
  283.1 0.7 copy.9
  (17 shorter events, 0.1 us)
Async XLA Ops:
  0.6 18.9 %copy-start.6 = (bf16[256,512]{1,0:T(8,128)(2,1)S(1)}, bf16[256,512]{1,0:T(8,128)(2,1)}, u32[]{:S(2)}) copy-start(bf16[256,512]{1,0:T(8,128)(2,1)} %w_ref.9) | copy-start | bytes 786436
  12.6 23.6 %collective-permute-start.1 = (bf16[1792,896]{1,0:T(8,128)(2,1)}, bf16[1792,896]{1,0:T(8,128)(2,1)S(1)}, u32[]{:S(2)}, u32[]{:S(2)}) collective-permute-start(bf16[1792,896]{1,0:T(8,128)(2,1)} %w_ref.8), channel_id=1, source_target_pairs={{0,32},{32,0},{1,33},{33,1},{2,34},{34,2},{3,35},{35,3},{4,36},{36... | collective-permute-start | bytes 9633800 | tf_op jit(solution)/shard_map/ppermute | solution.py:34
  14.9 21.3 %all-to-all-start = ((bf16[8,8,3584]{2,1,0:T(8,128)(2,1)}), bf16[8,8,3584]{2,1,0:T(8,128)(2,1)}, u32[]{:S(2)}, u32[]{:S(2)}) async-start(bf16[8,8,3584]{2,1,0:T(8,128)(2,1)} %bitcast.17), calls=%async_computation | async-start | bytes 917504 | tf_op jit(solution)/shard_map/all_to_all | solution.py:30
  19.5 3.6 %collective-permute-start = (bf16[256,512]{1,0:T(8,128)(2,1)S(1)}, bf16[256,512]{1,0:T(8,128)(2,1)}, u32[]{:S(2)}, u32[]{:S(2)}) collective-permute-start(bf16[256,512]{1,0:T(8,128)(2,1)S(1)} %copy-done.6), channel_id=1, source_target_pairs={{0,32},{32,0},{1,33},{33,1},{2,34},{34,2},{3,35},{35,3},{4,36},{36... | collective-permute-start | bytes 786440 | tf_op jit(solution)/shard_map/ppermute | solution.py:34
  36.2 1.6 copy-start.2
  40.2 26.7 %all-to-all-start.1 = ((bf16[4,48,3584]{2,1,0:T(8,128)(2,1)}), bf16[4,48,3584]{2,1,0:T(8,128)(2,1)S(1)}, u32[]{:S(2)}, u32[]{:S(2)}) async-start(bf16[4,48,3584]{2,1,0:T(8,128)(2,1)} %shard_map.78), calls=%async_computation.1 | async-start | bytes 2752512 | tf_op jit(solution)/shard_map/all_to_all | solution.py:30
  66.8 22.8 %all-to-all-start.2 = ((bf16[32,9,8,128]{3,2,1,0:T(8,128)(2,1)}), bf16[32,9,8,128]{3,2,1,0:T(8,128)(2,1)S(1)}, u32[]{:S(2)}, u32[]{:S(2)}) async-start(bf16[32,9,8,128]{3,2,1,0:T(8,128)(2,1)} %bitcast.16), calls=%async_computation.2 | async-start | bytes 1179648 | tf_op jit(solution)/shard_map/all_to_all | solution.py:30
  71.8 8.5 %collective-permute-start.2 = (bf16[896,512]{1,0:T(8,128)(2,1)}, bf16[896,512]{1,0:T(8,128)(2,1)S(1)}, u32[]{:S(2)}, u32[]{:S(2)}) collective-permute-start(bf16[896,512]{1,0:T(8,128)(2,1)} %e_ref.1), channel_id=1, source_target_pairs={{0,32},{32,0},{1,33},{33,1},{2,34},{34,2},{3,35},{35,3},{4,36},{36... | collective-permute-start | bytes 2752520 | tf_op jit(solution)/shard_map/ppermute | solution.py:34
  74.1 1.9 copy-start
  76.0 1.9 copy-start.3
  80.3 0.9 copy-start.9
  89.6 4.0 %copy-start.11 = (bf16[32,9,8,128]{3,2,1,0:T(8,128)(2,1)}, bf16[32,9,8,128]{3,2,1,0:T(8,128)(2,1)S(1)}, u32[]{:S(2)}) copy-start(bf16[32,9,8,128]{3,2,1,0:T(8,128)(2,1)S(1)} %all-to-all-done.2.x_ref) | copy-start | bytes 1769476
  89.6 14.6 %all-to-all-start.3 = ((bf16[8,24,896]{2,1,0:T(8,128)(2,1)}), bf16[8,24,896]{2,1,0:T(8,128)(2,1)S(1)}, u32[]{:S(2)}, u32[]{:S(2)}) async-start(bf16[8,24,896]{2,1,0:T(8,128)(2,1)} %bitcast.4), calls=%async_computation.3 | async-start | bytes 688128 | tf_op jit(solution)/shard_map/all_to_all | solution.py:30
  93.7 36.6 %copy-start.8 = (bf16[896,512]{1,0:T(8,128)(2,1)S(1)}, bf16[896,512]{1,0:T(8,128)(2,1)}, u32[]{:S(2)}) copy-start(bf16[896,512]{1,0:T(8,128)(2,1)} %e_ref.1) | copy-start | bytes 2752516
  104.3 26.0 %all-to-all-start.4 = ((bf16[32,9,8,128]{3,2,1,0:T(8,128)(2,1)}), bf16[32,9,8,128]{3,2,1,0:T(8,128)(2,1)S(1)}, u32[]{:S(2)}, u32[]{:S(2)}) async-start(bf16[32,9,8,128]{3,2,1,0:T(8,128)(2,1)} %bitcast.15), calls=%async_computation.4 | async-start | bytes 1179648 | tf_op jit(solution)/shard_map/all_to_all | solution.py:30
  130.3 1.2 copy-start.10
  131.5 23.1 %copy-start.1 = (bf16[1792,896]{1,0:T(8,128)(2,1)S(1)}, bf16[1792,896]{1,0:T(8,128)(2,1)}, u32[]{:S(2)}) copy-start(bf16[1792,896]{1,0:T(8,128)(2,1)} %w_ref.8) | copy-start | bytes 9633796
  154.5 1.9 copy-start.4
  156.4 43.8 %copy-start.5 = (bf16[1792,896]{1,0:T(8,128)(2,1)S(1)}, bf16[1792,896]{1,0:T(8,128)(2,1)}, u32[]{:S(2)}) copy-start(bf16[1792,896]{1,0:T(8,128)(2,1)} %copy-done.2) | copy-start | bytes 9633796
  224.1 33.9 %copy-start.7 = (bf16[256,512]{1,0:T(8,128)(2,1)S(1)}, bf16[256,512]{1,0:T(8,128)(2,1)}, u32[]{:S(2)}) copy-start(bf16[256,512]{1,0:T(8,128)(2,1)} %w_ref.9) | copy-start | bytes 786436
  225.2 15.9 %all-to-all-start.11 = ((bf16[32,3,8,128]{3,2,1,0:T(8,128)(2,1)}), bf16[32,3,8,128]{3,2,1,0:T(8,128)(2,1)S(1)}, u32[]{:S(2)}, u32[]{:S(2)}) async-start(bf16[32,3,8,128]{3,2,1,0:T(8,128)(2,1)} %bitcast.7), calls=%async_computation.11 | async-start | bytes 393216 | tf_op jit(solution)/shard_map/all_to_all | solution.py:30
  241.9 16.1 %all-to-all-start.12 = ((bf16[32,3,8,128]{3,2,1,0:T(8,128)(2,1)}), bf16[32,3,8,128]{3,2,1,0:T(8,128)(2,1)S(1)}, u32[]{:S(2)}, u32[]{:S(2)}) async-start(bf16[32,3,8,128]{3,2,1,0:T(8,128)(2,1)} %bitcast.8), calls=%async_computation.12 | async-start | bytes 393216 | tf_op jit(solution)/shard_map/all_to_all | solution.py:30
  247.2 10.7 %collective-permute-start.3 = (bf16[72,1792]{1,0:T(8,128)(2,1)S(1)}, bf16[72,1792]{1,0:T(8,128)(2,1)S(1)}, u32[]{:S(2)}, u32[]{:S(2)}) collective-permute-start(bf16[72,1792]{1,0:T(8,128)(2,1)S(1)} %get-tuple-element.53), channel_id=1, source_target_pairs={{0,32},{32,0},{1,33},{33,1},{2,34},{34,2},{3,35},{35,3},{4,36},{36... | collective-permute-start | bytes 774152 | tf_op jit(solution)/shard_map/ppermute | solution.py:34
  259.9 13.0 %all-to-all-start.13 = ((bf16[8,72,256]{2,1,0:T(8,128)(2,1)}), bf16[8,72,256]{2,1,0:T(8,128)(2,1)S(1)}, u32[]{:S(2)}, u32[]{:S(2)}) async-start(bf16[8,72,256]{2,1,0:T(8,128)(2,1)} %bitcast.10), calls=%async_computation.13 | async-start | bytes 589824 | tf_op jit(solution)/shard_map/all_to_all | solution.py:30

commit v6 on v5

--- a/solution.py
+++ b/solution.py
@@ -13,7 +13,7 @@
 MIB = 1024 * 1024
 
 
-def call(body, out, *args, limit=32):
+def call(body, out, *args, limit=52):
     many = isinstance(out, list)
     shapes = [jax.ShapeDtypeStruct(s, d) for s, d in (out if many else [out])]
     got = pl.pallas_call(
@@ -253,24 +253,24 @@
 def on_device(acts, grads, basis_in, basis_out, eigen, sketch):
     lines = jnp.pad(acts.reshape(12, 1792), ((0, 4), (0, 0)))
     lines = lax.all_gather(lines, "core").reshape(32, 1792)
-    packed = call(pack_body, ((64, 3584), BF), lines, limit=62)
-    packed, own_grads, away_out = lax.optimization_barrier((packed, grads, basis_out))
-    own_grads = own_grads.reshape(24, 256)
-    own_grads, away_in = lax.optimization_barrier((own_grads, basis_in))
-    far_out, far_in = from_sibling(away_out), from_sibling(away_in)
+    packed = call(pack_body, ((64, 3584), BF), lines)
+    packed, own_grads = lax.optimization_barrier((packed, grads))
+    all_grads = lax.all_gather(own_grads.reshape(24, 256), ROW).reshape(384, 256)
     near = swap(packed.reshape(8, 8, 3584), "z").reshape(64, 3584)
-    near, own_grads, far_out, far_in = lax.optimization_barrier((near, own_grads, far_out, far_in))
-    dense = call(dense_body, ((4, 48, 3584), BF), near, limit=62)
-    all_grads = lax.all_gather(own_grads, ROW).reshape(384, 256)
+    near, all_grads, away = lax.optimization_barrier(
+        (near, all_grads, (basis_in, basis_out, eigen))
+    )
+    dense = call(dense_body, ((4, 48, 3584), BF), near)
+    far_in, far_out, far_eigen = [from_sibling(w) for w in away]
     g_part = call(
-        grad_body, ((2304, 128), BF), all_grads, sketch, basis_out, far_out, limit=62
+        grad_body, ((2304, 128), BF), all_grads, sketch, basis_out, far_out
     )
     both = swap(dense, "x").reshape(192, 3584)
-    both, g_part, away = lax.optimization_barrier((both, g_part, eigen))
+    both, g_part, far_in, far_eigen = lax.optimization_barrier((both, g_part, far_in, far_eigen))
     g_pieces = swap(g_part.reshape(32, 9, 8, 128), COL)
     a_part = call(act_body, ((192, 896), BF), both, basis_in, far_in)
-    a_part, g_pieces, far_eigen = lax.optimization_barrier((a_part, g_pieces, from_sibling(away)))
-    g_own = call(sum_flat_body, ((2304, 128), BF), g_pieces, limit=62)
+    a_part, g_pieces = lax.optimization_barrier((a_part, g_pieces))
+    g_own = call(sum_flat_body, ((2304, 128), BF), g_pieces)
     a_own = summed(a_part.reshape(8, 24, 896), "y")
     a_own, g_own = lax.optimization_barrier((a_own, g_own))
     g_rot = swap(g_own.reshape(32, 9, 8, 128), COL)

time: 285 us -> 286 us (level)
  local copies, waits for them, and re-layouts: 11.7 us -> 1.51 us
  Pallas kernels: 27.9 us -> 35.1 us
  starting transfers between devices: 54.7 us -> 58.7 us
    unnamed x25 -> x9, local copies, waits for them, and re-layouts: 10.2 us -> 0.68 us
    pallas_call x18, Pallas kernels: 27.9 us -> 35.1 us  [call(): pl.pallas_call(body, out_shape=shapes, in_specs=[pl.BlockSpec(memory_spac...]
    all_to_all x8, starting transfers between devices: 38.8 us -> 43.1 us  [swap(): return lax.all_to_all(x, axes, 0, 0, tiled=True)]
  transfers between devices with their start and end apart: 12 -> 12, of which waited for: 6 -> 6; matrix products, arithmetic and copies ran while one was open for 0% -> 0% of each run, Pallas kernels for 5% -> 6%
where the time goes in v6:
time: 286 us; the launch traced here: 285 us
  blocking collectives  144 us (50%)
  starting transfers between devices  58.7 us (21%)
  waiting for transfers between devices  44.4 us (16%)
  Pallas kernels  35.1 us (12%)
    all_to_all x6, blocking collectives, swap(): return lax.all_to_all(x, axes, 0, 0, tiled=True)  85.9 us
    all_to_all x8, starting transfers between devices, swap(): return lax.all_to_all(x, axes, 0, 0, tiled=True)  43.1 us
    all_to_all x8, waiting for transfers between devices, swap(): return lax.all_to_all(x, axes, 0, 0, tiled=True)  42.9 us
    pallas_call x18, Pallas kernels, call(): pl.pallas_call(body, out_shape=shapes, in_specs=[pl.BlockSpec(memory_spac...  35.1 us
    all_gather x1, blocking collectives, on_device(): a_rot = lax.all_gather(a_own, ROW).reshape(8, 2, 24, 896)  19.6 us
    all_gather x1, blocking collectives, on_device(): lax.all_gather(own_grads.reshape(24, 256), ROW).reshape(384, 256)  18.6 us
    ppermute x4, starting transfers between devices, from_sibling(): return lax.ppermute(x, 'core', [(0, 1), (1, 0)])  15.5 us
    all_gather x1, blocking collectives, on_device(): return (basis, lax.all_gather(mine, 'core'))  9.94 us
  transfers between devices with their start and end apart: 12, of which 6 were waited for; matrix products, arithmetic and copies ran while one was open for 0% of the time, Pallas kernels for 6%

profile of v6, /device:TPU:1, one launch (start us, length us, event | category | flops | bytes accessed | tf_op | source)
XLA Modules:
  0.0 284.8 jit_solution(9714012541135233699)
XLA Ops:
  0.6 0.0 copy-start.3
  0.6 0.8 reshape.43
  1.5 8.4 %all-gather.x_ref = bf16[32,1792]{1,0:T(8,128)(2,1)S(1)} all-gather(bf16[16,1792]{1,0:T(8,128)(2,1)S(1)} %pad.4), channel_id=2, replica_groups=mesh['y'=8,'core'=2,'z'=8,'x'=4] {'core'}, dimensions={0}, use_global_device_ids=true | all-gather | bytes 172032 | tf_op jit(solution)/shard_map/all_gather | solution.py:255
  9.9 0.9 shard_map.77
  10.8 4.7 %all-to-all-start = ((bf16[8,8,3584]{2,1,0:T(8,128)(2,1)}), bf16[8,8,3584]{2,1,0:T(8,128)(2,1)S(1)}, u32[]{:S(2)}, u32[]{:S(2)}) async-start(bf16[8,8,3584]{2,1,0:T(8,128)(2,1)} %bitcast), calls=%async_computation | async-start | bytes 917504 | tf_op jit(solution)/shard_map/all_to_all | solution.py:30
  15.5 0.0 copy-done.3
  15.5 18.6 %all_gather.29 = bf16[16,24,256]{2,1,0:T(8,128)(2,1)S(1)} all-gather(bf16[1,24,256]{2,1,0:T(8,128)(2,1)S(1)} %all_gather_reshape.3), channel_id=1, replica_groups=mesh['y'=8,'core'=2,'z'=8,'x'=4] {'y','core'}, dimensions={0}, use_global_device_ids=true | all-gather | bytes 208896 | tf_op jit(solution)/shard_map/all_gather | solution.py:258
  34.1 0.0 all-to-all-done
  34.1 0.0 copy-start.2
  34.1 0.0 copy-start
  34.1 0.0 copy-start.1
  34.1 2.2 collective-permute-start.1
  36.3 1.3 shard_map.78
  37.6 4.0 %all-to-all-start.1 = ((bf16[4,48,3584]{2,1,0:T(8,128)(2,1)}), bf16[4,48,3584]{2,1,0:T(8,128)(2,1)S(1)}, u32[]{:S(2)}, u32[]{:S(2)}) async-start(bf16[4,48,3584]{2,1,0:T(8,128)(2,1)} %shard_map.78), calls=%async_computation.1 | async-start | bytes 2752512 | tf_op jit(solution)/shard_map/all_to_all | solution.py:30
  41.6 0.0 copy-done.2
  41.6 2.5 collective-permute-start.2
  44.2 0.0 copy-done
  44.2 1.9 collective-permute-start
  46.1 1.5 collective-permute-done.v_ref
  47.6 0.0 copy-done.1
  47.6 1.4 shard_map.79
  49.0 0.0 collective-permute-done.2.f_ref
  49.0 10.7 %all-to-all-done.1 = bf16[4,48,3584]{2,1,0:T(8,128)(2,1)S(1)} async-done(((bf16[4,48,3584]{2,1,0:T(8,128)(2,1)}), bf16[4,48,3584]{2,1,0:T(8,128)(2,1)S(1)}, u32[]{:S(2)}, u32[]{:S(2)}) %all-to-all-start.1) | async-done | bytes 1376288 | tf_op jit(solution)/shard_map/all_to_all | solution.py:30
  59.7 0.0 collective-permute-done.1.v_ref
  59.7 7.9 %all-to-all-start.2 = ((bf16[32,9,8,128]{3,2,1,0:T(8,128)(2,1)}), bf16[32,9,8,128]{3,2,1,0:T(8,128)(2,1)S(1)}, u32[]{:S(2)}, u32[]{:S(2)}) async-start(bf16[32,9,8,128]{3,2,1,0:T(8,128)(2,1)} %bitcast.4), calls=%async_computation.2 | async-start | bytes 1179648 | tf_op jit(solution)/shard_map/all_to_all | solution.py:30
  67.6 5.2 %shard_map.80 = bf16[192,896]{1,0:T(8,128)(2,1)} custom-call(bf16[192,3584]{1,0:T(8,128)(2,1)S(1)} %bitcast.13, bf16[1792,896]{1,0:T(8,128)(2,1)} %w_ref.8, bf16[1792,896]{1,0:T(8,128)(2,1)} %collective-permute-done.1.v_ref), custom_call_target="tpu_custom_call" | custom-call | tf_op jit(solution)/shard_map/pallas_call | solution.py:19
  72.9 11.2 %all-to-all-done.2.x_ref = bf16[32,9,8,128]{3,2,1,0:T(8,128)(2,1)S(1)} async-done(((bf16[32,9,8,128]{3,2,1,0:T(8,128)(2,1)}), bf16[32,9,8,128]{3,2,1,0:T(8,128)(2,1)S(1)}, u32[]{:S(2)}, u32[]{:S(2)}) %all-to-all-start.2) | async-done | bytes 589856 | tf_op jit(solution)/shard_map/all_to_all | solution.py:30
  84.1 4.0 %all-to-all-start.3 = ((bf16[8,24,896]{2,1,0:T(8,128)(2,1)}), bf16[8,24,896]{2,1,0:T(8,128)(2,1)S(1)}, u32[]{:S(2)}, u32[]{:S(2)}) async-start(bf16[8,24,896]{2,1,0:T(8,128)(2,1)} %bitcast.5), calls=%async_computation.3 | async-start | bytes 688128 | tf_op jit(solution)/shard_map/all_to_all | solution.py:30
  88.1 0.9 shard_map.82
  89.0 9.4 %all-to-all-done.3.x_ref = bf16[8,24,896]{2,1,0:T(8,128)(2,1)S(1)} async-done(((bf16[8,24,896]{2,1,0:T(8,128)(2,1)}), bf16[8,24,896]{2,1,0:T(8,128)(2,1)S(1)}, u32[]{:S(2)}, u32[]{:S(2)}) %all-to-all-start.3) | async-done | bytes 344096 | tf_op jit(solution)/shard_map/all_to_all | solution.py:30
  98.5 7.7 %all-to-all-start.4 = ((bf16[32,9,8,128]{3,2,1,0:T(8,128)(2,1)}), bf16[32,9,8,128]{3,2,1,0:T(8,128)(2,1)S(1)}, u32[]{:S(2)}, u32[]{:S(2)}) async-start(bf16[32,9,8,128]{3,2,1,0:T(8,128)(2,1)} %bitcast.7), calls=%async_computation.4 | async-start | bytes 1179648 | tf_op jit(solution)/shard_map/all_to_all | solution.py:30
  106.2 19.6 %all-gather.1 = bf16[384,896]{1,0:T(8,128)(2,1)S(1)} all-gather(bf16[24,896]{1,0:T(8,128)(2,1)S(1)} %shard_map.81), channel_id=3, replica_groups=mesh['y'=8,'core'=2,'z'=8,'x'=4] {'y','core'}, dimensions={0}, use_global_device_ids=true | all-gather | bytes 731136 | tf_op jit(solution)/shard_map/all_gather | solution.py:277
  125.8 0.0 all-to-all-done.4.g_ref
  125.8 3.5 %shard_map.83 = (bf16[896,1024]{1,0:T(8,128)(2,1)}, bf16[8,8,8,128]{3,2,1,0:T(8,128)(2,1)S(1)}) custom-call(bf16[8,2,24,896]{3,2,1,0:T(8,128)(2,1)S(1)} %bitcast.14, bf16[32,9,8,128]{3,2,1,0:T(8,128)(2,1)S(1)} %all-to-all-done.4.g_ref, bf16[896,512]{1,0:T(8,128)(2,1)} %e_ref.1, bf16[896,512]{1,0:T(8,128)(2,1)} %collective-permute-done.2.f_ref), custom_call_target="tpu_custom_call" | custom-call | tf_op jit(solution)/shard_map/pallas_call | solution.py:19
  129.3 11.5 %all_to_all.70.x_ref = bf16[8,8,8,128]{3,2,1,0:T(8,128)(2,1)S(1)} all-to-all(bf16[8,8,8,128]{3,2,1,0:T(8,128)(2,1)S(1)} %get-tuple-element.43), channel_id=1, replica_groups=mesh['y'=8,'core'=2,'z'=8,'x'=4] {'y'}, dimensions={0} | all-to-all | bytes 262144 | tf_op jit(solution)/shard_map/all_to_all | solution.py:30
  140.9 10.3 %all_to_all.71.r_ref = bf16[8,8,8,128]{3,2,1,0:T(8,128)(2,1)S(1)} all-to-all(bf16[8,8,8,128]{3,2,1,0:T(8,128)(2,1)S(1)} %shard_map.84), channel_id=1, replica_groups=mesh['y'=8,'core'=2,'z'=8,'x'=4] {'y'}, dimensions={0} | all-to-all | bytes 262144 | tf_op jit(solution)/shard_map/all_to_all | solution.py:30
  151.2 4.9 %shard_map.85 = bf16[32,8,8,128]{3,2,1,0:T(8,128)(2,1)S(1)} custom-call(bf16[8,8,8,128]{3,2,1,0:T(8,128)(2,1)S(1)} %all_to_all.71.r_ref, bf16[1792,896]{1,0:T(8,128)(2,1)} %w_ref.8, bf16[1792,896]{1,0:T(8,128)(2,1)} %collective-permute-done.1.v_ref), custom_call_target="tpu_custom_call" | custom-call | tf_op jit(solution)/shard_map/pallas_call | solution.py:19
  156.1 22.7 %all_to_all.72.x_ref = bf16[32,8,8,128]{3,2,1,0:T(8,128)(2,1)S(1)} all-to-all(bf16[32,8,8,128]{3,2,1,0:T(8,128)(2,1)S(1)} %shard_map.85), channel_id=1, replica_groups=mesh['y'=8,'core'=2,'z'=8,'x'=4] {'z','x'}, dimensions={0} | all-to-all | bytes 1048576 | tf_op jit(solution)/shard_map/all_to_all | solution.py:30
  178.9 0.1 shard_map.86
  179.0 18.9 %all_to_all.73.r_ref = bf16[32,8,8,128]{3,2,1,0:T(8,128)(2,1)S(1)} all-to-all(bf16[32,8,8,128]{3,2,1,0:T(8,128)(2,1)S(1)} %shard_map.86), channel_id=1, replica_groups=mesh['y'=8,'core'=2,'z'=8,'x'=4] {'z','x'}, dimensions={0} | all-to-all | bytes 1048576 | tf_op jit(solution)/shard_map/all_to_all | solution.py:30
  197.9 4.2 %shard_map.87 = (bf16[8,12,8,128]{3,2,1,0:T(8,128)(2,1)S(1)}, bf16[72,1792]{1,0:T(8,128)(2,1)S(1)}, bf16[72,1792]{1,0:T(8,128)(2,1)S(1)}) custom-call(bf16[32,8,8,128]{3,2,1,0:T(8,128)(2,1)S(1)} %all_to_all.73.r_ref, bf16[1792,896]{1,0:T(8,128)(2,1)} %w_ref.8, bf16[1792,896]{1,0:T(8,128)(2,1)} %collective-permute-done.1.v_ref), custom_call_target="tpu_custom_call" | custom-call | tf_op jit(solution)/shard_map/pallas_call | solution.py:19
  202.1 11.3 %all_to_all.74.x_ref = bf16[8,12,8,128]{3,2,1,0:T(8,128)(2,1)S(1)} all-to-all(bf16[8,12,8,128]{3,2,1,0:T(8,128)(2,1)S(1)} %get-tuple-element.44), channel_id=1, replica_groups=mesh['y'=8,'core'=2,'z'=8,'x'=4] {'y'}, dimensions={0} | all-to-all | bytes 393216 | tf_op jit(solution)/shard_map/all_to_all | solution.py:30
  213.5 11.0 %all_to_all.75.m_ref = bf16[8,12,8,128]{3,2,1,0:T(8,128)(2,1)S(1)} all-to-all(bf16[8,12,8,128]{3,2,1,0:T(8,128)(2,1)S(1)} %shard_map.88), channel_id=1, replica_groups=mesh['y'=8,'core'=2,'z'=8,'x'=4] {'y'}, dimensions={0} | all-to-all | bytes 393216 | tf_op jit(solution)/shard_map/all_to_all | solution.py:30
  224.5 2.6 shard_map.89
  227.2 6.1 %all-to-all-start.11 = ((bf16[32,3,8,128]{3,2,1,0:T(8,128)(2,1)}), bf16[32,3,8,128]{3,2,1,0:T(8,128)(2,1)S(1)}, u32[]{:S(2)}, u32[]{:S(2)}) async-start(bf16[32,3,8,128]{3,2,1,0:T(8,128)(2,1)} %bitcast.8), calls=%async_computation.11 | async-start | bytes 393216 | tf_op jit(solution)/shard_map/all_to_all | solution.py:30
  233.2 6.0 %shard_map.90.w_ref = f32[72,128]{1,0:T(8,128)S(1)} custom-call(bf16[8,12,8,128]{3,2,1,0:T(8,128)(2,1)S(1)} %all_to_all.75.m_ref), custom_call_target="tpu_custom_call" | custom-call | tf_op jit(solution)/shard_map/pallas_call | solution.py:19
  239.2 3.9 %all-to-all-done.11.x_ref = bf16[32,3,8,128]{3,2,1,0:T(8,128)(2,1)S(1)} async-done(((bf16[32,3,8,128]{3,2,1,0:T(8,128)(2,1)}), bf16[32,3,8,128]{3,2,1,0:T(8,128)(2,1)S(1)}, u32[]{:S(2)}, u32[]{:S(2)}) %all-to-all-start.11) | async-done | bytes 196640 | tf_op jit(solution)/shard_map/all_to_all | solution.py:30
  243.1 0.7 shard_map.91
  243.8 5.3 %all-to-all-start.12 = ((bf16[32,3,8,128]{3,2,1,0:T(8,128)(2,1)}), bf16[32,3,8,128]{3,2,1,0:T(8,128)(2,1)S(1)}, u32[]{:S(2)}, u32[]{:S(2)}) async-start(bf16[32,3,8,128]{3,2,1,0:T(8,128)(2,1)} %bitcast.9), calls=%async_computation.12 | async-start | bytes 393216 | tf_op jit(solution)/shard_map/all_to_all | solution.py:30
  249.2 8.9 %collective-permute-start.3 = (bf16[72,1792]{1,0:T(8,128)(2,1)S(1)}, bf16[72,1792]{1,0:T(8,128)(2,1)S(1)}, u32[]{:S(2)}, u32[]{:S(2)}) collective-permute-start(bf16[72,1792]{1,0:T(8,128)(2,1)S(1)} %get-tuple-element.49), channel_id=1, source_target_pairs={{0,32},{32,0},{1,33},{33,1},{2,34},{34,2},{3,35},{35,3},{4,36},{36... | collective-permute-start | bytes 774152 | tf_op jit(solution)/shard_map/ppermute | solution.py:34
  258.0 1.9 all-gather.2
  259.9 0.0 collective-permute-done.3.got_ref
  259.9 0.0 all-to-all-done.12.c_ref
  259.9 1.0 shard_map.93
  260.9 3.4 %all-to-all-start.13 = ((bf16[8,72,256]{2,1,0:T(8,128)(2,1)}), bf16[8,72,256]{2,1,0:T(8,128)(2,1)S(1)}, u32[]{:S(2)}, u32[]{:S(2)}) async-start(bf16[8,72,256]{2,1,0:T(8,128)(2,1)} %bitcast.11), calls=%async_computation.13 | async-start | bytes 589824 | tf_op jit(solution)/shard_map/all_to_all | solution.py:30
  264.3 1.9 shard_map.92
  266.3 7.7 %all-to-all-done.13.p_ref = bf16[8,72,256]{2,1,0:T(8,128)(2,1)S(1)} async-done(((bf16[8,72,256]{2,1,0:T(8,128)(2,1)}), bf16[8,72,256]{2,1,0:T(8,128)(2,1)S(1)}, u32[]{:S(2)}, u32[]{:S(2)}) %all-to-all-start.13) | async-done | bytes 294944 | tf_op jit(solution)/shard_map/all_to_all | solution.py:30
  273.9 0.2 shard_map.94
  274.2 9.9 %all-gather.3 = f32[144,256]{1,0:T(8,128)S(1)} all-gather(f32[72,256]{1,0:T(8,128)S(1)} %shard_map.94), channel_id=5, replica_groups=mesh['y'=8,'core'=2,'z'=8,'x'=4] {'core'}, dimensions={0}, use_global_device_ids=true | all-gather | bytes 221184 | tf_op jit(solution)/shard_map/all_gather | solution.py:302
  284.1 0.7 copy.9
  (5 shorter events, 0.1 us)
Async XLA Ops:
  0.6 14.9 %copy-start.3 = (bf16[12,2,256]{2,1,0:T(2,128)(2,1)S(1)}, bf16[12,2,256]{2,1,0:T(2,128)(2,1)}, u32[]{:S(2)}) copy-start(bf16[12,2,256]{2,1,0:T(2,128)(2,1)} %param.7) | copy-start | bytes 36868
  10.8 23.3 %all-to-all-start = ((bf16[8,8,3584]{2,1,0:T(8,128)(2,1)}), bf16[8,8,3584]{2,1,0:T(8,128)(2,1)S(1)}, u32[]{:S(2)}, u32[]{:S(2)}) async-start(bf16[8,8,3584]{2,1,0:T(8,128)(2,1)} %bitcast), calls=%async_computation | async-start | bytes 917504 | tf_op jit(solution)/shard_map/all_to_all | solution.py:30
  34.1 7.6 %copy-start.2 = (bf16[896,512]{1,0:T(8,128)(2,1)S(1)}, bf16[896,512]{1,0:T(8,128)(2,1)}, u32[]{:S(2)}) copy-start(bf16[896,512]{1,0:T(8,128)(2,1)} %e_ref.1) | copy-start | bytes 2752516
  34.1 10.1 %copy-start = (bf16[256,512]{1,0:T(8,128)(2,1)S(1)}, bf16[256,512]{1,0:T(8,128)(2,1)}, u32[]{:S(2)}) copy-start(bf16[256,512]{1,0:T(8,128)(2,1)} %w_ref.9) | copy-start | bytes 786436
  34.1 13.5 %copy-start.1 = (bf16[72,256]{1,0:T(8,128)(2,1)S(1)}, bf16[72,256]{1,0:T(8,128)(2,1)}, u32[]{:S(2)}) copy-start(bf16[72,256]{1,0:T(8,128)(2,1)} %s_ref.1) | copy-start | bytes 110596
  34.1 25.6 %collective-permute-start.1 = (bf16[1792,896]{1,0:T(8,128)(2,1)}, bf16[1792,896]{1,0:T(8,128)(2,1)}, u32[]{:S(2)}, u32[]{:S(2)}) collective-permute-start(bf16[1792,896]{1,0:T(8,128)(2,1)} %w_ref.8), channel_id=1, source_target_pairs={{0,32},{32,0},{1,33},{33,1},{2,34},{34,2},{3,35},{35,3},{4,36},{36... | collective-permute-start | bytes 9633800 | tf_op jit(solution)/shard_map/ppermute | solution.py:34
  37.6 22.1 %all-to-all-start.1 = ((bf16[4,48,3584]{2,1,0:T(8,128)(2,1)}), bf16[4,48,3584]{2,1,0:T(8,128)(2,1)S(1)}, u32[]{:S(2)}, u32[]{:S(2)}) async-start(bf16[4,48,3584]{2,1,0:T(8,128)(2,1)} %shard_map.78), calls=%async_computation.1 | async-start | bytes 2752512 | tf_op jit(solution)/shard_map/all_to_all | solution.py:30
  41.6 7.3 %collective-permute-start.2 = (bf16[896,512]{1,0:T(8,128)(2,1)S(1)}, bf16[896,512]{1,0:T(8,128)(2,1)}, u32[]{:S(2)}, u32[]{:S(2)}) collective-permute-start(bf16[896,512]{1,0:T(8,128)(2,1)S(1)} %copy-done.2), channel_id=1, source_target_pairs={{0,32},{32,0},{1,33},{33,1},{2,34},{34,2},{3,35},{35,3},{4,36},{36... | collective-permute-start | bytes 2752520 | tf_op jit(solution)/shard_map/ppermute | solution.py:34
  44.2 3.4 %collective-permute-start = (bf16[256,512]{1,0:T(8,128)(2,1)S(1)}, bf16[256,512]{1,0:T(8,128)(2,1)S(1)}, u32[]{:S(2)}, u32[]{:S(2)}) collective-permute-start(bf16[256,512]{1,0:T(8,128)(2,1)S(1)} %copy-done), channel_id=1, source_target_pairs={{0,32},{32,0},{1,33},{33,1},{2,34},{34,2},{3,35},{35,3},{4,36},{36... | collective-permute-start | bytes 786440 | tf_op jit(solution)/shard_map/ppermute | solution.py:34
  59.7 24.3 %all-to-all-start.2 = ((bf16[32,9,8,128]{3,2,1,0:T(8,128)(2,1)}), bf16[32,9,8,128]{3,2,1,0:T(8,128)(2,1)S(1)}, u32[]{:S(2)}, u32[]{:S(2)}) async-start(bf16[32,9,8,128]{3,2,1,0:T(8,128)(2,1)} %bitcast.4), calls=%async_computation.2 | async-start | bytes 1179648 | tf_op jit(solution)/shard_map/all_to_all | solution.py:30
  84.1 14.4 %all-to-all-start.3 = ((bf16[8,24,896]{2,1,0:T(8,128)(2,1)}), bf16[8,24,896]{2,1,0:T(8,128)(2,1)S(1)}, u32[]{:S(2)}, u32[]{:S(2)}) async-start(bf16[8,24,896]{2,1,0:T(8,128)(2,1)} %bitcast.5), calls=%async_computation.3 | async-start | bytes 688128 | tf_op jit(solution)/shard_map/all_to_all | solution.py:30
  98.5 27.3 %all-to-all-start.4 = ((bf16[32,9,8,128]{3,2,1,0:T(8,128)(2,1)}), bf16[32,9,8,128]{3,2,1,0:T(8,128)(2,1)S(1)}, u32[]{:S(2)}, u32[]{:S(2)}) async-start(bf16[32,9,8,128]{3,2,1,0:T(8,128)(2,1)} %bitcast.7), calls=%async_computation.4 | async-start | bytes 1179648 | tf_op jit(solution)/shard_map/all_to_all | solution.py:30
  227.2 15.9 %all-to-all-start.11 = ((bf16[32,3,8,128]{3,2,1,0:T(8,128)(2,1)}), bf16[32,3,8,128]{3,2,1,0:T(8,128)(2,1)S(1)}, u32[]{:S(2)}, u32[]{:S(2)}) async-start(bf16[32,3,8,128]{3,2,1,0:T(8,128)(2,1)} %bitcast.8), calls=%async_computation.11 | async-start | bytes 393216 | tf_op jit(solution)/shard_map/all_to_all | solution.py:30
  243.8 16.1 %all-to-all-start.12 = ((bf16[32,3,8,128]{3,2,1,0:T(8,128)(2,1)}), bf16[32,3,8,128]{3,2,1,0:T(8,128)(2,1)S(1)}, u32[]{:S(2)}, u32[]{:S(2)}) async-start(bf16[32,3,8,128]{3,2,1,0:T(8,128)(2,1)} %bitcast.9), calls=%async_computation.12 | async-start | bytes 393216 | tf_op jit(solution)/shard_map/all_to_all | solution.py:30
  249.2 10.8 %collective-permute-start.3 = (bf16[72,1792]{1,0:T(8,128)(2,1)S(1)}, bf16[72,1792]{1,0:T(8,128)(2,1)S(1)}, u32[]{:S(2)}, u32[]{:S(2)}) collective-permute-start(bf16[72,1792]{1,0:T(8,128)(2,1)S(1)} %get-tuple-element.49), channel_id=1, source_target_pairs={{0,32},{32,0},{1,33},{33,1},{2,34},{34,2},{3,35},{35,3},{4,36},{36... | collective-permute-start | bytes 774152 | tf_op jit(solution)/shard_map/ppermute | solution.py:34
  260.9 13.0 %all-to-all-start.13 = ((bf16[8,72,256]{2,1,0:T(8,128)(2,1)}), bf16[8,72,256]{2,1,0:T(8,128)(2,1)S(1)}, u32[]{:S(2)}, u32[]{:S(2)}) async-start(bf16[8,72,256]{2,1,0:T(8,128)(2,1)} %bitcast.11), calls=%async_computation.13 | async-start | bytes 589824 | tf_op jit(solution)/shard_map/all_to_all | solution.py:30

commit v7 on v6

--- a/solution.py
+++ b/solution.py
@@ -13,14 +13,36 @@
 MIB = 1024 * 1024
 
 
-def call(body, out, *args, limit=52):
+class Late:
+    def __init__(self, source, buffer, semaphore):
+        self.copy = pltpu.make_async_copy(source, buffer, semaphore)
+        self.copy.start()
+        self.buffer, self.shape = buffer, buffer.shape
+
+    def get(self):
+        self.copy.wait()
+        return self.buffer[...]
+
+
+def call(body, out, *args, late=(), limit=32):
     many = isinstance(out, list)
     shapes = [jax.ShapeDtypeStruct(s, d) for s, d in (out if many else [out])]
+    n, m = len(args), len(shapes)
+    whole, away = pl.BlockSpec(memory_space=pltpu.VMEM), pl.BlockSpec(memory_space=pltpu.HBM)
+    buffers = [pltpu.VMEM(args[i].shape, args[i].dtype) for i in late]
+
+    def run(*refs):
+        given, held = list(refs[:n]), refs[n + m :]
+        for k, i in enumerate(late):
+            given[i] = Late(given[i], held[k], held[-1].at[k])
+        body(*given, *refs[n : n + m])
+
     got = pl.pallas_call(
-        body,
+        run if late else body,
         out_shape=shapes,
-        in_specs=[pl.BlockSpec(memory_space=pltpu.VMEM)] * len(args),
-        out_specs=[pl.BlockSpec(memory_space=pltpu.VMEM)] * len(shapes),
+        in_specs=[away if i in late else whole for i in range(n)],
+        out_specs=[whole] * m,
+        scratch_shapes=buffers + [pltpu.SemaphoreType.DMA((len(late),))] if late else (),
         compiler_params=pltpu.CompilerParams(vmem_limit_bytes=limit * MIB),
     )(*args)
     return got if many else got[0]
@@ -162,7 +184,7 @@
 
 def range_body(r_ref, w_ref, v_ref, out_ref):
     r = from_tiles(r_ref, 7).astype(BF)
-    both = [dot(r, w_ref[...], 1, 1), dot(r, v_ref[...], 1, 1)]
+    both = [dot(r, w_ref[...], 1, 1), dot(r, v_ref.get(), 1, 1)]
     to_tiles(jnp.concatenate(both, axis=1), out_ref)
 
 
@@ -182,7 +204,7 @@
     n = w_ref.shape[0]
     keep_ref[...] = r[:, :n]
     give_ref[...] = r[:, n:]
-    to_tiles(dot(r[:, :n], w_ref[...]) + dot(r[:, n:], v_ref[...]), out_ref, 9)
+    to_tiles(dot(r[:, :n], w_ref[...]) + dot(r[:, n:], v_ref.get()), out_ref, 9)
     gram = jnp.concatenate([dot(r, r, 1, 1), jnp.zeros((72, 56), F32)], axis=1)
     for g in range(9):
         p, s = gram_at(g)
@@ -253,17 +275,17 @@
 def on_device(acts, grads, basis_in, basis_out, eigen, sketch):
     lines = jnp.pad(acts.reshape(12, 1792), ((0, 4), (0, 0)))
     lines = lax.all_gather(lines, "core").reshape(32, 1792)
-    packed = call(pack_body, ((64, 3584), BF), lines)
+    packed = call(pack_body, ((64, 3584), BF), lines, limit=62)
     packed, own_grads = lax.optimization_barrier((packed, grads))
     all_grads = lax.all_gather(own_grads.reshape(24, 256), ROW).reshape(384, 256)
     near = swap(packed.reshape(8, 8, 3584), "z").reshape(64, 3584)
     near, all_grads, away = lax.optimization_barrier(
         (near, all_grads, (basis_in, basis_out, eigen))
     )
-    dense = call(dense_body, ((4, 48, 3584), BF), near)
+    dense = call(dense_body, ((4, 48, 3584), BF), near, limit=62)
     far_in, far_out, far_eigen = [from_sibling(w) for w in away]
     g_part = call(
-        grad_body, ((2304, 128), BF), all_grads, sketch, basis_out, far_out
+        grad_body, ((2304, 128), BF), all_grads, sketch, basis_out, far_out, limit=62
     )
     both = swap(dense, "x").reshape(192, 3584)
     both, g_part, far_in, far_eigen = lax.optimization_barrier((both, g_part, far_in, far_eigen))
@@ -280,22 +302,21 @@
         a_rot, g_rot, eigen, far_eigen,
     )
     reduced = sum_over(red, "y")
-    span = call(range_body, ((32, 8, 8, 128), BF), reduced, basis_in, far_in)
+    span = call(range_body, ((32, 8, 8, 128), BF), reduced, basis_in, far_in, late=(2,))
     span = sum_over(span, COL)
     mapped, keep, give = call(
         mapped_body,
         [((8, 12, 8, 128), BF), ((72, 1792), BF), ((72, 1792), BF)],
-        span, basis_in, far_in,
+        span, basis_in, far_in, late=(2,),
     )
     mapped = swap(call(gram_sum_body, ((8, 12, 8, 128), BF), swap(mapped, "y")), "y")
     core = call(core_body, ((768, 128), BF), mapped, scaled)
     core = swap(core.reshape(32, 3, 8, 128), COL)
     inverse = call(inverse_body, ((72, 128), F32), mapped)
-    core, inverse, give = lax.optimization_barrier((core, inverse, give))
-    core = call(sum_flat_body, ((768, 128), BF), core)
-    core = swap(core.reshape(32, 3, 8, 128), COL)
-    both_inverses = lax.all_gather(inverse, "core")
-    core, both_inverses, got = lax.optimization_barrier((core, both_inverses, from_sibling(give)))
+    core, inverse, got = lax.optimization_barrier((core, inverse, from_sibling(give)))
+    core = swap(call(sum_flat_body, ((768, 128), BF), core).reshape(32, 3, 8, 128), COL)
+    core, given = lax.optimization_barrier((core, inverse))
+    both_inverses = lax.all_gather(given, "core")
     part = call(project_body, ((576, 256), BF), core, basis_out, far_out)
     basis = call(basis_body, ((2, 72, 1792), F32), both_inverses, keep, got)
     mine = call(final_body, ((72, 256), F32), inverse, swap(part.reshape(8, 72, 256), "y"))

time: 286 us -> 289 us (1.010)
  blocking collectives: 144 us -> 163 us
  waiting for transfers between devices: 44.4 us -> 34.6 us
  starting transfers between devices: 58.7 us -> 52.9 us
    all_to_all x6 -> x7, blocking collectives: 85.9 us -> 106 us  [swap(): return lax.all_to_all(x, axes, 0, 0, tiled=True)]
    all_to_all x8 -> x7, waiting for transfers between devices: 42.9 us -> 33.1 us  [swap(): return lax.all_to_all(x, axes, 0, 0, tiled=True)]
    all_to_all x8 -> x7, starting transfers between devices: 43.1 us -> 37.8 us  [swap(): return lax.all_to_all(x, axes, 0, 0, tiled=True)]
    all_gather x1, blocking collectives: 9.94 us -> 5.11 us  [on_device(): return (basis, lax.all_gather(mine, 'core'))]
  transfers between devices with their start and end apart: 12 -> 11, of which waited for: 6 -> 5; matrix products, arithmetic and copies ran while one was open for 0% -> 0% of each run, Pallas kernels for 6% -> 6%
where the time goes in v7:
time: 289 us; the launch traced here: 287 us
  blocking collectives  163 us (56%)
  starting transfers between devices  52.9 us (18%)
  waiting for transfers between devices  34.6 us (12%)
  Pallas kernels  32.3 us (11%)
  local copies, waits for them, and re-layouts  4.13 us (1%)
    all_to_all x7, blocking collectives, swap(): return lax.all_to_all(x, axes, 0, 0, tiled=True)  106 us
    all_to_all x7, starting transfers between devices, swap(): return lax.all_to_all(x, axes, 0, 0, tiled=True)  37.8 us
    all_to_all x7, waiting for transfers between devices, swap(): return lax.all_to_all(x, axes, 0, 0, tiled=True)  33.1 us
    pallas_call x18, Pallas kernels, call(): pl.pallas_call(run if late else body, out_shape=shapes, in_specs=[away if...  32.3 us
    all_gather x1, blocking collectives, on_device(): lax.all_gather(own_grads.reshape(24, 256), ROW).reshape(384, 256)  20 us
    all_gather x1, blocking collectives, on_device(): a_rot = lax.all_gather(a_own, ROW).reshape(8, 2, 24, 896)  19.6 us
    ppermute x4, starting transfers between devices, from_sibling(): return lax.ppermute(x, 'core', [(0, 1), (1, 0)])  15.1 us
    all_gather x1, blocking collectives, on_device(): lines = lax.all_gather(lines, 'core').reshape(32, 1792)  8.55 us
  transfers between devices with their start and end apart: 11, of which 5 were waited for; matrix products, arithmetic and copies ran while one was open for 0% of the time, Pallas kernels for 6%

profile of v7, /device:TPU:1, one launch (start us, length us, event | category | flops | bytes accessed | tf_op | source)
XLA Modules:
  0.0 287.5 jit_solution(14548766100110726711)
XLA Ops:
  0.6 0.0 copy-start.8
  0.6 0.8 reshape.43
  1.5 8.5 %all-gather.x_ref = bf16[32,1792]{1,0:T(8,128)(2,1)} all-gather(bf16[16,1792]{1,0:T(8,128)(2,1)S(1)} %pad.4), channel_id=2, replica_groups=mesh['y'=8,'core'=2,'z'=8,'x'=4] {'core'}, dimensions={0}, use_global_device_ids=true | all-gather | bytes 172032 | tf_op jit(solution)/shard_map/all_gather | solution.py:277
  10.0 1.8 shard_map.77
  11.9 4.7 %all-to-all-start = ((bf16[8,8,3584]{2,1,0:T(8,128)(2,1)}), bf16[8,8,3584]{2,1,0:T(8,128)(2,1)S(1)}, u32[]{:S(2)}, u32[]{:S(2)}) async-start(bf16[8,8,3584]{2,1,0:T(8,128)(2,1)} %bitcast.19), calls=%async_computation | async-start | bytes 917504 | tf_op jit(solution)/shard_map/all_to_all | solution.py:52
  16.5 0.0 copy-done.8
  16.5 20.0 %all_gather.29 = bf16[16,24,256]{2,1,0:T(8,128)(2,1)} all-gather(bf16[1,24,256]{2,1,0:T(8,128)(2,1)S(1)} %all_gather_reshape.3), channel_id=1, replica_groups=mesh['y'=8,'core'=2,'z'=8,'x'=4] {'y','core'}, dimensions={0}, use_global_device_ids=true | all-gather | bytes 208896 | tf_op jit(solution)/shard_map/all_gather | solution.py:280
  36.5 0.0 all-to-all-done
  36.5 0.0 copy-start.7
  36.5 0.0 copy-start.2
  36.5 2.2 collective-permute-start.1
  38.7 0.0 copy-done.7
  38.7 2.3 shard_map.78
  41.1 4.0 %all-to-all-start.1 = ((bf16[4,48,3584]{2,1,0:T(8,128)(2,1)}), bf16[4,48,3584]{2,1,0:T(8,128)(2,1)S(1)}, u32[]{:S(2)}, u32[]{:S(2)}) async-start(bf16[4,48,3584]{2,1,0:T(8,128)(2,1)} %shard_map.78), calls=%async_computation.1 | async-start | bytes 2752512 | tf_op jit(solution)/shard_map/all_to_all | solution.py:52
  45.1 2.5 collective-permute-start.2
  47.6 0.0 copy-done.2
  47.6 1.9 collective-permute-start
  49.6 1.5 collective-permute-done.v_ref
  51.1 0.0 copy-start.4
  51.1 0.7 copy-done.4
  51.8 2.5 shard_map.79
  54.3 0.0 collective-permute-done.2.f_ref
  54.3 8.9 %all-to-all-done.1 = bf16[4,48,3584]{2,1,0:T(8,128)(2,1)S(1)} async-done(((bf16[4,48,3584]{2,1,0:T(8,128)(2,1)}), bf16[4,48,3584]{2,1,0:T(8,128)(2,1)S(1)}, u32[]{:S(2)}, u32[]{:S(2)}) %all-to-all-start.1) | async-done | bytes 1376288 | tf_op jit(solution)/shard_map/all_to_all | solution.py:52
  63.2 0.0 collective-permute-done.1.v_ref.refs_2_
  63.2 7.9 %all-to-all-start.2 = ((bf16[32,9,8,128]{3,2,1,0:T(8,128)(2,1)}), bf16[32,9,8,128]{3,2,1,0:T(8,128)(2,1)S(1)}, u32[]{:S(2)}, u32[]{:S(2)}) async-start(bf16[32,9,8,128]{3,2,1,0:T(8,128)(2,1)} %bitcast.17), calls=%async_computation.2 | async-start | bytes 1179648 | tf_op jit(solution)/shard_map/all_to_all | solution.py:52
  71.1 0.0 copy-start
  71.1 1.9 copy-done
  73.0 4.2 %shard_map.80 = bf16[192,896]{1,0:T(8,128)(2,1)} custom-call(bf16[192,3584]{1,0:T(8,128)(2,1)S(1)} %bitcast.13, bf16[1792,896]{1,0:T(8,128)(2,1)S(1)} %copy-done, bf16[1792,896]{1,0:T(8,128)(2,1)} %collective-permute-done.1.v_ref.refs_2_), custom_call_target="tpu_custom_call" | custom-call | tf_op jit(solution)/shard_map/pallas_call | solution.py:40
  77.2 10.3 %all-to-all-done.2.x_ref = bf16[32,9,8,128]{3,2,1,0:T(8,128)(2,1)S(1)} async-done(((bf16[32,9,8,128]{3,2,1,0:T(8,128)(2,1)}), bf16[32,9,8,128]{3,2,1,0:T(8,128)(2,1)S(1)}, u32[]{:S(2)}, u32[]{:S(2)}) %all-to-all-start.2) | async-done | bytes 589856 | tf_op jit(solution)/shard_map/all_to_all | solution.py:52
  87.5 4.0 %all-to-all-start.3 = ((bf16[8,24,896]{2,1,0:T(8,128)(2,1)}), bf16[8,24,896]{2,1,0:T(8,128)(2,1)S(1)}, u32[]{:S(2)}, u32[]{:S(2)}) async-start(bf16[8,24,896]{2,1,0:T(8,128)(2,1)} %bitcast.5), calls=%async_computation.3 | async-start | bytes 688128 | tf_op jit(solution)/shard_map/all_to_all | solution.py:52
  91.5 0.9 shard_map.82
  92.5 9.4 %all-to-all-done.3.x_ref = bf16[8,24,896]{2,1,0:T(8,128)(2,1)S(1)} async-done(((bf16[8,24,896]{2,1,0:T(8,128)(2,1)}), bf16[8,24,896]{2,1,0:T(8,128)(2,1)S(1)}, u32[]{:S(2)}, u32[]{:S(2)}) %all-to-all-start.3) | async-done | bytes 344096 | tf_op jit(solution)/shard_map/all_to_all | solution.py:52
  101.9 7.7 %all-to-all-start.4 = ((bf16[32,9,8,128]{3,2,1,0:T(8,128)(2,1)}), bf16[32,9,8,128]{3,2,1,0:T(8,128)(2,1)S(1)}, u32[]{:S(2)}, u32[]{:S(2)}) async-start(bf16[32,9,8,128]{3,2,1,0:T(8,128)(2,1)} %bitcast.7), calls=%async_computation.4 | async-start | bytes 1179648 | tf_op jit(solution)/shard_map/all_to_all | solution.py:52
  109.6 19.6 %all-gather.1 = bf16[384,896]{1,0:T(8,128)(2,1)S(1)} all-gather(bf16[24,896]{1,0:T(8,128)(2,1)S(1)} %shard_map.81), channel_id=3, replica_groups=mesh['y'=8,'core'=2,'z'=8,'x'=4] {'y','core'}, dimensions={0}, use_global_device_ids=true | all-gather | bytes 731136 | tf_op jit(solution)/shard_map/all_gather | solution.py:299
  129.3 0.0 all-to-all-done.4.g_ref
  129.3 0.0 copy-done.6
  129.3 2.5 shard_map.83
  131.8 11.5 %all_to_all.70.x_ref = bf16[8,8,8,128]{3,2,1,0:T(8,128)(2,1)S(1)} all-to-all(bf16[8,8,8,128]{3,2,1,0:T(8,128)(2,1)S(1)} %get-tuple-element.42), channel_id=1, replica_groups=mesh['y'=8,'core'=2,'z'=8,'x'=4] {'y'}, dimensions={0} | all-to-all | bytes 262144 | tf_op jit(solution)/shard_map/all_to_all | solution.py:52
  143.3 10.3 %all_to_all.71.refs_0_ = bf16[8,8,8,128]{3,2,1,0:T(8,128)(2,1)S(1)} all-to-all(bf16[8,8,8,128]{3,2,1,0:T(8,128)(2,1)S(1)} %shard_map.84), channel_id=1, replica_groups=mesh['y'=8,'core'=2,'z'=8,'x'=4] {'y'}, dimensions={0} | all-to-all | bytes 262144 | tf_op jit(solution)/shard_map/all_to_all | solution.py:52
  153.6 0.0 copy-done.1
  153.6 4.2 %shard_map.85 = bf16[32,8,8,128]{3,2,1,0:T(8,128)(2,1)S(1)} custom-call(bf16[8,8,8,128]{3,2,1,0:T(8,128)(2,1)S(1)} %all_to_all.71.refs_0_, bf16[1792,896]{1,0:T(8,128)(2,1)S(1)} %copy-done.1, bf16[1792,896]{1,0:T(8,128)(2,1)} %collective-permute-done.1.v_ref.refs_2_), custom_call_target="tpu_custom_call" | custom-call | tf_op jit(solution)/shard_map/pallas_call | solution.py:40
  157.8 22.7 %all_to_all.72.x_ref = bf16[32,8,8,128]{3,2,1,0:T(8,128)(2,1)S(1)} all-to-all(bf16[32,8,8,128]{3,2,1,0:T(8,128)(2,1)S(1)} %shard_map.85), channel_id=1, replica_groups=mesh['y'=8,'core'=2,'z'=8,'x'=4] {'z','x'}, dimensions={0} | all-to-all | bytes 1048576 | tf_op jit(solution)/shard_map/all_to_all | solution.py:52
  180.6 0.1 shard_map.86
  180.7 18.9 %all_to_all.73.refs_0_ = bf16[32,8,8,128]{3,2,1,0:T(8,128)(2,1)S(1)} all-to-all(bf16[32,8,8,128]{3,2,1,0:T(8,128)(2,1)S(1)} %shard_map.86), channel_id=1, replica_groups=mesh['y'=8,'core'=2,'z'=8,'x'=4] {'z','x'}, dimensions={0} | all-to-all | bytes 1048576 | tf_op jit(solution)/shard_map/all_to_all | solution.py:52
  199.6 3.2 %shard_map.87 = (bf16[8,12,8,128]{3,2,1,0:T(8,128)(2,1)S(1)}, bf16[72,1792]{1,0:T(8,128)(2,1)S(1)}, bf16[72,1792]{1,0:T(8,128)(2,1)S(1)}) custom-call(bf16[32,8,8,128]{3,2,1,0:T(8,128)(2,1)S(1)} %all_to_all.73.refs_0_, bf16[1792,896]{1,0:T(8,128)(2,1)S(1)} %copy-done.1, bf16[1792,896]{1,0:T(8,128)(2,1)} %collective-permute-done.1.v_ref.refs_2_), custom_call_target="tpu_custom_call" | custom-call | tf_op jit(solution)/shard_map/pallas_call | solution.py:40
  202.8 11.4 %all_to_all.74.x_ref = bf16[8,12,8,128]{3,2,1,0:T(8,128)(2,1)S(1)} all-to-all(bf16[8,12,8,128]{3,2,1,0:T(8,128)(2,1)S(1)} %get-tuple-element.43), channel_id=1, replica_groups=mesh['y'=8,'core'=2,'z'=8,'x'=4] {'y'}, dimensions={0} | all-to-all | bytes 393216 | tf_op jit(solution)/shard_map/all_to_all | solution.py:52
  214.3 11.0 %all_to_all.75.m_ref = bf16[8,12,8,128]{3,2,1,0:T(8,128)(2,1)S(1)} all-to-all(bf16[8,12,8,128]{3,2,1,0:T(8,128)(2,1)S(1)} %shard_map.88), channel_id=1, replica_groups=mesh['y'=8,'core'=2,'z'=8,'x'=4] {'y'}, dimensions={0} | all-to-all | bytes 393216 | tf_op jit(solution)/shard_map/all_to_all | solution.py:52
  225.3 1.1 shard_map.89
  226.4 6.1 %all-to-all-start.11 = ((bf16[32,3,8,128]{3,2,1,0:T(8,128)(2,1)}), bf16[32,3,8,128]{3,2,1,0:T(8,128)(2,1)S(1)}, u32[]{:S(2)}, u32[]{:S(2)}) async-start(bf16[32,3,8,128]{3,2,1,0:T(8,128)(2,1)} %bitcast.8), calls=%async_computation.11 | async-start | bytes 393216 | tf_op jit(solution)/shard_map/all_to_all | solution.py:52
  232.5 8.5 %collective-permute-start.3 = (bf16[72,1792]{1,0:T(8,128)(2,1)S(1)}, bf16[72,1792]{1,0:T(8,128)(2,1)S(1)}, u32[]{:S(2)}, u32[]{:S(2)}) collective-permute-start(bf16[72,1792]{1,0:T(8,128)(2,1)S(1)} %get-tuple-element.45), channel_id=1, source_target_pairs={{0,32},{32,0},{1,33},{33,1},{2,34},{34,2},{3,35},{35,3},{4,36},{36... | collective-permute-start | bytes 774152 | tf_op jit(solution)/shard_map/ppermute | solution.py:56
  241.0 6.0 %shard_map.90.w_ref = f32[72,128]{1,0:T(8,128)S(1)} custom-call(bf16[8,12,8,128]{3,2,1,0:T(8,128)(2,1)S(1)} %all_to_all.75.m_ref), custom_call_target="tpu_custom_call" | custom-call | tf_op jit(solution)/shard_map/pallas_call | solution.py:40
  247.0 0.0 collective-permute-done.3.got_ref
  247.0 0.0 all-to-all-done.11.x_ref
  247.0 20.1 %all_to_all.76.c_ref = bf16[32,3,8,128]{3,2,1,0:T(8,128)(2,1)S(1)} all-to-all(bf16[32,3,8,128]{3,2,1,0:T(8,128)(2,1)S(1)} %bitcast.15), channel_id=1, replica_groups=mesh['y'=8,'core'=2,'z'=8,'x'=4] {'z','x'}, dimensions={0} | all-to-all | bytes 393216 | tf_op jit(solution)/shard_map/all_to_all | solution.py:52
  267.1 0.0 copy-done.3
  267.1 0.0 copy-done.5
  267.1 1.0 shard_map.93
  268.1 3.4 %all-to-all-start.13 = ((bf16[8,72,256]{2,1,0:T(8,128)(2,1)}), bf16[8,72,256]{2,1,0:T(8,128)(2,1)S(1)}, u32[]{:S(2)}, u32[]{:S(2)}) async-start(bf16[8,72,256]{2,1,0:T(8,128)(2,1)} %bitcast.11), calls=%async_computation.13 | async-start | bytes 589824 | tf_op jit(solution)/shard_map/all_to_all | solution.py:52
  271.6 3.4 %all-gather.2 = f32[144,128]{1,0:T(8,128)S(1)} all-gather(f32[72,128]{1,0:T(8,128)S(1)} %shard_map.90.w_ref), channel_id=4, replica_groups=mesh['y'=8,'core'=2,'z'=8,'x'=4] {'core'}, dimensions={0}, use_global_device_ids=true | all-gather | bytes 110592 | tf_op jit(solution)/shard_map/all_gather | solution.py:319
  275.0 1.9 shard_map.92
  276.9 4.5 %all-to-all-done.13.p_ref = bf16[8,72,256]{2,1,0:T(8,128)(2,1)S(1)} async-done(((bf16[8,72,256]{2,1,0:T(8,128)(2,1)}), bf16[8,72,256]{2,1,0:T(8,128)(2,1)S(1)}, u32[]{:S(2)}, u32[]{:S(2)}) %all-to-all-start.13) | async-done | bytes 294944 | tf_op jit(solution)/shard_map/all_to_all | solution.py:52
  281.5 0.2 shard_map.94
  281.7 5.1 %all-gather.3 = f32[144,256]{1,0:T(8,128)S(1)} all-gather(f32[72,256]{1,0:T(8,128)S(1)} %shard_map.94), channel_id=5, replica_groups=mesh['y'=8,'core'=2,'z'=8,'x'=4] {'core'}, dimensions={0}, use_global_device_ids=true | all-gather | bytes 221184 | tf_op jit(solution)/shard_map/all_gather | solution.py:323
  286.8 0.7 copy.9
  (10 shorter events, 0.2 us)
Async XLA Ops:
  0.6 15.9 %copy-start.8 = (bf16[12,2,256]{2,1,0:T(2,128)(2,1)S(1)}, bf16[12,2,256]{2,1,0:T(2,128)(2,1)}, u32[]{:S(2)}) copy-start(bf16[12,2,256]{2,1,0:T(2,128)(2,1)} %param.7) | copy-start | bytes 36868
  11.9 24.7 %all-to-all-start = ((bf16[8,8,3584]{2,1,0:T(8,128)(2,1)}), bf16[8,8,3584]{2,1,0:T(8,128)(2,1)S(1)}, u32[]{:S(2)}, u32[]{:S(2)}) async-start(bf16[8,8,3584]{2,1,0:T(8,128)(2,1)} %bitcast.19), calls=%async_computation | async-start | bytes 917504 | tf_op jit(solution)/shard_map/all_to_all | solution.py:52
  36.5 2.2 copy-start.7
  36.5 11.1 %copy-start.2 = (bf16[256,512]{1,0:T(8,128)(2,1)S(1)}, bf16[256,512]{1,0:T(8,128)(2,1)}, u32[]{:S(2)}) copy-start(bf16[256,512]{1,0:T(8,128)(2,1)} %w_ref.5) | copy-start | bytes 786436
  36.5 26.6 %collective-permute-start.1 = (bf16[1792,896]{1,0:T(8,128)(2,1)}, bf16[1792,896]{1,0:T(8,128)(2,1)}, u32[]{:S(2)}, u32[]{:S(2)}) collective-permute-start(bf16[1792,896]{1,0:T(8,128)(2,1)} %refs_1_.3), channel_id=1, source_target_pairs={{0,32},{32,0},{1,33},{33,1},{2,34},{34,2},{3,35},{35,3},{4,36},{36... | collective-permute-start | bytes 9633800 | tf_op jit(solution)/shard_map/ppermute | solution.py:56
  41.1 22.1 %all-to-all-start.1 = ((bf16[4,48,3584]{2,1,0:T(8,128)(2,1)}), bf16[4,48,3584]{2,1,0:T(8,128)(2,1)S(1)}, u32[]{:S(2)}, u32[]{:S(2)}) async-start(bf16[4,48,3584]{2,1,0:T(8,128)(2,1)} %shard_map.78), calls=%async_computation.1 | async-start | bytes 2752512 | tf_op jit(solution)/shard_map/all_to_all | solution.py:52
  45.1 9.2 %collective-permute-start.2 = (bf16[896,512]{1,0:T(8,128)(2,1)}, bf16[896,512]{1,0:T(8,128)(2,1)}, u32[]{:S(2)}, u32[]{:S(2)}) collective-permute-start(bf16[896,512]{1,0:T(8,128)(2,1)} %e_ref.1), channel_id=1, source_target_pairs={{0,32},{32,0},{1,33},{33,1},{2,34},{34,2},{3,35},{35,3},{4,36},{36... | collective-permute-start | bytes 2752520 | tf_op jit(solution)/shard_map/ppermute | solution.py:56
  47.6 3.4 %collective-permute-start = (bf16[256,512]{1,0:T(8,128)(2,1)S(1)}, bf16[256,512]{1,0:T(8,128)(2,1)S(1)}, u32[]{:S(2)}, u32[]{:S(2)}) collective-permute-start(bf16[256,512]{1,0:T(8,128)(2,1)S(1)} %copy-done.2), channel_id=1, source_target_pairs={{0,32},{32,0},{1,33},{33,1},{2,34},{34,2},{3,35},{35,3},{4,36},{36... | collective-permute-start | bytes 786440 | tf_op jit(solution)/shard_map/ppermute | solution.py:56
  51.1 0.7 copy-start.4
  63.2 24.4 %all-to-all-start.2 = ((bf16[32,9,8,128]{3,2,1,0:T(8,128)(2,1)}), bf16[32,9,8,128]{3,2,1,0:T(8,128)(2,1)S(1)}, u32[]{:S(2)}, u32[]{:S(2)}) async-start(bf16[32,9,8,128]{3,2,1,0:T(8,128)(2,1)} %bitcast.17), calls=%async_computation.2 | async-start | bytes 1179648 | tf_op jit(solution)/shard_map/all_to_all | solution.py:52
  71.1 1.9 copy-start
  87.5 14.4 %all-to-all-start.3 = ((bf16[8,24,896]{2,1,0:T(8,128)(2,1)}), bf16[8,24,896]{2,1,0:T(8,128)(2,1)S(1)}, u32[]{:S(2)}, u32[]{:S(2)}) async-start(bf16[8,24,896]{2,1,0:T(8,128)(2,1)} %bitcast.5), calls=%async_computation.3 | async-start | bytes 688128 | tf_op jit(solution)/shard_map/all_to_all | solution.py:52
  91.5 37.7 %copy-start.6 = (bf16[896,512]{1,0:T(8,128)(2,1)S(1)}, bf16[896,512]{1,0:T(8,128)(2,1)}, u32[]{:S(2)}) copy-start(bf16[896,512]{1,0:T(8,128)(2,1)} %e_ref.1) | copy-start | bytes 2752516
  101.9 27.3 %all-to-all-start.4 = ((bf16[32,9,8,128]{3,2,1,0:T(8,128)(2,1)}), bf16[32,9,8,128]{3,2,1,0:T(8,128)(2,1)S(1)}, u32[]{:S(2)}, u32[]{:S(2)}) async-start(bf16[32,9,8,128]{3,2,1,0:T(8,128)(2,1)} %bitcast.7), calls=%async_computation.4 | async-start | bytes 1179648 | tf_op jit(solution)/shard_map/all_to_all | solution.py:52
  129.3 24.4 %copy-start.1 = (bf16[1792,896]{1,0:T(8,128)(2,1)S(1)}, bf16[1792,896]{1,0:T(8,128)(2,1)}, u32[]{:S(2)}) copy-start(bf16[1792,896]{1,0:T(8,128)(2,1)} %refs_1_.3) | copy-start | bytes 9633796
  225.3 41.8 %copy-start.3 = (bf16[256,512]{1,0:T(8,128)(2,1)S(1)}, bf16[256,512]{1,0:T(8,128)(2,1)}, u32[]{:S(2)}) copy-start(bf16[256,512]{1,0:T(8,128)(2,1)} %w_ref.5) | copy-start | bytes 786436
  225.3 41.8 %copy-start.5 = (bf16[256,512]{1,0:T(8,128)(2,1)S(1)}, bf16[256,512]{1,0:T(8,128)(2,1)}, u32[]{:S(2)}) copy-start(bf16[256,512]{1,0:T(8,128)(2,1)} %copy-done.4) | copy-start | bytes 786436
  226.4 20.5 %all-to-all-start.11 = ((bf16[32,3,8,128]{3,2,1,0:T(8,128)(2,1)}), bf16[32,3,8,128]{3,2,1,0:T(8,128)(2,1)S(1)}, u32[]{:S(2)}, u32[]{:S(2)}) async-start(bf16[32,3,8,128]{3,2,1,0:T(8,128)(2,1)} %bitcast.8), calls=%async_computation.11 | async-start | bytes 393216 | tf_op jit(solution)/shard_map/all_to_all | solution.py:52
  232.5 14.5 %collective-permute-start.3 = (bf16[72,1792]{1,0:T(8,128)(2,1)S(1)}, bf16[72,1792]{1,0:T(8,128)(2,1)S(1)}, u32[]{:S(2)}, u32[]{:S(2)}) collective-permute-start(bf16[72,1792]{1,0:T(8,128)(2,1)S(1)} %get-tuple-element.45), channel_id=1, source_target_pairs={{0,32},{32,0},{1,33},{33,1},{2,34},{34,2},{3,35},{35,3},{4,36},{36... | collective-permute-start | bytes 774152 | tf_op jit(solution)/shard_map/ppermute | solution.py:56
  268.1 13.3 %all-to-all-start.13 = ((bf16[8,72,256]{2,1,0:T(8,128)(2,1)}), bf16[8,72,256]{2,1,0:T(8,128)(2,1)S(1)}, u32[]{:S(2)}, u32[]{:S(2)}) async-start(bf16[8,72,256]{2,1,0:T(8,128)(2,1)} %bitcast.11), calls=%async_computation.13 | async-start | bytes 589824 | tf_op jit(solution)/shard_map/all_to_all | solution.py:52

commit v8 on v6

--- a/solution.py
+++ b/solution.py
@@ -11,9 +11,10 @@
 BF = jnp.bfloat16
 F32 = jnp.float32
 MIB = 1024 * 1024
-
-
-def call(body, out, *args, limit=52):
+FRONT = 60
+
+
+def call(body, out, *args, limit=32):
     many = isinstance(out, list)
     shapes = [jax.ShapeDtypeStruct(s, d) for s, d in (out if many else [out])]
     got = pl.pallas_call(
@@ -253,24 +254,24 @@
 def on_device(acts, grads, basis_in, basis_out, eigen, sketch):
     lines = jnp.pad(acts.reshape(12, 1792), ((0, 4), (0, 0)))
     lines = lax.all_gather(lines, "core").reshape(32, 1792)
-    packed = call(pack_body, ((64, 3584), BF), lines)
+    packed = call(pack_body, ((64, 3584), BF), lines, limit=FRONT)
     packed, own_grads = lax.optimization_barrier((packed, grads))
     all_grads = lax.all_gather(own_grads.reshape(24, 256), ROW).reshape(384, 256)
     near = swap(packed.reshape(8, 8, 3584), "z").reshape(64, 3584)
     near, all_grads, away = lax.optimization_barrier(
         (near, all_grads, (basis_in, basis_out, eigen))
     )
-    dense = call(dense_body, ((4, 48, 3584), BF), near)
+    dense = call(dense_body, ((4, 48, 3584), BF), near, limit=FRONT)
     far_in, far_out, far_eigen = [from_sibling(w) for w in away]
     g_part = call(
-        grad_body, ((2304, 128), BF), all_grads, sketch, basis_out, far_out
+        grad_body, ((2304, 128), BF), all_grads, sketch, basis_out, far_out, limit=FRONT
     )
     both = swap(dense, "x").reshape(192, 3584)
     both, g_part, far_in, far_eigen = lax.optimization_barrier((both, g_part, far_in, far_eigen))
     g_pieces = swap(g_part.reshape(32, 9, 8, 128), COL)
-    a_part = call(act_body, ((192, 896), BF), both, basis_in, far_in)
+    a_part = call(act_body, ((192, 896), BF), both, basis_in, far_in, limit=FRONT)
     a_part, g_pieces = lax.optimization_barrier((a_part, g_pieces))
-    g_own = call(sum_flat_body, ((2304, 128), BF), g_pieces)
+    g_own = call(sum_flat_body, ((2304, 128), BF), g_pieces, limit=FRONT)
     a_own = summed(a_part.reshape(8, 24, 896), "y")
     a_own, g_own = lax.optimization_barrier((a_own, g_own))
     g_rot = swap(g_own.reshape(32, 9, 8, 128), COL)

time: 286 us -> 288 us (level)
  local copies, waits for them, and re-layouts: 1.51 us -> 5.89 us
  Pallas kernels: 35.1 us -> 31.7 us
  waiting for transfers between devices: 44.4 us -> 41.3 us
  blocking collectives: 144 us -> 147 us
    unnamed x9 -> x27, local copies, waits for them, and re-layouts: 0.68 us -> 5.06 us
    pallas_call x18, Pallas kernels: 35.1 us -> 31.7 us  [call(): pl.pallas_call(body, out_shape=shapes, in_specs=[pl.BlockSpec(memory_spac...]
    all_to_all x8, waiting for transfers between devices: 42.9 us -> 39.9 us  [swap(): return lax.all_to_all(x, axes, 0, 0, tiled=True)]
  transfers between devices with their start and end apart: 12 -> 12, of which waited for: 6 -> 6; matrix products, arithmetic and copies ran while one was open for 0% -> 0% of each run, Pallas kernels for 6% -> 7%
where the time goes in v8:
time: 288 us; the launch traced here: 286 us
  blocking collectives  147 us (51%)
  starting transfers between devices  59.2 us (21%)
  waiting for transfers between devices  41.3 us (14%)
  Pallas kernels  31.7 us (11%)
  local copies, waits for them, and re-layouts  5.89 us (2%)
    all_to_all x6, blocking collectives, swap(): return lax.all_to_all(x, axes, 0, 0, tiled=True)  85.8 us
    all_to_all x8, starting transfers between devices, swap(): return lax.all_to_all(x, axes, 0, 0, tiled=True)  43.9 us
    all_to_all x8, waiting for transfers between devices, swap(): return lax.all_to_all(x, axes, 0, 0, tiled=True)  39.9 us
    pallas_call x18, Pallas kernels, call(): pl.pallas_call(body, out_shape=shapes, in_specs=[pl.BlockSpec(memory_spac...  31.7 us
    all_gather x1, blocking collectives, on_device(): a_rot = lax.all_gather(a_own, ROW).reshape(8, 2, 24, 896)  21.3 us
    all_gather x1, blocking collectives, on_device(): lax.all_gather(own_grads.reshape(24, 256), ROW).reshape(384, 256)  20 us
    ppermute x4, starting transfers between devices, from_sibling(): return lax.ppermute(x, 'core', [(0, 1), (1, 0)])  15.4 us
    all_gather x1, blocking collectives, on_device(): return (basis, lax.all_gather(mine, 'core'))  9.93 us
  transfers between devices with their start and end apart: 12, of which 6 were waited for; matrix products, arithmetic and copies ran while one was open for 0% of the time, Pallas kernels for 7%

profile of v8, /device:TPU:1, one launch (start us, length us, event | category | flops | bytes accessed | tf_op | source)
XLA Modules:
  0.0 286.3 jit_solution(3963191931416492385)
XLA Ops:
  0.6 0.0 copy-start.12
  0.6 0.8 reshape.43
  1.5 8.5 %all-gather.x_ref = bf16[32,1792]{1,0:T(8,128)(2,1)} all-gather(bf16[16,1792]{1,0:T(8,128)(2,1)S(1)} %pad.4), channel_id=2, replica_groups=mesh['y'=8,'core'=2,'z'=8,'x'=4] {'core'}, dimensions={0}, use_global_device_ids=true | all-gather | bytes 172032 | tf_op jit(solution)/shard_map/all_gather | solution.py:256
  10.0 1.8 shard_map.77
  11.9 4.7 %all-to-all-start = ((bf16[8,8,3584]{2,1,0:T(8,128)(2,1)}), bf16[8,8,3584]{2,1,0:T(8,128)(2,1)S(1)}, u32[]{:S(2)}, u32[]{:S(2)}) async-start(bf16[8,8,3584]{2,1,0:T(8,128)(2,1)} %bitcast.18), calls=%async_computation | async-start | bytes 917504 | tf_op jit(solution)/shard_map/all_to_all | solution.py:31
  16.5 0.0 copy-done.12
  16.5 20.0 %all_gather.29 = bf16[16,24,256]{2,1,0:T(8,128)(2,1)} all-gather(bf16[1,24,256]{2,1,0:T(8,128)(2,1)S(1)} %all_gather_reshape.3), channel_id=1, replica_groups=mesh['y'=8,'core'=2,'z'=8,'x'=4] {'y','core'}, dimensions={0}, use_global_device_ids=true | all-gather | bytes 208896 | tf_op jit(solution)/shard_map/all_gather | solution.py:259
  36.5 0.0 all-to-all-done
  36.5 0.8 copy-done.11
  37.3 2.2 collective-permute-start.1
  39.5 2.3 shard_map.78
  41.8 4.3 %all-to-all-start.1 = ((bf16[4,48,3584]{2,1,0:T(8,128)(2,1)}), bf16[4,48,3584]{2,1,0:T(8,128)(2,1)}, u32[]{:S(2)}, u32[]{:S(2)}) async-start(bf16[4,48,3584]{2,1,0:T(8,128)(2,1)} %shard_map.78), calls=%async_computation.1 | async-start | bytes 2752512 | tf_op jit(solution)/shard_map/all_to_all | solution.py:31
  46.2 2.3 collective-permute-start.2
  48.4 0.0 copy-done.4
  48.4 2.1 collective-permute-start
  50.5 1.3 collective-permute-done.v_ref
  51.9 0.7 copy-done.6
  52.6 2.5 shard_map.79
  55.1 0.0 collective-permute-done.2.f_ref
  55.1 9.5 %all-to-all-done.1 = bf16[4,48,3584]{2,1,0:T(8,128)(2,1)} async-done(((bf16[4,48,3584]{2,1,0:T(8,128)(2,1)}), bf16[4,48,3584]{2,1,0:T(8,128)(2,1)}, u32[]{:S(2)}, u32[]{:S(2)}) %all-to-all-start.1) | async-done | bytes 1376288 | tf_op jit(solution)/shard_map/all_to_all | solution.py:31
  64.6 0.0 collective-permute-done.1.v_ref
  64.6 8.0 %all-to-all-start.2 = ((bf16[32,9,8,128]{3,2,1,0:T(8,128)(2,1)}), bf16[32,9,8,128]{3,2,1,0:T(8,128)(2,1)}, u32[]{:S(2)}, u32[]{:S(2)}) async-start(bf16[32,9,8,128]{3,2,1,0:T(8,128)(2,1)} %bitcast.16), calls=%async_computation.2 | async-start | bytes 1179648 | tf_op jit(solution)/shard_map/all_to_all | solution.py:31
  72.6 0.0 copy-done.1
  72.6 5.7 %shard_map.80 = bf16[192,896]{1,0:T(8,128)(2,1)} custom-call(bf16[192,3584]{1,0:T(8,128)(2,1)} %bitcast.3.x_ref, bf16[1792,896]{1,0:T(8,128)(2,1)} %w_ref.8, bf16[1792,896]{1,0:T(8,128)(2,1)} %copy-done.1), custom_call_target="tpu_custom_call" | custom-call | tf_op jit(solution)/shard_map/pallas_call | solution.py:20
  78.3 10.9 %all-to-all-done.2.x_ref = bf16[32,9,8,128]{3,2,1,0:T(8,128)(2,1)} async-done(((bf16[32,9,8,128]{3,2,1,0:T(8,128)(2,1)}), bf16[32,9,8,128]{3,2,1,0:T(8,128)(2,1)}, u32[]{:S(2)}, u32[]{:S(2)}) %all-to-all-start.2) | async-done | bytes 589856 | tf_op jit(solution)/shard_map/all_to_all | solution.py:31
  89.2 4.1 %all-to-all-start.3 = ((bf16[8,24,896]{2,1,0:T(8,128)(2,1)}), bf16[8,24,896]{2,1,0:T(8,128)(2,1)S(1)}, u32[]{:S(2)}, u32[]{:S(2)}) async-start(bf16[8,24,896]{2,1,0:T(8,128)(2,1)} %bitcast.19), calls=%async_computation.3 | async-start | bytes 688128 | tf_op jit(solution)/shard_map/all_to_all | solution.py:31
  93.2 2.1 shard_map.82
  95.4 8.1 %all-to-all-done.3.x_ref = bf16[8,24,896]{2,1,0:T(8,128)(2,1)S(1)} async-done(((bf16[8,24,896]{2,1,0:T(8,128)(2,1)}), bf16[8,24,896]{2,1,0:T(8,128)(2,1)S(1)}, u32[]{:S(2)}, u32[]{:S(2)}) %all-to-all-start.3) | async-done | bytes 344096 | tf_op jit(solution)/shard_map/all_to_all | solution.py:31
  103.5 0.0 copy-start.9
  103.5 0.6 copy-done.9
  104.2 7.8 %all-to-all-start.4 = ((bf16[32,9,8,128]{3,2,1,0:T(8,128)(2,1)}), bf16[32,9,8,128]{3,2,1,0:T(8,128)(2,1)}, u32[]{:S(2)}, u32[]{:S(2)}) async-start(bf16[32,9,8,128]{3,2,1,0:T(8,128)(2,1)} %bitcast.15), calls=%async_computation.4 | async-start | bytes 1179648 | tf_op jit(solution)/shard_map/all_to_all | solution.py:31
  111.9 21.3 %all-gather.1 = bf16[384,896]{1,0:T(8,128)(2,1)} all-gather(bf16[24,896]{1,0:T(8,128)(2,1)} %copy-done.9), channel_id=3, replica_groups=mesh['y'=8,'core'=2,'z'=8,'x'=4] {'y','core'}, dimensions={0}, use_global_device_ids=true | all-gather | bytes 731136 | tf_op jit(solution)/shard_map/all_gather | solution.py:278
  133.2 0.0 all-to-all-done.4.g_ref
  133.2 1.1 copy-done.3
  134.3 1.2 copy-done.8
  135.5 2.7 shard_map.83
  138.2 11.5 %all_to_all.70.x_ref = bf16[8,8,8,128]{3,2,1,0:T(8,128)(2,1)S(1)} all-to-all(bf16[8,8,8,128]{3,2,1,0:T(8,128)(2,1)S(1)} %get-tuple-element.43), channel_id=1, replica_groups=mesh['y'=8,'core'=2,'z'=8,'x'=4] {'y'}, dimensions={0} | all-to-all | bytes 262144 | tf_op jit(solution)/shard_map/all_to_all | solution.py:31
  149.7 10.3 %all_to_all.71.r_ref = bf16[8,8,8,128]{3,2,1,0:T(8,128)(2,1)S(1)} all-to-all(bf16[8,8,8,128]{3,2,1,0:T(8,128)(2,1)S(1)} %shard_map.84), channel_id=1, replica_groups=mesh['y'=8,'core'=2,'z'=8,'x'=4] {'y'}, dimensions={0} | all-to-all | bytes 262144 | tf_op jit(solution)/shard_map/all_to_all | solution.py:31
  160.0 0.0 copy-done
  160.0 2.1 shard_map.85
  162.1 22.7 %all_to_all.72.x_ref = bf16[32,8,8,128]{3,2,1,0:T(8,128)(2,1)S(1)} all-to-all(bf16[32,8,8,128]{3,2,1,0:T(8,128)(2,1)S(1)} %shard_map.85), channel_id=1, replica_groups=mesh['y'=8,'core'=2,'z'=8,'x'=4] {'z','x'}, dimensions={0} | all-to-all | bytes 1048576 | tf_op jit(solution)/shard_map/all_to_all | solution.py:31
  184.7 0.1 shard_map.86
  184.8 18.9 %all_to_all.73.r_ref = bf16[32,8,8,128]{3,2,1,0:T(8,128)(2,1)S(1)} all-to-all(bf16[32,8,8,128]{3,2,1,0:T(8,128)(2,1)S(1)} %shard_map.86), channel_id=1, replica_groups=mesh['y'=8,'core'=2,'z'=8,'x'=4] {'z','x'}, dimensions={0} | all-to-all | bytes 1048576 | tf_op jit(solution)/shard_map/all_to_all | solution.py:31
  203.8 1.3 shard_map.87
  205.1 0.0 copy-start.10
  205.1 11.4 %all_to_all.74.x_ref = bf16[8,12,8,128]{3,2,1,0:T(8,128)(2,1)S(1)} all-to-all(bf16[8,12,8,128]{3,2,1,0:T(8,128)(2,1)S(1)} %get-tuple-element.44), channel_id=1, replica_groups=mesh['y'=8,'core'=2,'z'=8,'x'=4] {'y'}, dimensions={0} | all-to-all | bytes 393216 | tf_op jit(solution)/shard_map/all_to_all | solution.py:31
  216.5 11.0 %all_to_all.75.m_ref = bf16[8,12,8,128]{3,2,1,0:T(8,128)(2,1)S(1)} all-to-all(bf16[8,12,8,128]{3,2,1,0:T(8,128)(2,1)S(1)} %shard_map.88), channel_id=1, replica_groups=mesh['y'=8,'core'=2,'z'=8,'x'=4] {'y'}, dimensions={0} | all-to-all | bytes 393216 | tf_op jit(solution)/shard_map/all_to_all | solution.py:31
  227.6 1.1 shard_map.89
  228.7 6.3 %all-to-all-start.11 = ((bf16[32,3,8,128]{3,2,1,0:T(8,128)(2,1)}), bf16[32,3,8,128]{3,2,1,0:T(8,128)(2,1)S(1)}, u32[]{:S(2)}, u32[]{:S(2)}) async-start(bf16[32,3,8,128]{3,2,1,0:T(8,128)(2,1)} %bitcast.8), calls=%async_computation.11 | async-start | bytes 393216 | tf_op jit(solution)/shard_map/all_to_all | solution.py:31
  235.0 6.0 %shard_map.90.w_ref = f32[72,128]{1,0:T(8,128)S(1)} custom-call(bf16[8,12,8,128]{3,2,1,0:T(8,128)(2,1)S(1)} %all_to_all.75.m_ref), custom_call_target="tpu_custom_call" | custom-call | tf_op jit(solution)/shard_map/pallas_call | solution.py:20
  240.9 3.7 %all-to-all-done.11.x_ref = bf16[32,3,8,128]{3,2,1,0:T(8,128)(2,1)S(1)} async-done(((bf16[32,3,8,128]{3,2,1,0:T(8,128)(2,1)}), bf16[32,3,8,128]{3,2,1,0:T(8,128)(2,1)S(1)}, u32[]{:S(2)}, u32[]{:S(2)}) %all-to-all-start.11) | async-done | bytes 196640 | tf_op jit(solution)/shard_map/all_to_all | solution.py:31
  244.7 0.7 shard_map.91
  245.4 5.3 %all-to-all-start.12 = ((bf16[32,3,8,128]{3,2,1,0:T(8,128)(2,1)}), bf16[32,3,8,128]{3,2,1,0:T(8,128)(2,1)S(1)}, u32[]{:S(2)}, u32[]{:S(2)}) async-start(bf16[32,3,8,128]{3,2,1,0:T(8,128)(2,1)} %bitcast.9), calls=%async_computation.12 | async-start | bytes 393216 | tf_op jit(solution)/shard_map/all_to_all | solution.py:31
  250.7 8.8 %collective-permute-start.3 = (bf16[72,1792]{1,0:T(8,128)(2,1)}, bf16[72,1792]{1,0:T(8,128)(2,1)S(1)}, u32[]{:S(2)}, u32[]{:S(2)}) collective-permute-start(bf16[72,1792]{1,0:T(8,128)(2,1)} %copy-done.10), channel_id=1, source_target_pairs={{0,32},{32,0},{1,33},{33,1},{2,34},{34,2},{3,35},{35,3},{4,36},{36... | collective-permute-start | bytes 774152 | tf_op jit(solution)/shard_map/ppermute | solution.py:35
  259.6 1.9 all-gather.2
  261.4 0.0 collective-permute-done.3.got_ref
  261.4 0.0 all-to-all-done.12.c_ref
  261.5 1.0 shard_map.93
  262.4 3.4 %all-to-all-start.13 = ((bf16[8,72,256]{2,1,0:T(8,128)(2,1)}), bf16[8,72,256]{2,1,0:T(8,128)(2,1)S(1)}, u32[]{:S(2)}, u32[]{:S(2)}) async-start(bf16[8,72,256]{2,1,0:T(8,128)(2,1)} %bitcast.11), calls=%async_computation.13 | async-start | bytes 589824 | tf_op jit(solution)/shard_map/all_to_all | solution.py:31
  265.9 1.9 shard_map.92
  267.8 7.7 %all-to-all-done.13.p_ref = bf16[8,72,256]{2,1,0:T(8,128)(2,1)S(1)} async-done(((bf16[8,72,256]{2,1,0:T(8,128)(2,1)}), bf16[8,72,256]{2,1,0:T(8,128)(2,1)S(1)}, u32[]{:S(2)}, u32[]{:S(2)}) %all-to-all-start.13) | async-done | bytes 294944 | tf_op jit(solution)/shard_map/all_to_all | solution.py:31
  275.5 0.2 shard_map.94
  275.7 9.9 %all-gather.3 = f32[144,256]{1,0:T(8,128)S(1)} all-gather(f32[72,256]{1,0:T(8,128)S(1)} %shard_map.94), channel_id=5, replica_groups=mesh['y'=8,'core'=2,'z'=8,'x'=4] {'core'}, dimensions={0}, use_global_device_ids=true | all-gather | bytes 221184 | tf_op jit(solution)/shard_map/all_gather | solution.py:303
  285.6 0.7 copy.9
  (19 shorter events, 0.2 us)
Async XLA Ops:
  0.6 15.9 %copy-start.12 = (bf16[12,2,256]{2,1,0:T(2,128)(2,1)S(1)}, bf16[12,2,256]{2,1,0:T(2,128)(2,1)}, u32[]{:S(2)}) copy-start(bf16[12,2,256]{2,1,0:T(2,128)(2,1)} %param.7) | copy-start | bytes 36868
  11.9 24.7 %all-to-all-start = ((bf16[8,8,3584]{2,1,0:T(8,128)(2,1)}), bf16[8,8,3584]{2,1,0:T(8,128)(2,1)S(1)}, u32[]{:S(2)}, u32[]{:S(2)}) async-start(bf16[8,8,3584]{2,1,0:T(8,128)(2,1)} %bitcast.18), calls=%async_computation | async-start | bytes 917504 | tf_op jit(solution)/shard_map/all_to_all | solution.py:31
  36.5 0.8 copy-start.11
  37.3 11.1 %copy-start.4 = (bf16[256,512]{1,0:T(8,128)(2,1)S(1)}, bf16[256,512]{1,0:T(8,128)(2,1)}, u32[]{:S(2)}) copy-start(bf16[256,512]{1,0:T(8,128)(2,1)} %w_ref.9) | copy-start | bytes 786436
  37.3 27.3 %collective-permute-start.1 = (bf16[1792,896]{1,0:T(8,128)(2,1)}, bf16[1792,896]{1,0:T(8,128)(2,1)S(1)}, u32[]{:S(2)}, u32[]{:S(2)}) collective-permute-start(bf16[1792,896]{1,0:T(8,128)(2,1)} %w_ref.8), channel_id=1, source_target_pairs={{0,32},{32,0},{1,33},{33,1},{2,34},{34,2},{3,35},{35,3},{4,36},{36... | collective-permute-start | bytes 9633800 | tf_op jit(solution)/shard_map/ppermute | solution.py:35
  41.8 22.8 %all-to-all-start.1 = ((bf16[4,48,3584]{2,1,0:T(8,128)(2,1)}), bf16[4,48,3584]{2,1,0:T(8,128)(2,1)}, u32[]{:S(2)}, u32[]{:S(2)}) async-start(bf16[4,48,3584]{2,1,0:T(8,128)(2,1)} %shard_map.78), calls=%async_computation.1 | async-start | bytes 2752512 | tf_op jit(solution)/shard_map/all_to_all | solution.py:31
  46.2 8.9 %collective-permute-start.2 = (bf16[896,512]{1,0:T(8,128)(2,1)}, bf16[896,512]{1,0:T(8,128)(2,1)}, u32[]{:S(2)}, u32[]{:S(2)}) collective-permute-start(bf16[896,512]{1,0:T(8,128)(2,1)} %e_ref.1), channel_id=1, source_target_pairs={{0,32},{32,0},{1,33},{33,1},{2,34},{34,2},{3,35},{35,3},{4,36},{36... | collective-permute-start | bytes 2752520 | tf_op jit(solution)/shard_map/ppermute | solution.py:35
  48.4 3.4 %collective-permute-start = (bf16[256,512]{1,0:T(8,128)(2,1)S(1)}, bf16[256,512]{1,0:T(8,128)(2,1)S(1)}, u32[]{:S(2)}, u32[]{:S(2)}) collective-permute-start(bf16[256,512]{1,0:T(8,128)(2,1)S(1)} %copy-done.4), channel_id=1, source_target_pairs={{0,32},{32,0},{1,33},{33,1},{2,34},{34,2},{3,35},{35,3},{4,36},{36... | collective-permute-start | bytes 786440 | tf_op jit(solution)/shard_map/ppermute | solution.py:35
  51.9 0.7 copy-start.6
  64.6 8.0 %copy-start.1 = (bf16[1792,896]{1,0:T(8,128)(2,1)}, bf16[1792,896]{1,0:T(8,128)(2,1)S(1)}, u32[]{:S(2)}) copy-start(bf16[1792,896]{1,0:T(8,128)(2,1)S(1)} %collective-permute-done.1.v_ref) | copy-start | bytes 9633796
  64.6 24.6 %all-to-all-start.2 = ((bf16[32,9,8,128]{3,2,1,0:T(8,128)(2,1)}), bf16[32,9,8,128]{3,2,1,0:T(8,128)(2,1)}, u32[]{:S(2)}, u32[]{:S(2)}) async-start(bf16[32,9,8,128]{3,2,1,0:T(8,128)(2,1)} %bitcast.16), calls=%async_computation.2 | async-start | bytes 1179648 | tf_op jit(solution)/shard_map/all_to_all | solution.py:31
  89.2 14.3 %all-to-all-start.3 = ((bf16[8,24,896]{2,1,0:T(8,128)(2,1)}), bf16[8,24,896]{2,1,0:T(8,128)(2,1)S(1)}, u32[]{:S(2)}, u32[]{:S(2)}) async-start(bf16[8,24,896]{2,1,0:T(8,128)(2,1)} %bitcast.19), calls=%async_computation.3 | async-start | bytes 688128 | tf_op jit(solution)/shard_map/all_to_all | solution.py:31
  93.2 66.8 %copy-start.2 = (bf16[1792,896]{1,0:T(8,128)(2,1)S(1)}, bf16[1792,896]{1,0:T(8,128)(2,1)}, u32[]{:S(2)}) copy-start(bf16[1792,896]{1,0:T(8,128)(2,1)} %copy-done.1) | copy-start | bytes 9633796
  103.5 0.6 copy-start.9
  104.2 29.0 %all-to-all-start.4 = ((bf16[32,9,8,128]{3,2,1,0:T(8,128)(2,1)}), bf16[32,9,8,128]{3,2,1,0:T(8,128)(2,1)}, u32[]{:S(2)}, u32[]{:S(2)}) async-start(bf16[32,9,8,128]{3,2,1,0:T(8,128)(2,1)} %bitcast.15), calls=%async_computation.4 | async-start | bytes 1179648 | tf_op jit(solution)/shard_map/all_to_all | solution.py:31
  133.2 1.1 copy-start.3
  134.3 1.2 copy-start.8
  135.5 24.5 %copy-start = (bf16[1792,896]{1,0:T(8,128)(2,1)S(1)}, bf16[1792,896]{1,0:T(8,128)(2,1)}, u32[]{:S(2)}) copy-start(bf16[1792,896]{1,0:T(8,128)(2,1)} %w_ref.8) | copy-start | bytes 9633796
  205.1 23.6 %copy-start.10 = (bf16[72,1792]{1,0:T(8,128)(2,1)}, bf16[72,1792]{1,0:T(8,128)(2,1)S(1)}, u32[]{:S(2)}) copy-start(bf16[72,1792]{1,0:T(8,128)(2,1)S(1)} %get-tuple-element.49) | copy-start | bytes 774148
  227.6 33.9 %copy-start.5 = (bf16[256,512]{1,0:T(8,128)(2,1)S(1)}, bf16[256,512]{1,0:T(8,128)(2,1)}, u32[]{:S(2)}) copy-start(bf16[256,512]{1,0:T(8,128)(2,1)} %w_ref.9) | copy-start | bytes 786436
  227.6 33.9 %copy-start.7 = (bf16[256,512]{1,0:T(8,128)(2,1)S(1)}, bf16[256,512]{1,0:T(8,128)(2,1)}, u32[]{:S(2)}) copy-start(bf16[256,512]{1,0:T(8,128)(2,1)} %copy-done.6) | copy-start | bytes 786436
  228.7 16.0 %all-to-all-start.11 = ((bf16[32,3,8,128]{3,2,1,0:T(8,128)(2,1)}), bf16[32,3,8,128]{3,2,1,0:T(8,128)(2,1)S(1)}, u32[]{:S(2)}, u32[]{:S(2)}) async-start(bf16[32,3,8,128]{3,2,1,0:T(8,128)(2,1)} %bitcast.8), calls=%async_computation.11 | async-start | bytes 393216 | tf_op jit(solution)/shard_map/all_to_all | solution.py:31
  245.4 16.1 %all-to-all-start.12 = ((bf16[32,3,8,128]{3,2,1,0:T(8,128)(2,1)}), bf16[32,3,8,128]{3,2,1,0:T(8,128)(2,1)S(1)}, u32[]{:S(2)}, u32[]{:S(2)}) async-start(bf16[32,3,8,128]{3,2,1,0:T(8,128)(2,1)} %bitcast.9), calls=%async_computation.12 | async-start | bytes 393216 | tf_op jit(solution)/shard_map/all_to_all | solution.py:31
  250.7 10.7 %collective-permute-start.3 = (bf16[72,1792]{1,0:T(8,128)(2,1)}, bf16[72,1792]{1,0:T(8,128)(2,1)S(1)}, u32[]{:S(2)}, u32[]{:S(2)}) collective-permute-start(bf16[72,1792]{1,0:T(8,128)(2,1)} %copy-done.10), channel_id=1, source_target_pairs={{0,32},{32,0},{1,33},{33,1},{2,34},{34,2},{3,35},{35,3},{4,36},{36... | collective-permute-start | bytes 774152 | tf_op jit(solution)/shard_map/ppermute | solution.py:35
  262.4 13.0 %all-to-all-start.13 = ((bf16[8,72,256]{2,1,0:T(8,128)(2,1)}), bf16[8,72,256]{2,1,0:T(8,128)(2,1)S(1)}, u32[]{:S(2)}, u32[]{:S(2)}) async-start(bf16[8,72,256]{2,1,0:T(8,128)(2,1)} %bitcast.11), calls=%async_computation.13 | async-start | bytes 589824 | tf_op jit(solution)/shard_map/all_to_all | solution.py:31

commit v9 on v6

--- a/solution.py
+++ b/solution.py
@@ -280,12 +280,12 @@
         a_rot, g_rot, eigen, far_eigen,
     )
     reduced = sum_over(red, "y")
-    span = call(range_body, ((32, 8, 8, 128), BF), reduced, basis_in, far_in)
+    span = call(range_body, ((32, 8, 8, 128), BF), reduced, basis_in, far_in, limit=24)
     span = sum_over(span, COL)
     mapped, keep, give = call(
         mapped_body,
         [((8, 12, 8, 128), BF), ((72, 1792), BF), ((72, 1792), BF)],
-        span, basis_in, far_in,
+        span, basis_in, far_in, limit=24,
     )
     mapped = swap(call(gram_sum_body, ((8, 12, 8, 128), BF), swap(mapped, "y")), "y")
     core = call(core_body, ((768, 128), BF), mapped, scaled)

time: 286 us -> 288 us (level)
  local copies, waits for them, and re-layouts: 1.51 us -> 8.87 us
  Pallas kernels: 35.1 us -> 28.7 us
  blocking collectives: 144 us -> 147 us
    unnamed x9 -> x39, local copies, waits for them, and re-layouts: 0.68 us -> 8.03 us
    pallas_call x18, Pallas kernels: 35.1 us -> 28.7 us  [call(): pl.pallas_call(body, out_shape=shapes, in_specs=[pl.BlockSpec(memory_spac...]
  transfers between devices with their start and end apart: 12 -> 12, of which waited for: 6 -> 6; matrix products, arithmetic and copies ran while one was open for 0% -> 0% of each run, Pallas kernels for 6% -> 5%
where the time goes in v9:
time: 288 us; the launch traced here: 287 us
  blocking collectives  147 us (51%)
  starting transfers between devices  59.1 us (21%)
  waiting for transfers between devices  42 us (15%)
  Pallas kernels  28.7 us (10%)
  local copies, waits for them, and re-layouts  8.87 us (3%)
    all_to_all x6, blocking collectives, swap(): return lax.all_to_all(x, axes, 0, 0, tiled=True)  85.8 us
    all_to_all x8, starting transfers between devices, swap(): return lax.all_to_all(x, axes, 0, 0, tiled=True)  43.8 us
    all_to_all x8, waiting for transfers between devices, swap(): return lax.all_to_all(x, axes, 0, 0, tiled=True)  40.7 us
    pallas_call x18, Pallas kernels, call(): pl.pallas_call(body, out_shape=shapes, in_specs=[pl.BlockSpec(memory_spac...  28.7 us
    all_gather x1, blocking collectives, on_device(): a_rot = lax.all_gather(a_own, ROW).reshape(8, 2, 24, 896)  21.3 us
    all_gather x1, blocking collectives, on_device(): lax.all_gather(own_grads.reshape(24, 256), ROW).reshape(384, 256)  20 us
    ppermute x4, starting transfers between devices, from_sibling(): return lax.ppermute(x, 'core', [(0, 1), (1, 0)])  15.2 us
    all_gather x1, blocking collectives, on_device(): return (basis, lax.all_gather(mine, 'core'))  9.92 us
  transfers between devices with their start and end apart: 12, of which 6 were waited for; matrix products, arithmetic and copies ran while one was open for 0% of the time, Pallas kernels for 5%

profile of v9, /device:TPU:1, one launch (start us, length us, event | category | flops | bytes accessed | tf_op | source)
XLA Modules:
  0.0 286.8 jit_solution(4856822800841609827)
XLA Ops:
  0.6 0.8 reshape.43
  1.5 8.4 %all-gather.x_ref = bf16[32,1792]{1,0:T(8,128)(2,1)S(1)} all-gather(bf16[16,1792]{1,0:T(8,128)(2,1)S(1)} %pad.4), channel_id=2, replica_groups=mesh['y'=8,'core'=2,'z'=8,'x'=4] {'core'}, dimensions={0}, use_global_device_ids=true | all-gather | bytes 172032 | tf_op jit(solution)/shard_map/all_gather | solution.py:255
  9.9 0.9 shard_map.77
  10.8 4.7 %all-to-all-start = ((bf16[8,8,3584]{2,1,0:T(8,128)(2,1)}), bf16[8,8,3584]{2,1,0:T(8,128)(2,1)S(1)}, u32[]{:S(2)}, u32[]{:S(2)}) async-start(bf16[8,8,3584]{2,1,0:T(8,128)(2,1)} %bitcast), calls=%async_computation | async-start | bytes 917504 | tf_op jit(solution)/shard_map/all_to_all | solution.py:30
  15.5 20.0 %all_gather.29 = bf16[16,24,256]{2,1,0:T(8,128)(2,1)} all-gather(bf16[1,24,256]{2,1,0:T(8,128)(2,1)S(1)} %all_gather_reshape.3), channel_id=1, replica_groups=mesh['y'=8,'core'=2,'z'=8,'x'=4] {'y','core'}, dimensions={0}, use_global_device_ids=true | all-gather | bytes 208896 | tf_op jit(solution)/shard_map/all_gather | solution.py:258
  35.5 0.0 all-to-all-done
  35.5 0.8 copy-done.7
  36.3 2.1 collective-permute-start.1
  38.3 0.0 copy-start.8
  38.3 1.0 copy-done.8
  39.4 0.2 shard_map.78
  39.6 1.1 copy-done.3
  40.7 4.3 %all-to-all-start.1 = ((bf16[4,48,3584]{2,1,0:T(8,128)(2,1)}), bf16[4,48,3584]{2,1,0:T(8,128)(2,1)}, u32[]{:S(2)}, u32[]{:S(2)}) async-start(bf16[4,48,3584]{2,1,0:T(8,128)(2,1)} %copy-done.3), calls=%async_computation.1 | async-start | bytes 2752512 | tf_op jit(solution)/shard_map/all_to_all | solution.py:30
  45.0 2.3 collective-permute-start.2
  47.3 2.1 collective-permute-start
  49.4 1.3 collective-permute-done.v_ref
  50.7 0.9 copy-done.13
  51.7 0.5 shard_map.79
  52.2 0.2 copy-done.11
  52.4 0.8 copy-done.6
  53.2 0.0 collective-permute-done.2.f_ref
  53.2 10.3 %all-to-all-done.1 = bf16[4,48,3584]{2,1,0:T(8,128)(2,1)} async-done(((bf16[4,48,3584]{2,1,0:T(8,128)(2,1)}), bf16[4,48,3584]{2,1,0:T(8,128)(2,1)}, u32[]{:S(2)}, u32[]{:S(2)}) %all-to-all-start.1) | async-done | bytes 1376288 | tf_op jit(solution)/shard_map/all_to_all | solution.py:30
  63.5 0.0 collective-permute-done.1.v_ref
  63.5 8.0 %all-to-all-start.2 = ((bf16[32,9,8,128]{3,2,1,0:T(8,128)(2,1)}), bf16[32,9,8,128]{3,2,1,0:T(8,128)(2,1)}, u32[]{:S(2)}, u32[]{:S(2)}) async-start(bf16[32,9,8,128]{3,2,1,0:T(8,128)(2,1)} %bitcast.15), calls=%async_computation.2 | async-start | bytes 1179648 | tf_op jit(solution)/shard_map/all_to_all | solution.py:30
  71.5 5.6 %shard_map.80 = bf16[192,896]{1,0:T(8,128)(2,1)} custom-call(bf16[192,3584]{1,0:T(8,128)(2,1)} %bitcast.3.x_ref, bf16[1792,896]{1,0:T(8,128)(2,1)} %w_ref.8, bf16[1792,896]{1,0:T(8,128)(2,1)} %copy-done.1), custom_call_target="tpu_custom_call" | custom-call | tf_op jit(solution)/shard_map/pallas_call | solution.py:19
  77.2 10.9 %all-to-all-done.2.x_ref = bf16[32,9,8,128]{3,2,1,0:T(8,128)(2,1)} async-done(((bf16[32,9,8,128]{3,2,1,0:T(8,128)(2,1)}), bf16[32,9,8,128]{3,2,1,0:T(8,128)(2,1)}, u32[]{:S(2)}, u32[]{:S(2)}) %all-to-all-start.2) | async-done | bytes 589856 | tf_op jit(solution)/shard_map/all_to_all | solution.py:30
  88.1 4.0 %all-to-all-start.3 = ((bf16[8,24,896]{2,1,0:T(8,128)(2,1)}), bf16[8,24,896]{2,1,0:T(8,128)(2,1)S(1)}, u32[]{:S(2)}, u32[]{:S(2)}) async-start(bf16[8,24,896]{2,1,0:T(8,128)(2,1)} %bitcast.5), calls=%async_computation.3 | async-start | bytes 688128 | tf_op jit(solution)/shard_map/all_to_all | solution.py:30
  92.1 1.3 shard_map.82
  93.4 0.0 copy-start.5
  93.4 0.8 copy-done.5
  94.2 8.1 %all-to-all-done.3.x_ref = bf16[8,24,896]{2,1,0:T(8,128)(2,1)S(1)} async-done(((bf16[8,24,896]{2,1,0:T(8,128)(2,1)}), bf16[8,24,896]{2,1,0:T(8,128)(2,1)S(1)}, u32[]{:S(2)}, u32[]{:S(2)}) %all-to-all-start.3) | async-done | bytes 344096 | tf_op jit(solution)/shard_map/all_to_all | solution.py:30
  102.4 0.0 copy-start.14
  102.4 0.6 copy-done.14
  103.0 7.8 %all-to-all-start.4 = ((bf16[32,9,8,128]{3,2,1,0:T(8,128)(2,1)}), bf16[32,9,8,128]{3,2,1,0:T(8,128)(2,1)}, u32[]{:S(2)}, u32[]{:S(2)}) async-start(bf16[32,9,8,128]{3,2,1,0:T(8,128)(2,1)} %bitcast.14), calls=%async_computation.4 | async-start | bytes 1179648 | tf_op jit(solution)/shard_map/all_to_all | solution.py:30
  110.8 21.3 %all-gather.1 = bf16[384,896]{1,0:T(8,128)(2,1)} all-gather(bf16[24,896]{1,0:T(8,128)(2,1)} %copy-done.14), channel_id=3, replica_groups=mesh['y'=8,'core'=2,'z'=8,'x'=4] {'y','core'}, dimensions={0}, use_global_device_ids=true | all-gather | bytes 731136 | tf_op jit(solution)/shard_map/all_gather | solution.py:277
  132.0 0.0 all-to-all-done.4.g_ref
  132.1 1.1 copy-done.4
  133.2 3.8 %shard_map.83 = (bf16[896,1024]{1,0:T(8,128)(2,1)}, bf16[8,8,8,128]{3,2,1,0:T(8,128)(2,1)S(1)}) custom-call(bf16[8,2,24,896]{3,2,1,0:T(8,128)(2,1)S(1)} %bitcast.13, bf16[32,9,8,128]{3,2,1,0:T(8,128)(2,1)} %all-to-all-done.4.g_ref, bf16[896,512]{1,0:T(8,128)(2,1)} %e_ref.1, bf16[896,512]{1,0:T(8,128)(2,1)} %collective-permute-done.2.f_ref), custom_call_target="tpu_custom_call" | custom-call | tf_op jit(solution)/shard_map/pallas_call | solution.py:19
  137.0 11.5 %all_to_all.70.x_ref = bf16[8,8,8,128]{3,2,1,0:T(8,128)(2,1)S(1)} all-to-all(bf16[8,8,8,128]{3,2,1,0:T(8,128)(2,1)S(1)} %get-tuple-element.43), channel_id=1, replica_groups=mesh['y'=8,'core'=2,'z'=8,'x'=4] {'y'}, dimensions={0} | all-to-all | bytes 262144 | tf_op jit(solution)/shard_map/all_to_all | solution.py:30
  148.5 10.3 %all_to_all.71.r_ref = bf16[8,8,8,128]{3,2,1,0:T(8,128)(2,1)S(1)} all-to-all(bf16[8,8,8,128]{3,2,1,0:T(8,128)(2,1)S(1)} %shard_map.84), channel_id=1, replica_groups=mesh['y'=8,'core'=2,'z'=8,'x'=4] {'y'}, dimensions={0} | all-to-all | bytes 262144 | tf_op jit(solution)/shard_map/all_to_all | solution.py:30
  158.8 2.1 shard_map.85
  160.9 22.7 %all_to_all.72.x_ref = bf16[32,8,8,128]{3,2,1,0:T(8,128)(2,1)S(1)} all-to-all(bf16[32,8,8,128]{3,2,1,0:T(8,128)(2,1)S(1)} %shard_map.85), channel_id=1, replica_groups=mesh['y'=8,'core'=2,'z'=8,'x'=4] {'z','x'}, dimensions={0} | all-to-all | bytes 1048576 | tf_op jit(solution)/shard_map/all_to_all | solution.py:30
  183.5 0.1 shard_map.86
  183.7 18.9 %all_to_all.73.r_ref = bf16[32,8,8,128]{3,2,1,0:T(8,128)(2,1)S(1)} all-to-all(bf16[32,8,8,128]{3,2,1,0:T(8,128)(2,1)S(1)} %shard_map.86), channel_id=1, replica_groups=mesh['y'=8,'core'=2,'z'=8,'x'=4] {'z','x'}, dimensions={0} | all-to-all | bytes 1048576 | tf_op jit(solution)/shard_map/all_to_all | solution.py:30
  202.6 1.3 shard_map.87
  203.9 0.0 copy-start.16
  204.0 11.4 %all_to_all.74.x_ref = bf16[8,12,8,128]{3,2,1,0:T(8,128)(2,1)S(1)} all-to-all(bf16[8,12,8,128]{3,2,1,0:T(8,128)(2,1)S(1)} %get-tuple-element.44), channel_id=1, replica_groups=mesh['y'=8,'core'=2,'z'=8,'x'=4] {'y'}, dimensions={0} | all-to-all | bytes 393216 | tf_op jit(solution)/shard_map/all_to_all | solution.py:30
  215.4 11.0 %all_to_all.75.m_ref = bf16[8,12,8,128]{3,2,1,0:T(8,128)(2,1)S(1)} all-to-all(bf16[8,12,8,128]{3,2,1,0:T(8,128)(2,1)S(1)} %shard_map.88), channel_id=1, replica_groups=mesh['y'=8,'core'=2,'z'=8,'x'=4] {'y'}, dimensions={0} | all-to-all | bytes 393216 | tf_op jit(solution)/shard_map/all_to_all | solution.py:30
  226.4 2.7 shard_map.89
  229.1 6.3 %all-to-all-start.11 = ((bf16[32,3,8,128]{3,2,1,0:T(8,128)(2,1)}), bf16[32,3,8,128]{3,2,1,0:T(8,128)(2,1)S(1)}, u32[]{:S(2)}, u32[]{:S(2)}) async-start(bf16[32,3,8,128]{3,2,1,0:T(8,128)(2,1)} %bitcast.8), calls=%async_computation.11 | async-start | bytes 393216 | tf_op jit(solution)/shard_map/all_to_all | solution.py:30
  235.4 6.0 %shard_map.90.w_ref = f32[72,128]{1,0:T(8,128)S(1)} custom-call(bf16[8,12,8,128]{3,2,1,0:T(8,128)(2,1)S(1)} %all_to_all.75.m_ref), custom_call_target="tpu_custom_call" | custom-call | tf_op jit(solution)/shard_map/pallas_call | solution.py:19
  241.4 3.7 %all-to-all-done.11.x_ref = bf16[32,3,8,128]{3,2,1,0:T(8,128)(2,1)S(1)} async-done(((bf16[32,3,8,128]{3,2,1,0:T(8,128)(2,1)}), bf16[32,3,8,128]{3,2,1,0:T(8,128)(2,1)S(1)}, u32[]{:S(2)}, u32[]{:S(2)}) %all-to-all-start.11) | async-done | bytes 196640 | tf_op jit(solution)/shard_map/all_to_all | solution.py:30
  245.1 0.7 shard_map.91
  245.8 5.3 %all-to-all-start.12 = ((bf16[32,3,8,128]{3,2,1,0:T(8,128)(2,1)}), bf16[32,3,8,128]{3,2,1,0:T(8,128)(2,1)S(1)}, u32[]{:S(2)}, u32[]{:S(2)}) async-start(bf16[32,3,8,128]{3,2,1,0:T(8,128)(2,1)} %bitcast.9), calls=%async_computation.12 | async-start | bytes 393216 | tf_op jit(solution)/shard_map/all_to_all | solution.py:30
  251.2 8.8 %collective-permute-start.3 = (bf16[72,1792]{1,0:T(8,128)(2,1)S(1)}, bf16[72,1792]{1,0:T(8,128)(2,1)S(1)}, u32[]{:S(2)}, u32[]{:S(2)}) collective-permute-start(bf16[72,1792]{1,0:T(8,128)(2,1)S(1)} %copy-done.17), channel_id=1, source_target_pairs={{0,32},{32,0},{1,33},{33,1},{2,34},{34,2},{3,35},{35,3},{4,36},{36... | collective-permute-start | bytes 774152 | tf_op jit(solution)/shard_map/ppermute | solution.py:34
  260.0 1.9 all-gather.2
  261.9 0.0 collective-permute-done.3.got_ref
  261.9 1.0 shard_map.93
  262.9 3.4 %all-to-all-start.13 = ((bf16[8,72,256]{2,1,0:T(8,128)(2,1)}), bf16[8,72,256]{2,1,0:T(8,128)(2,1)S(1)}, u32[]{:S(2)}, u32[]{:S(2)}) async-start(bf16[8,72,256]{2,1,0:T(8,128)(2,1)} %bitcast.11), calls=%async_computation.13 | async-start | bytes 589824 | tf_op jit(solution)/shard_map/all_to_all | solution.py:30
  266.3 1.9 shard_map.92
  268.3 7.7 %all-to-all-done.13.p_ref = bf16[8,72,256]{2,1,0:T(8,128)(2,1)S(1)} async-done(((bf16[8,72,256]{2,1,0:T(8,128)(2,1)}), bf16[8,72,256]{2,1,0:T(8,128)(2,1)S(1)}, u32[]{:S(2)}, u32[]{:S(2)}) %all-to-all-start.13) | async-done | bytes 294944 | tf_op jit(solution)/shard_map/all_to_all | solution.py:30
  275.9 0.2 shard_map.94
  276.2 9.9 %all-gather.3 = f32[144,256]{1,0:T(8,128)S(1)} all-gather(f32[72,256]{1,0:T(8,128)S(1)} %shard_map.94), channel_id=5, replica_groups=mesh['y'=8,'core'=2,'z'=8,'x'=4] {'core'}, dimensions={0}, use_global_device_ids=true | all-gather | bytes 221184 | tf_op jit(solution)/shard_map/all_gather | solution.py:302
  286.1 0.7 copy.9
  (31 shorter events, 0.2 us)
Async XLA Ops:
  0.6 14.9 %copy-start.18 = (bf16[12,2,256]{2,1,0:T(2,128)(2,1)S(1)}, bf16[12,2,256]{2,1,0:T(2,128)(2,1)}, u32[]{:S(2)}) copy-start(bf16[12,2,256]{2,1,0:T(2,128)(2,1)} %param.7) | copy-start | bytes 36868
  10.8 24.7 %all-to-all-start = ((bf16[8,8,3584]{2,1,0:T(8,128)(2,1)}), bf16[8,8,3584]{2,1,0:T(8,128)(2,1)S(1)}, u32[]{:S(2)}, u32[]{:S(2)}) async-start(bf16[8,8,3584]{2,1,0:T(8,128)(2,1)} %bitcast), calls=%async_computation | async-start | bytes 917504 | tf_op jit(solution)/shard_map/all_to_all | solution.py:30
  35.5 0.8 copy-start.7
  36.3 27.2 %collective-permute-start.1 = (bf16[1792,896]{1,0:T(8,128)(2,1)}, bf16[1792,896]{1,0:T(8,128)(2,1)S(1)}, u32[]{:S(2)}, u32[]{:S(2)}) collective-permute-start(bf16[1792,896]{1,0:T(8,128)(2,1)} %w_ref.8), channel_id=1, source_target_pairs={{0,32},{32,0},{1,33},{33,1},{2,34},{34,2},{3,35},{35,3},{4,36},{36... | collective-permute-start | bytes 9633800 | tf_op jit(solution)/shard_map/ppermute | solution.py:34
  38.3 1.0 copy-start.8
  39.4 8.0 %copy-start.9 = (bf16[256,512]{1,0:T(8,128)(2,1)S(1)}, bf16[256,512]{1,0:T(8,128)(2,1)}, u32[]{:S(2)}) copy-start(bf16[256,512]{1,0:T(8,128)(2,1)} %w_ref.9) | copy-start | bytes 786436
  39.4 11.4 %copy-start.15 = (bf16[72,256]{1,0:T(8,128)(2,1)S(1)}, bf16[72,256]{1,0:T(8,128)(2,1)}, u32[]{:S(2)}) copy-start(bf16[72,256]{1,0:T(8,128)(2,1)} %s_ref.1) | copy-start | bytes 110596
  39.6 1.1 copy-start.3
  40.7 22.8 %all-to-all-start.1 = ((bf16[4,48,3584]{2,1,0:T(8,128)(2,1)}), bf16[4,48,3584]{2,1,0:T(8,128)(2,1)}, u32[]{:S(2)}, u32[]{:S(2)}) async-start(bf16[4,48,3584]{2,1,0:T(8,128)(2,1)} %copy-done.3), calls=%async_computation.1 | async-start | bytes 2752512 | tf_op jit(solution)/shard_map/all_to_all | solution.py:30
  45.0 8.2 %collective-permute-start.2 = (bf16[896,512]{1,0:T(8,128)(2,1)}, bf16[896,512]{1,0:T(8,128)(2,1)}, u32[]{:S(2)}, u32[]{:S(2)}) collective-permute-start(bf16[896,512]{1,0:T(8,128)(2,1)} %e_ref.1), channel_id=1, source_target_pairs={{0,32},{32,0},{1,33},{33,1},{2,34},{34,2},{3,35},{35,3},{4,36},{36... | collective-permute-start | bytes 2752520 | tf_op jit(solution)/shard_map/ppermute | solution.py:34
  47.3 3.4 %collective-permute-start = (bf16[256,512]{1,0:T(8,128)(2,1)S(1)}, bf16[256,512]{1,0:T(8,128)(2,1)S(1)}, u32[]{:S(2)}, u32[]{:S(2)}) collective-permute-start(bf16[256,512]{1,0:T(8,128)(2,1)S(1)} %copy-done.9), channel_id=1, source_target_pairs={{0,32},{32,0},{1,33},{33,1},{2,34},{34,2},{3,35},{35,3},{4,36},{36... | collective-permute-start | bytes 786440 | tf_op jit(solution)/shard_map/ppermute | solution.py:34
  50.7 0.9 copy-start.13
  51.7 0.7 copy-start.11
  52.4 0.8 copy-start.6
  63.5 8.0 %copy-start.1 = (bf16[1792,896]{1,0:T(8,128)(2,1)}, bf16[1792,896]{1,0:T(8,128)(2,1)S(1)}, u32[]{:S(2)}) copy-start(bf16[1792,896]{1,0:T(8,128)(2,1)S(1)} %collective-permute-done.1.v_ref) | copy-start | bytes 9633796
  63.5 24.6 %all-to-all-start.2 = ((bf16[32,9,8,128]{3,2,1,0:T(8,128)(2,1)}), bf16[32,9,8,128]{3,2,1,0:T(8,128)(2,1)}, u32[]{:S(2)}, u32[]{:S(2)}) async-start(bf16[32,9,8,128]{3,2,1,0:T(8,128)(2,1)} %bitcast.15), calls=%async_computation.2 | async-start | bytes 1179648 | tf_op jit(solution)/shard_map/all_to_all | solution.py:30
  88.1 14.3 %all-to-all-start.3 = ((bf16[8,24,896]{2,1,0:T(8,128)(2,1)}), bf16[8,24,896]{2,1,0:T(8,128)(2,1)S(1)}, u32[]{:S(2)}, u32[]{:S(2)}) async-start(bf16[8,24,896]{2,1,0:T(8,128)(2,1)} %bitcast.5), calls=%async_computation.3 | async-start | bytes 688128 | tf_op jit(solution)/shard_map/all_to_all | solution.py:30
  92.1 66.8 %copy-start.2 = (bf16[1792,896]{1,0:T(8,128)(2,1)S(1)}, bf16[1792,896]{1,0:T(8,128)(2,1)}, u32[]{:S(2)}) copy-start(bf16[1792,896]{1,0:T(8,128)(2,1)} %copy-done.1) | copy-start | bytes 9633796
  93.4 0.8 copy-start.5
  102.4 0.6 copy-start.14
  103.0 29.1 %all-to-all-start.4 = ((bf16[32,9,8,128]{3,2,1,0:T(8,128)(2,1)}), bf16[32,9,8,128]{3,2,1,0:T(8,128)(2,1)}, u32[]{:S(2)}, u32[]{:S(2)}) async-start(bf16[32,9,8,128]{3,2,1,0:T(8,128)(2,1)} %bitcast.14), calls=%async_computation.4 | async-start | bytes 1179648 | tf_op jit(solution)/shard_map/all_to_all | solution.py:30
  132.1 1.1 copy-start.4
  133.2 25.7 %copy-start = (bf16[1792,896]{1,0:T(8,128)(2,1)S(1)}, bf16[1792,896]{1,0:T(8,128)(2,1)}, u32[]{:S(2)}) copy-start(bf16[1792,896]{1,0:T(8,128)(2,1)} %w_ref.8) | copy-start | bytes 9633796
  203.9 22.5 %copy-start.16 = (bf16[72,1792]{1,0:T(8,128)(2,1)}, bf16[72,1792]{1,0:T(8,128)(2,1)S(1)}, u32[]{:S(2)}) copy-start(bf16[72,1792]{1,0:T(8,128)(2,1)S(1)} %get-tuple-element.49) | copy-start | bytes 774148
  226.4 24.8 %copy-start.17 = (bf16[72,1792]{1,0:T(8,128)(2,1)S(1)}, bf16[72,1792]{1,0:T(8,128)(2,1)}, u32[]{:S(2)}) copy-start(bf16[72,1792]{1,0:T(8,128)(2,1)} %copy-done.16) | copy-start | bytes 774148
  226.4 35.5 %copy-start.10 = (bf16[256,512]{1,0:T(8,128)(2,1)S(1)}, bf16[256,512]{1,0:T(8,128)(2,1)}, u32[]{:S(2)}) copy-start(bf16[256,512]{1,0:T(8,128)(2,1)} %w_ref.9) | copy-start | bytes 786436
  226.4 35.5 %copy-start.12 = (bf16[256,512]{1,0:T(8,128)(2,1)S(1)}, bf16[256,512]{1,0:T(8,128)(2,1)}, u32[]{:S(2)}) copy-start(bf16[256,512]{1,0:T(8,128)(2,1)} %copy-done.11) | copy-start | bytes 786436
  229.1 16.0 %all-to-all-start.11 = ((bf16[32,3,8,128]{3,2,1,0:T(8,128)(2,1)}), bf16[32,3,8,128]{3,2,1,0:T(8,128)(2,1)S(1)}, u32[]{:S(2)}, u32[]{:S(2)}) async-start(bf16[32,3,8,128]{3,2,1,0:T(8,128)(2,1)} %bitcast.8), calls=%async_computation.11 | async-start | bytes 393216 | tf_op jit(solution)/shard_map/all_to_all | solution.py:30
  245.8 16.1 %all-to-all-start.12 = ((bf16[32,3,8,128]{3,2,1,0:T(8,128)(2,1)}), bf16[32,3,8,128]{3,2,1,0:T(8,128)(2,1)S(1)}, u32[]{:S(2)}, u32[]{:S(2)}) async-start(bf16[32,3,8,128]{3,2,1,0:T(8,128)(2,1)} %bitcast.9), calls=%async_computation.12 | async-start | bytes 393216 | tf_op jit(solution)/shard_map/all_to_all | solution.py:30
  251.2 10.7 %collective-permute-start.3 = (bf16[72,1792]{1,0:T(8,128)(2,1)S(1)}, bf16[72,1792]{1,0:T(8,128)(2,1)S(1)}, u32[]{:S(2)}, u32[]{:S(2)}) collective-permute-start(bf16[72,1792]{1,0:T(8,128)(2,1)S(1)} %copy-done.17), channel_id=1, source_target_pairs={{0,32},{32,0},{1,33},{33,1},{2,34},{34,2},{3,35},{35,3},{4,36},{36... | collective-permute-start | bytes 774152 | tf_op jit(solution)/shard_map/ppermute | solution.py:34
  262.9 13.0 %all-to-all-start.13 = ((bf16[8,72,256]{2,1,0:T(8,128)(2,1)}), bf16[8,72,256]{2,1,0:T(8,128)(2,1)S(1)}, u32[]{:S(2)}, u32[]{:S(2)}) async-start(bf16[8,72,256]{2,1,0:T(8,128)(2,1)} %bitcast.11), calls=%async_computation.13 | async-start | bytes 589824 | tf_op jit(solution)/shard_map/all_to_all | solution.py:30

commit v10 on v5

--- a/solution.py
+++ b/solution.py
@@ -257,16 +257,17 @@
     packed, own_grads, away_out = lax.optimization_barrier((packed, grads, basis_out))
     own_grads = own_grads.reshape(24, 256)
     own_grads, away_in = lax.optimization_barrier((own_grads, basis_in))
-    far_out, far_in = from_sibling(away_out), from_sibling(away_in)
+    far_out = from_sibling(away_out)
     near = swap(packed.reshape(8, 8, 3584), "z").reshape(64, 3584)
-    near, own_grads, far_out, far_in = lax.optimization_barrier((near, own_grads, far_out, far_in))
+    near, own_grads, far_out, away_in = lax.optimization_barrier((near, own_grads, far_out, away_in))
+    far_in = from_sibling(away_in)
     dense = call(dense_body, ((4, 48, 3584), BF), near, limit=62)
     all_grads = lax.all_gather(own_grads, ROW).reshape(384, 256)
     g_part = call(
         grad_body, ((2304, 128), BF), all_grads, sketch, basis_out, far_out, limit=62
     )
     both = swap(dense, "x").reshape(192, 3584)
-    both, g_part, away = lax.optimization_barrier((both, g_part, eigen))
+    both, g_part, away, far_in = lax.optimization_barrier((both, g_part, eigen, far_in))
     g_pieces = swap(g_part.reshape(32, 9, 8, 128), COL)
     a_part = call(act_body, ((192, 896), BF), both, basis_in, far_in)
     a_part, g_pieces, far_eigen = lax.optimization_barrier((a_part, g_pieces, from_sibling(away)))

time: 285 us -> 283 us (level)
  local copies, waits for them, and re-layouts: 11.7 us -> 5.57 us
  Pallas kernels: 27.9 us -> 32.6 us
    unnamed x25, local copies, waits for them, and re-layouts: 10.2 us -> 4.7 us
    pallas_call x18, Pallas kernels: 27.9 us -> 32.6 us  [call(): pl.pallas_call(body, out_shape=shapes, in_specs=[pl.BlockSpec(memory_spac...]
  transfers between devices with their start and end apart: 12 -> 12, of which waited for: 6 -> 6; matrix products, arithmetic and copies ran while one was open for 0% -> 0% of each run, Pallas kernels for 5% -> 7%
where the time goes in v10:
time: 283 us; the launch traced here: 282 us
  blocking collectives  146 us (52%)
  starting transfers between devices  54.8 us (19%)
  waiting for transfers between devices  42.5 us (15%)
  Pallas kernels  32.6 us (12%)
  local copies, waits for them, and re-layouts  5.57 us (2%)
    all_to_all x6, blocking collectives, swap(): return lax.all_to_all(x, axes, 0, 0, tiled=True)  85.9 us
    all_to_all x8, waiting for transfers between devices, swap(): return lax.all_to_all(x, axes, 0, 0, tiled=True)  41.4 us
    all_to_all x8, starting transfers between devices, swap(): return lax.all_to_all(x, axes, 0, 0, tiled=True)  38.6 us
    pallas_call x18, Pallas kernels, call(): pl.pallas_call(body, out_shape=shapes, in_specs=[pl.BlockSpec(memory_spac...  32.6 us
    all_gather x1, blocking collectives, on_device(): a_rot = lax.all_gather(a_own, ROW).reshape(8, 2, 24, 896)  19.8 us
    all_gather x1, blocking collectives, on_device(): all_grads = lax.all_gather(own_grads, ROW).reshape(384, 256)  19.6 us
    ppermute x4, starting transfers between devices, from_sibling(): return lax.ppermute(x, 'core', [(0, 1), (1, 0)])  16.2 us
    all_gather x1, blocking collectives, on_device(): return (basis, lax.all_gather(mine, 'core'))  9.93 us
  transfers between devices with their start and end apart: 12, of which 6 were waited for; matrix products, arithmetic and copies ran while one was open for 0% of the time, Pallas kernels for 7%

profile of v10, /device:TPU:1, one launch (start us, length us, event | category | flops | bytes accessed | tf_op | source)
XLA Modules:
  0.0 281.9 jit_solution(6486328565655267874)
XLA Ops:
  0.6 0.0 copy-start.2
  0.6 0.0 copy-start.11
  0.7 0.8 reshape.46
  1.5 8.5 %all-gather.x_ref = bf16[32,1792]{1,0:T(8,128)(2,1)} all-gather(bf16[16,1792]{1,0:T(8,128)(2,1)S(1)} %pad.4), channel_id=2, replica_groups=mesh['y'=8,'core'=2,'z'=8,'x'=4] {'core'}, dimensions={0}, use_global_device_ids=true | all-gather | bytes 172032 | tf_op jit(solution)/shard_map/all_gather | solution.py:255
  10.1 1.8 shard_map.77
  11.9 4.7 %all-to-all-start = ((bf16[8,8,3584]{2,1,0:T(8,128)(2,1)}), bf16[8,8,3584]{2,1,0:T(8,128)(2,1)S(1)}, u32[]{:S(2)}, u32[]{:S(2)}) async-start(bf16[8,8,3584]{2,1,0:T(8,128)(2,1)} %bitcast.18), calls=%async_computation | async-start | bytes 917504 | tf_op jit(solution)/shard_map/all_to_all | solution.py:30
  16.6 0.0 copy-done.2
  16.6 2.5 collective-permute-start
  19.1 0.0 copy-done.11
  19.1 1.1 collective-permute-done.v_ref
  20.3 12.9 %all-to-all-done = bf16[8,8,3584]{2,1,0:T(8,128)(2,1)S(1)} async-done(((bf16[8,8,3584]{2,1,0:T(8,128)(2,1)}), bf16[8,8,3584]{2,1,0:T(8,128)(2,1)S(1)}, u32[]{:S(2)}, u32[]{:S(2)}) %all-to-all-start) | async-done | bytes 458784 | tf_op jit(solution)/shard_map/all_to_all | solution.py:30
  33.1 2.4 collective-permute-start.1
  35.5 0.0 copy-done.10
  35.5 2.3 shard_map.78
  37.8 0.0 copy-done.4
  37.9 4.0 %all-to-all-start.1 = ((bf16[4,48,3584]{2,1,0:T(8,128)(2,1)}), bf16[4,48,3584]{2,1,0:T(8,128)(2,1)S(1)}, u32[]{:S(2)}, u32[]{:S(2)}) async-start(bf16[4,48,3584]{2,1,0:T(8,128)(2,1)} %shard_map.78), calls=%async_computation.1 | async-start | bytes 2752512 | tf_op jit(solution)/shard_map/all_to_all | solution.py:30
  41.9 19.6 %all-gather.1.g_ref = bf16[384,256]{1,0:T(8,128)(2,1)} all-gather(bf16[24,256]{1,0:T(8,128)(2,1)S(1)} %reshape.50), channel_id=3, replica_groups=mesh['y'=8,'core'=2,'z'=8,'x'=4] {'y','core'}, dimensions={0}, use_global_device_ids=true | all-gather | bytes 208896 | tf_op jit(solution)/shard_map/all_gather | solution.py:265
  61.5 2.6 shard_map.79
  64.0 0.0 all-to-all-done.1
  64.0 0.0 collective-permute-done.1.v_ref
  64.0 4.9 %all-to-all-start.2 = ((bf16[32,9,8,128]{3,2,1,0:T(8,128)(2,1)}), bf16[32,9,8,128]{3,2,1,0:T(8,128)(2,1)S(1)}, u32[]{:S(2)}, u32[]{:S(2)}) async-start(bf16[32,9,8,128]{3,2,1,0:T(8,128)(2,1)} %bitcast.16), calls=%async_computation.2 | async-start | bytes 1179648 | tf_op jit(solution)/shard_map/all_to_all | solution.py:30
  69.0 2.4 collective-permute-start.2
  71.3 0.0 copy-start
  71.3 1.9 copy-done
  73.2 4.2 %shard_map.80 = bf16[192,896]{1,0:T(8,128)(2,1)} custom-call(bf16[192,3584]{1,0:T(8,128)(2,1)S(1)} %bitcast.12, bf16[1792,896]{1,0:T(8,128)(2,1)S(1)} %copy-done, bf16[1792,896]{1,0:T(8,128)(2,1)} %collective-permute-done.1.v_ref), custom_call_target="tpu_custom_call" | custom-call | tf_op jit(solution)/shard_map/pallas_call | solution.py:19
  77.5 0.0 collective-permute-done.2.f_ref
  77.5 0.9 copy-done.7
  78.4 8.4 %all-to-all-done.2.x_ref = bf16[32,9,8,128]{3,2,1,0:T(8,128)(2,1)S(1)} async-done(((bf16[32,9,8,128]{3,2,1,0:T(8,128)(2,1)}), bf16[32,9,8,128]{3,2,1,0:T(8,128)(2,1)S(1)}, u32[]{:S(2)}, u32[]{:S(2)}) %all-to-all-start.2) | async-done | bytes 589856 | tf_op jit(solution)/shard_map/all_to_all | solution.py:30
  86.8 4.0 %all-to-all-start.3 = ((bf16[8,24,896]{2,1,0:T(8,128)(2,1)}), bf16[8,24,896]{2,1,0:T(8,128)(2,1)S(1)}, u32[]{:S(2)}, u32[]{:S(2)}) async-start(bf16[8,24,896]{2,1,0:T(8,128)(2,1)} %bitcast.4), calls=%async_computation.3 | async-start | bytes 688128 | tf_op jit(solution)/shard_map/all_to_all | solution.py:30
  90.9 0.0 copy-done.9
  90.9 0.0 copy-start.6
  90.9 2.1 shard_map.82
  93.0 8.5 %all-to-all-done.3.x_ref = bf16[8,24,896]{2,1,0:T(8,128)(2,1)S(1)} async-done(((bf16[8,24,896]{2,1,0:T(8,128)(2,1)}), bf16[8,24,896]{2,1,0:T(8,128)(2,1)S(1)}, u32[]{:S(2)}, u32[]{:S(2)}) %all-to-all-start.3) | async-done | bytes 344096 | tf_op jit(solution)/shard_map/all_to_all | solution.py:30
  101.5 6.2 %all-to-all-start.4 = ((bf16[32,9,8,128]{3,2,1,0:T(8,128)(2,1)}), bf16[32,9,8,128]{3,2,1,0:T(8,128)(2,1)S(1)}, u32[]{:S(2)}, u32[]{:S(2)}) async-start(bf16[32,9,8,128]{3,2,1,0:T(8,128)(2,1)} %bitcast.15), calls=%async_computation.4 | async-start | bytes 1179648 | tf_op jit(solution)/shard_map/all_to_all | solution.py:30
  107.7 19.8 %all-gather.2 = bf16[384,896]{1,0:T(8,128)(2,1)S(1)} all-gather(bf16[24,896]{1,0:T(8,128)(2,1)S(1)} %shard_map.81), channel_id=4, replica_groups=mesh['y'=8,'core'=2,'z'=8,'x'=4] {'y','core'}, dimensions={0}, use_global_device_ids=true | all-gather | bytes 731136 | tf_op jit(solution)/shard_map/all_gather | solution.py:278
  127.5 0.0 all-to-all-done.4.g_ref
  127.5 1.2 copy-done.8
  128.7 1.2 shard_map.83
  129.9 11.5 %all_to_all.70.x_ref = bf16[8,8,8,128]{3,2,1,0:T(8,128)(2,1)S(1)} all-to-all(bf16[8,8,8,128]{3,2,1,0:T(8,128)(2,1)S(1)} %get-tuple-element.49), channel_id=1, replica_groups=mesh['y'=8,'core'=2,'z'=8,'x'=4] {'y'}, dimensions={0} | all-to-all | bytes 262144 | tf_op jit(solution)/shard_map/all_to_all | solution.py:30
  141.4 10.3 %all_to_all.71.r_ref = bf16[8,8,8,128]{3,2,1,0:T(8,128)(2,1)S(1)} all-to-all(bf16[8,8,8,128]{3,2,1,0:T(8,128)(2,1)S(1)} %shard_map.84), channel_id=1, replica_groups=mesh['y'=8,'core'=2,'z'=8,'x'=4] {'y'}, dimensions={0} | all-to-all | bytes 262144 | tf_op jit(solution)/shard_map/all_to_all | solution.py:30
  151.7 4.0 %shard_map.85 = bf16[32,8,8,128]{3,2,1,0:T(8,128)(2,1)S(1)} custom-call(bf16[8,8,8,128]{3,2,1,0:T(8,128)(2,1)S(1)} %all_to_all.71.r_ref, bf16[1792,896]{1,0:T(8,128)(2,1)S(1)} %copy-done.1, bf16[1792,896]{1,0:T(8,128)(2,1)} %collective-permute-done.1.v_ref), custom_call_target="tpu_custom_call" | custom-call | tf_op jit(solution)/shard_map/pallas_call | solution.py:19
  155.7 22.7 %all_to_all.72.x_ref = bf16[32,8,8,128]{3,2,1,0:T(8,128)(2,1)S(1)} all-to-all(bf16[32,8,8,128]{3,2,1,0:T(8,128)(2,1)S(1)} %shard_map.85), channel_id=1, replica_groups=mesh['y'=8,'core'=2,'z'=8,'x'=4] {'z','x'}, dimensions={0} | all-to-all | bytes 1048576 | tf_op jit(solution)/shard_map/all_to_all | solution.py:30
  178.4 0.1 shard_map.86
  178.6 18.9 %all_to_all.73.r_ref = bf16[32,8,8,128]{3,2,1,0:T(8,128)(2,1)S(1)} all-to-all(bf16[32,8,8,128]{3,2,1,0:T(8,128)(2,1)S(1)} %shard_map.86), channel_id=1, replica_groups=mesh['y'=8,'core'=2,'z'=8,'x'=4] {'z','x'}, dimensions={0} | all-to-all | bytes 1048576 | tf_op jit(solution)/shard_map/all_to_all | solution.py:30
  197.5 3.2 %shard_map.87 = (bf16[8,12,8,128]{3,2,1,0:T(8,128)(2,1)S(1)}, bf16[72,1792]{1,0:T(8,128)(2,1)S(1)}, bf16[72,1792]{1,0:T(8,128)(2,1)S(1)}) custom-call(bf16[32,8,8,128]{3,2,1,0:T(8,128)(2,1)S(1)} %all_to_all.73.r_ref, bf16[1792,896]{1,0:T(8,128)(2,1)S(1)} %copy-done.1, bf16[1792,896]{1,0:T(8,128)(2,1)} %collective-permute-done.1.v_ref), custom_call_target="tpu_custom_call" | custom-call | tf_op jit(solution)/shard_map/pallas_call | solution.py:19
  200.7 11.3 %all_to_all.74.x_ref = bf16[8,12,8,128]{3,2,1,0:T(8,128)(2,1)S(1)} all-to-all(bf16[8,12,8,128]{3,2,1,0:T(8,128)(2,1)S(1)} %get-tuple-element.50), channel_id=1, replica_groups=mesh['y'=8,'core'=2,'z'=8,'x'=4] {'y'}, dimensions={0} | all-to-all | bytes 393216 | tf_op jit(solution)/shard_map/all_to_all | solution.py:30
  212.1 11.0 %all_to_all.75.m_ref = bf16[8,12,8,128]{3,2,1,0:T(8,128)(2,1)S(1)} all-to-all(bf16[8,12,8,128]{3,2,1,0:T(8,128)(2,1)S(1)} %shard_map.88), channel_id=1, replica_groups=mesh['y'=8,'core'=2,'z'=8,'x'=4] {'y'}, dimensions={0} | all-to-all | bytes 393216 | tf_op jit(solution)/shard_map/all_to_all | solution.py:30
  223.1 1.1 shard_map.89
  224.3 6.1 %all-to-all-start.11 = ((bf16[32,3,8,128]{3,2,1,0:T(8,128)(2,1)}), bf16[32,3,8,128]{3,2,1,0:T(8,128)(2,1)S(1)}, u32[]{:S(2)}, u32[]{:S(2)}) async-start(bf16[32,3,8,128]{3,2,1,0:T(8,128)(2,1)} %bitcast.7), calls=%async_computation.11 | async-start | bytes 393216 | tf_op jit(solution)/shard_map/all_to_all | solution.py:30
  230.4 6.0 %shard_map.90.w_ref = f32[72,128]{1,0:T(8,128)S(1)} custom-call(bf16[8,12,8,128]{3,2,1,0:T(8,128)(2,1)S(1)} %all_to_all.75.m_ref), custom_call_target="tpu_custom_call" | custom-call | tf_op jit(solution)/shard_map/pallas_call | solution.py:19
  236.3 3.9 %all-to-all-done.11.x_ref = bf16[32,3,8,128]{3,2,1,0:T(8,128)(2,1)S(1)} async-done(((bf16[32,3,8,128]{3,2,1,0:T(8,128)(2,1)}), bf16[32,3,8,128]{3,2,1,0:T(8,128)(2,1)S(1)}, u32[]{:S(2)}, u32[]{:S(2)}) %all-to-all-start.11) | async-done | bytes 196640 | tf_op jit(solution)/shard_map/all_to_all | solution.py:30
  240.2 0.7 shard_map.91
  241.0 5.3 %all-to-all-start.12 = ((bf16[32,3,8,128]{3,2,1,0:T(8,128)(2,1)}), bf16[32,3,8,128]{3,2,1,0:T(8,128)(2,1)S(1)}, u32[]{:S(2)}, u32[]{:S(2)}) async-start(bf16[32,3,8,128]{3,2,1,0:T(8,128)(2,1)} %bitcast.8), calls=%async_computation.12 | async-start | bytes 393216 | tf_op jit(solution)/shard_map/all_to_all | solution.py:30
  246.3 8.9 %collective-permute-start.3 = (bf16[72,1792]{1,0:T(8,128)(2,1)S(1)}, bf16[72,1792]{1,0:T(8,128)(2,1)S(1)}, u32[]{:S(2)}, u32[]{:S(2)}) collective-permute-start(bf16[72,1792]{1,0:T(8,128)(2,1)S(1)} %get-tuple-element.55), channel_id=1, source_target_pairs={{0,32},{32,0},{1,33},{33,1},{2,34},{34,2},{3,35},{35,3},{4,36},{36... | collective-permute-start | bytes 774152 | tf_op jit(solution)/shard_map/ppermute | solution.py:34
  255.2 1.9 all-gather.3
  257.0 0.0 collective-permute-done.3.got_ref
  257.0 0.0 all-to-all-done.12.c_ref
  257.0 1.0 shard_map.93
  258.0 3.4 %all-to-all-start.13 = ((bf16[8,72,256]{2,1,0:T(8,128)(2,1)}), bf16[8,72,256]{2,1,0:T(8,128)(2,1)S(1)}, u32[]{:S(2)}, u32[]{:S(2)}) async-start(bf16[8,72,256]{2,1,0:T(8,128)(2,1)} %bitcast.10), calls=%async_computation.13 | async-start | bytes 589824 | tf_op jit(solution)/shard_map/all_to_all | solution.py:30
  261.5 1.9 shard_map.92
  263.4 7.7 %all-to-all-done.13.p_ref = bf16[8,72,256]{2,1,0:T(8,128)(2,1)S(1)} async-done(((bf16[8,72,256]{2,1,0:T(8,128)(2,1)}), bf16[8,72,256]{2,1,0:T(8,128)(2,1)S(1)}, u32[]{:S(2)}, u32[]{:S(2)}) %all-to-all-start.13) | async-done | bytes 294944 | tf_op jit(solution)/shard_map/all_to_all | solution.py:30
  271.1 0.2 shard_map.94
  271.3 9.9 %all-gather.4 = f32[144,256]{1,0:T(8,128)S(1)} all-gather(f32[72,256]{1,0:T(8,128)S(1)} %shard_map.94), channel_id=6, replica_groups=mesh['y'=8,'core'=2,'z'=8,'x'=4] {'core'}, dimensions={0}, use_global_device_ids=true | all-gather | bytes 221184 | tf_op jit(solution)/shard_map/all_gather | solution.py:303
  281.2 0.7 copy.9
  (17 shorter events, 0.2 us)
Async XLA Ops:
  0.6 15.9 %copy-start.2 = (bf16[256,512]{1,0:T(8,128)(2,1)S(1)}, bf16[256,512]{1,0:T(8,128)(2,1)}, u32[]{:S(2)}) copy-start(bf16[256,512]{1,0:T(8,128)(2,1)} %w_ref.9) | copy-start | bytes 786436
  0.6 18.5 %copy-start.11 = (bf16[12,2,256]{2,1,0:T(2,128)(2,1)S(1)}, bf16[12,2,256]{2,1,0:T(2,128)(2,1)}, u32[]{:S(2)}) copy-start(bf16[12,2,256]{2,1,0:T(2,128)(2,1)} %param.7) | copy-start | bytes 36868
  11.9 21.2 %all-to-all-start = ((bf16[8,8,3584]{2,1,0:T(8,128)(2,1)}), bf16[8,8,3584]{2,1,0:T(8,128)(2,1)S(1)}, u32[]{:S(2)}, u32[]{:S(2)}) async-start(bf16[8,8,3584]{2,1,0:T(8,128)(2,1)} %bitcast.18), calls=%async_computation | async-start | bytes 917504 | tf_op jit(solution)/shard_map/all_to_all | solution.py:30
  16.6 3.7 %collective-permute-start = (bf16[256,512]{1,0:T(8,128)(2,1)S(1)}, bf16[256,512]{1,0:T(8,128)(2,1)S(1)}, u32[]{:S(2)}, u32[]{:S(2)}) collective-permute-start(bf16[256,512]{1,0:T(8,128)(2,1)S(1)} %copy-done.2), channel_id=1, source_target_pairs={{0,32},{32,0},{1,33},{33,1},{2,34},{34,2},{3,35},{35,3},{4,36},{36... | collective-permute-start | bytes 786440 | tf_op jit(solution)/shard_map/ppermute | solution.py:34
  20.3 17.6 %copy-start.4 = (bf16[256,512]{1,0:T(8,128)(2,1)}, bf16[256,512]{1,0:T(8,128)(2,1)S(1)}, u32[]{:S(2)}) copy-start(bf16[256,512]{1,0:T(8,128)(2,1)S(1)} %collective-permute-done.v_ref) | copy-start | bytes 786436
  33.1 2.4 copy-start.10
  33.1 30.9 %collective-permute-start.1 = (bf16[1792,896]{1,0:T(8,128)(2,1)}, bf16[1792,896]{1,0:T(8,128)(2,1)}, u32[]{:S(2)}, u32[]{:S(2)}) collective-permute-start(bf16[1792,896]{1,0:T(8,128)(2,1)} %w_ref.8), channel_id=1, source_target_pairs={{0,32},{32,0},{1,33},{33,1},{2,34},{34,2},{3,35},{35,3},{4,36},{36... | collective-permute-start | bytes 9633800 | tf_op jit(solution)/shard_map/ppermute | solution.py:34
  37.9 26.2 %all-to-all-start.1 = ((bf16[4,48,3584]{2,1,0:T(8,128)(2,1)}), bf16[4,48,3584]{2,1,0:T(8,128)(2,1)S(1)}, u32[]{:S(2)}, u32[]{:S(2)}) async-start(bf16[4,48,3584]{2,1,0:T(8,128)(2,1)} %shard_map.78), calls=%async_computation.1 | async-start | bytes 2752512 | tf_op jit(solution)/shard_map/all_to_all | solution.py:30
  64.0 22.8 %all-to-all-start.2 = ((bf16[32,9,8,128]{3,2,1,0:T(8,128)(2,1)}), bf16[32,9,8,128]{3,2,1,0:T(8,128)(2,1)S(1)}, u32[]{:S(2)}, u32[]{:S(2)}) async-start(bf16[32,9,8,128]{3,2,1,0:T(8,128)(2,1)} %bitcast.16), calls=%async_computation.2 | async-start | bytes 1179648 | tf_op jit(solution)/shard_map/all_to_all | solution.py:30
  69.0 8.5 %collective-permute-start.2 = (bf16[896,512]{1,0:T(8,128)(2,1)}, bf16[896,512]{1,0:T(8,128)(2,1)S(1)}, u32[]{:S(2)}, u32[]{:S(2)}) collective-permute-start(bf16[896,512]{1,0:T(8,128)(2,1)} %e_ref.1), channel_id=1, source_target_pairs={{0,32},{32,0},{1,33},{33,1},{2,34},{34,2},{3,35},{35,3},{4,36},{36... | collective-permute-start | bytes 2752520 | tf_op jit(solution)/shard_map/ppermute | solution.py:34
  71.3 1.9 copy-start
  77.5 0.9 copy-start.7
  86.8 4.0 %copy-start.9 = (bf16[32,9,8,128]{3,2,1,0:T(8,128)(2,1)}, bf16[32,9,8,128]{3,2,1,0:T(8,128)(2,1)S(1)}, u32[]{:S(2)}) copy-start(bf16[32,9,8,128]{3,2,1,0:T(8,128)(2,1)S(1)} %all-to-all-done.2.x_ref) | copy-start | bytes 1769476
  86.8 14.6 %all-to-all-start.3 = ((bf16[8,24,896]{2,1,0:T(8,128)(2,1)}), bf16[8,24,896]{2,1,0:T(8,128)(2,1)S(1)}, u32[]{:S(2)}, u32[]{:S(2)}) async-start(bf16[8,24,896]{2,1,0:T(8,128)(2,1)} %bitcast.4), calls=%async_computation.3 | async-start | bytes 688128 | tf_op jit(solution)/shard_map/all_to_all | solution.py:30
  90.9 36.6 %copy-start.6 = (bf16[896,512]{1,0:T(8,128)(2,1)S(1)}, bf16[896,512]{1,0:T(8,128)(2,1)}, u32[]{:S(2)}) copy-start(bf16[896,512]{1,0:T(8,128)(2,1)} %e_ref.1) | copy-start | bytes 2752516
  101.5 26.0 %all-to-all-start.4 = ((bf16[32,9,8,128]{3,2,1,0:T(8,128)(2,1)}), bf16[32,9,8,128]{3,2,1,0:T(8,128)(2,1)S(1)}, u32[]{:S(2)}, u32[]{:S(2)}) async-start(bf16[32,9,8,128]{3,2,1,0:T(8,128)(2,1)} %bitcast.15), calls=%async_computation.4 | async-start | bytes 1179648 | tf_op jit(solution)/shard_map/all_to_all | solution.py:30
  127.5 1.2 copy-start.8
  128.7 23.1 %copy-start.1 = (bf16[1792,896]{1,0:T(8,128)(2,1)S(1)}, bf16[1792,896]{1,0:T(8,128)(2,1)}, u32[]{:S(2)}) copy-start(bf16[1792,896]{1,0:T(8,128)(2,1)} %w_ref.8) | copy-start | bytes 9633796
  223.1 33.9 %copy-start.3 = (bf16[256,512]{1,0:T(8,128)(2,1)S(1)}, bf16[256,512]{1,0:T(8,128)(2,1)}, u32[]{:S(2)}) copy-start(bf16[256,512]{1,0:T(8,128)(2,1)} %w_ref.9) | copy-start | bytes 786436
  223.1 33.9 %copy-start.5 = (bf16[256,512]{1,0:T(8,128)(2,1)S(1)}, bf16[256,512]{1,0:T(8,128)(2,1)}, u32[]{:S(2)}) copy-start(bf16[256,512]{1,0:T(8,128)(2,1)} %copy-done.4) | copy-start | bytes 786436
  224.3 16.0 %all-to-all-start.11 = ((bf16[32,3,8,128]{3,2,1,0:T(8,128)(2,1)}), bf16[32,3,8,128]{3,2,1,0:T(8,128)(2,1)S(1)}, u32[]{:S(2)}, u32[]{:S(2)}) async-start(bf16[32,3,8,128]{3,2,1,0:T(8,128)(2,1)} %bitcast.7), calls=%async_computation.11 | async-start | bytes 393216 | tf_op jit(solution)/shard_map/all_to_all | solution.py:30
  241.0 16.1 %all-to-all-start.12 = ((bf16[32,3,8,128]{3,2,1,0:T(8,128)(2,1)}), bf16[32,3,8,128]{3,2,1,0:T(8,128)(2,1)S(1)}, u32[]{:S(2)}, u32[]{:S(2)}) async-start(bf16[32,3,8,128]{3,2,1,0:T(8,128)(2,1)} %bitcast.8), calls=%async_computation.12 | async-start | bytes 393216 | tf_op jit(solution)/shard_map/all_to_all | solution.py:30
  246.3 10.7 %collective-permute-start.3 = (bf16[72,1792]{1,0:T(8,128)(2,1)S(1)}, bf16[72,1792]{1,0:T(8,128)(2,1)S(1)}, u32[]{:S(2)}, u32[]{:S(2)}) collective-permute-start(bf16[72,1792]{1,0:T(8,128)(2,1)S(1)} %get-tuple-element.55), channel_id=1, source_target_pairs={{0,32},{32,0},{1,33},{33,1},{2,34},{34,2},{3,35},{35,3},{4,36},{36... | collective-permute-start | bytes 774152 | tf_op jit(solution)/shard_map/ppermute | solution.py:34
  258.0 13.0 %all-to-all-start.13 = ((bf16[8,72,256]{2,1,0:T(8,128)(2,1)}), bf16[8,72,256]{2,1,0:T(8,128)(2,1)S(1)}, u32[]{:S(2)}, u32[]{:S(2)}) async-start(bf16[8,72,256]{2,1,0:T(8,128)(2,1)} %bitcast.10), calls=%async_computation.13 | async-start | bytes 589824 | tf_op jit(solution)/shard_map/all_to_all | solution.py:30
